TPU v7x, 512 devices: a whole 4x4x16 slice. The times are simulated.
512 devices in a mesh: con: 8 (over x_lo, y), slab: 64 (over x_hi, z, core).
Axes of the slice: x: 4 (x_hi: 2, x_lo: 2; x = x_hi * 2 + x_lo), y: 4, z: 16, core: 2. Of those that a mesh axis runs over, the one named last changes fastest.
Arguments:
- image: float32 [8, 2, 2, 320, 320], P('con', None, None, 'slab'), may hold values from -6 to 6
- dual: float32 [8, 6, 2, 320, 320], P('con', None, None, 'slab'), may hold values from -4 to 4
- adjoint_data: float32 [8, 2, 2, 320, 320], P('con', None, None, 'slab'), may hold values from -6 to 6
- sens: float32 [8, 2, 2, 320, 320], P(None, None, None, 'slab'), may hold values from -2 to 2
- kern: float32 [8, 640, 640], P('con', 'slab'), may hold values from 0.05 to 2
Outputs:
- new_image: float32 [8, 2, 2, 320, 320], P('con', None, None, 'slab')
- new_dual: float32 [8, 6, 2, 320, 320], P('con', None, None, 'slab')
All inputs are finite; a program needn't handle non-finite values.
Results may differ from a plain program's by a relative error of at most 0.00005.
Values sent between devices are 32-bit elements; how exact they have to be, the bound alone decides.
No kernel may reach another device: no remote copies, remote signals or barrier semaphores. Data moves between devices by JAX's collectives and lax.ppermute only.
A program may use at most 64 MiB of HBM per device.

v0:
```python
import functools
import math

import jax
import jax.numpy as jnp
import ml_dtypes
import numpy as np
from jax import lax
from jax.experimental import pallas as pl
from jax.experimental.pallas import tpu as pltpu
from jax.sharding import PartitionSpec as P

FULL = 320
PADDED = 640
SLABS = 64
ROWS = 5
BAND = 10
COILS = 8
PLANES = 2
PIECE = 2 * PLANES * COILS
TILES = 13
LANES = 128


def tile_of(x, b):
    if b < 8:
        return 2 * x + b // 4, b % 4
    return 10 + x // 2, (x % 2) * 2 + b - 8


def split(value):
    high = value.astype(jnp.bfloat16)
    return high, (value - high.astype(jnp.float32)).astype(jnp.bfloat16)


def np_split(value):
    high = value.astype(np.float32).astype(ml_dtypes.bfloat16)
    low = (value - high.astype(np.float64)).astype(np.float32).astype(ml_dtypes.bfloat16)
    return high, low


@functools.cache
def tables():
    order = np.arange(BAND)[:, None] + BAND * np.arange(SLABS)[None, :]
    k2 = order.reshape(-1)
    place = (np.arange(ROWS)[:, None] + ROWS * np.arange(SLABS)[None, :]).reshape(-1)
    k1 = np.arange(PADDED)
    y = np.arange(FULL)
    turn_y = 2 * np.pi * (k2[:, None] * y[None, :] % PADDED) / PADDED
    turn_x = 2 * np.pi * (k1[:, None] * place[None, :] % PADDED) / PADDED
    cos_y, sin_y = np.cos(turn_y), np.sin(turn_y)
    cos_x, sin_x = np.cos(turn_x), np.sin(turn_x)
    forward_x = np.concatenate([cos_x, sin_x], axis=1)
    back_x = np.concatenate([cos_x.T, sin_x.T], axis=0)
    gap = ((0, 384 - FULL), (0, 0))
    back_y = np.concatenate([np.pad(cos_y.T, gap), np.pad(sin_y.T, gap)], axis=0) / PADDED**2
    spread = np.zeros((BAND, 384), np.float32)
    for b in range(BAND):
        spread[b, b * PIECE : (b + 1) * PIECE] = 1.0
    first = (*np_split(cos_y), *np_split(sin_y))
    second = (*np_split(forward_x), *np_split(back_x), spread.astype(ml_dtypes.bfloat16))
    third = np_split(back_y)
    return first, second, third


def dot(left, right, transposed=False):
    form = (((1,), (1 if transposed else 0,)), ((), ()))
    return lax.dot_general(left, right, form, preferred_element_type=jnp.float32)


def dot3(left_high, left_low, right, transposed=False):
    high, low = split(right)
    return (
        dot(left_high, high, transposed)
        + dot(left_high, low, transposed)
        + dot(left_low, high, transposed)
    )


def group_of_lane(rows):
    return lax.broadcasted_iota(jnp.int32, (rows, LANES), 1) // 32


def turn(value, shift):
    shift %= LANES
    return value if shift == 0 else pltpu.roll(value, shift, 1)


def gather_pieces(sources, groups):
    result = None
    for at, source in enumerate(sources):
        if source is None:
            continue
        moved = turn(source[0], 32 * (at - source[1]))
        result = moved if result is None else jnp.where(groups == at, moved, result)
    return result


def swap_parts(value):
    rows = value.shape[0]
    is_real = lax.broadcasted_iota(jnp.int32, (rows, LANES), 1) % 32 < 16
    parts = []
    for at in range(0, value.shape[1], LANES):
        tile = value[:, at : at + LANES]
        parts.append(jnp.where(is_real, turn(tile, -16), turn(tile, 16)))
    return jnp.concatenate(parts, axis=1), jnp.concatenate([is_real] * len(parts), axis=1)


def first_kernel(image_ref, sens_ref, ch_ref, cl_ref, sh_ref, sl_ref, out_ref, rows_ref):
    for x in range(ROWS):
        for part in range(2):
            for z in range(PLANES):
                for j in range(COILS):
                    row = x * PIECE + part * 16 + z * 8 + j
                    rows_ref[row : row + 1, :] = sens_ref[j, part, z, x : x + 1, :]
    direct, crossed = [], []
    for x in range(ROWS):
        real, imag = [], []
        for z in range(PLANES):
            sr = rows_ref[x * PIECE + z * 8 : x * PIECE + z * 8 + 8, :]
            si = rows_ref[x * PIECE + 16 + z * 8 : x * PIECE + 16 + z * 8 + 8, :]
            ur = image_ref[0, 0, z, x : x + 1, :]
            ui = image_ref[0, 1, z, x : x + 1, :]
            real.append(sr * ur - si * ui)
            imag.append(sr * ui + si * ur)
        direct += real + imag
        crossed += imag + [-part for part in real]
    rest = jnp.zeros((256 - ROWS * PIECE, FULL), jnp.float32)
    direct = jnp.concatenate(direct + [rest], axis=0)
    crossed = jnp.concatenate(crossed + [rest], axis=0)
    bands = dot3(ch_ref[...], cl_ref[...], direct, True) + dot3(
        sh_ref[...], sl_ref[...], crossed, True
    )
    groups = group_of_lane(SLABS)
    wanted = [[None] * 4 for _ in range(TILES)]
    for x in range(ROWS):
        for b in range(BAND):
            tile, at = tile_of(x, b)
            column = x // 4 * LANES
            wanted[tile][at] = (
                bands[b * SLABS : (b + 1) * SLABS, column : column + LANES],
                x % 4,
            )
    for tile in range(TILES):
        out_ref[pl.ds(tile, SLABS, stride=TILES), :] = gather_pieces(wanted[tile], groups)


def second_kernel(in_ref, kern_ref, fh_ref, fl_ref, bh_ref, bl_ref, spread_ref, out_ref):
    def tile(t):
        return in_ref[pl.ds(t, SLABS, stride=TILES), :]

    rows = []
    for x in range(ROWS):
        rest = turn(tile(10 + x // 2), -64 * (x % 2))
        rows.append(jnp.concatenate([tile(2 * x), tile(2 * x + 1), rest], axis=1))
    data = jnp.concatenate(rows, axis=0)
    swapped, is_real = swap_parts(data)
    data = jnp.concatenate([data, jnp.where(is_real, swapped, -swapped)], axis=0)
    spectrum = dot3(fh_ref[...], fl_ref[...], data)
    kern_high, kern_low = split(kern_ref[0])
    form = (((0,), (0,)), ((), ()))
    weight = lax.dot_general(
        kern_high, spread_ref[...], form, preferred_element_type=jnp.float32
    ) + lax.dot_general(kern_low, spread_ref[...], form, preferred_element_type=jnp.float32)
    both = dot3(bh_ref[...], bl_ref[...], spectrum * weight)
    swapped, is_real = swap_parts(both[FULL:])
    result = both[:FULL] + jnp.where(is_real, -swapped, swapped)
    lower = lax.broadcasted_iota(jnp.int32, (SLABS, LANES), 1) < 64
    for x in range(ROWS):
        for g in range(2):
            out_ref[pl.ds(2 * x + g, SLABS, stride=TILES), :] = result[
                x * SLABS : (x + 1) * SLABS, g * LANES : (g + 1) * LANES
            ]
    for pair in range(3):
        rest = result[2 * pair * SLABS : (2 * pair + 1) * SLABS, 256:384]
        if pair < 2:
            other = result[(2 * pair + 1) * SLABS : (2 * pair + 2) * SLABS, 256:384]
            rest = jnp.where(lower, rest, turn(other, 64))
        out_ref[pl.ds(10 + pair, SLABS, stride=TILES), :] = rest


def third_kernel(in_ref, rows_ref, th_ref, tl_ref, normal_ref):
    def tile(t):
        return in_ref[pl.ds(t, SLABS, stride=TILES), :]

    groups = group_of_lane(SLABS)
    bands = []
    for b in range(BAND):
        pieces = []
        for x in range(ROWS):
            t, at = tile_of(x, b)
            pieces.append((tile(t), at))
        columns = [gather_pieces(pieces[:4], groups), gather_pieces(pieces[4:], groups)]
        bands.append(jnp.concatenate(columns, axis=1))
    both = dot3(th_ref[...], tl_ref[...], jnp.concatenate(bands, axis=0))
    swapped, is_real = swap_parts(both[384:])
    back = (both[:384] + jnp.where(is_real, -swapped, swapped)).T
    for x in range(ROWS):
        for z in range(PLANES):
            at = x * PIECE + z * 8
            sr = rows_ref[at : at + 8, :]
            si = rows_ref[at + 16 : at + 24, :]
            br = back[at : at + 8, :FULL]
            bi = back[at + 16 : at + 24, :FULL]
            normal_ref[0, z, x : x + 1, :] = jnp.sum(sr * br + si * bi, axis=0, keepdims=True)
            normal_ref[1, z, x : x + 1, :] = jnp.sum(sr * bi - si * br, axis=0, keepdims=True)


PARAMS = pltpu.CompilerParams(vmem_limit_bytes=40 * 2**20)


def exchange(value):
    blocks = value.reshape(SLABS, 1, TILES * LANES)
    return lax.all_to_all(blocks, "slab", 0, 0, tiled=True).reshape(SLABS * TILES, LANES)


def normal_image(image, sens, kern):
    first, second, third = tables()
    block = jax.ShapeDtypeStruct((SLABS * TILES, LANES), jnp.float32)
    bands, sens_rows = pl.pallas_call(
        first_kernel,
        out_shape=(block, jax.ShapeDtypeStruct((ROWS * PIECE, FULL), jnp.float32)),
        compiler_params=PARAMS,
        name="first",
    )(image, sens, *first)
    returned = pl.pallas_call(
        second_kernel, out_shape=block, compiler_params=PARAMS, name="second"
    )(exchange(bands), kern, *second)
    return pl.pallas_call(
        third_kernel,
        out_shape=jax.ShapeDtypeStruct((2, PLANES, ROWS, FULL), jnp.float32),
        compiler_params=PARAMS,
        name="third",
    )(exchange(returned), sens_rows, *third)


def shifted(value, axis, by):
    count = lax.axis_size(axis)
    pairs = [(i, i + by) for i in range(count) if 0 <= i + by < count]
    return lax.ppermute(value, axis, pairs)


def local_forward(field, axis):
    length = field.shape[axis]
    steps_along = lax.slice_in_dim(field, 1, length, axis=axis) - lax.slice_in_dim(
        field, 0, length - 1, axis=axis
    )
    edge = jnp.zeros_like(lax.slice_in_dim(field, 0, 1, axis=axis))
    return jnp.concatenate([steps_along, edge], axis=axis)


def local_adjoint(field, axis):
    length = field.shape[axis]
    shape = [1] * field.ndim
    shape[axis] = length
    inner = (jnp.arange(length) < length - 1).astype(jnp.float32).reshape(shape)
    masked = field * inner
    edge = jnp.zeros_like(lax.slice_in_dim(field, 0, 1, axis=axis))
    before = jnp.concatenate([edge, lax.slice_in_dim(masked, 0, length - 1, axis=axis)], axis=axis)
    return before - masked


def total_over(value, axis):
    count = lax.axis_size(axis)
    copies = jnp.broadcast_to(value[None], (count, *value.shape))
    return jnp.sum(lax.all_to_all(copies, axis, 0, 0, tiled=True), axis=0)


def local(image, dual, adjoint_data, sens, kern):
    field = image[0]
    dual_now = dual[0]
    measured = adjoint_data[0]
    slab_count = lax.axis_size("slab")
    local_x = field.shape[2]
    full_x = local_x * slab_count
    global_x = lax.axis_index("slab") * local_x + jnp.arange(local_x, dtype=jnp.int32)
    inner_x = (global_x < full_x - 1).astype(jnp.float32)[None, None, :, None]
    rim_dual = shifted(dual_now[0:2, :, local_x - 1 :, :], "slab", 1)
    masked_x = dual_now[0:2] * inner_x
    adjoint_x = jnp.concatenate([rim_dual, masked_x[:, :, : local_x - 1]], axis=2) - masked_x
    adjoint_grad = adjoint_x + local_adjoint(dual_now[2:4], 3) + local_adjoint(dual_now[4:6], 1)
    normal = normal_image(image, sens, kern)
    new_field = field - 0.2 * (normal - measured + adjoint_grad)
    extra = 2.0 * new_field - field
    rim_image = shifted(extra[:, :, :1, :], "slab", -1)
    grad_x = (jnp.concatenate([extra[:, :, 1:], rim_image], axis=2) - extra) * inner_x
    grads = jnp.concatenate([grad_x, local_forward(extra, 3), local_forward(extra, 1)], axis=0)
    moved = dual_now + 0.5 * grads
    energy = total_over(jnp.sum(moved * moved, axis=0), "con")
    contrasts = lax.axis_size("con") * image.shape[0]
    limit = 0.9 * math.sqrt(6.0 * contrasts)
    factor = jnp.maximum(1.0, jnp.sqrt(energy) / limit)
    new_dual = moved / factor[None]
    return (new_field[None], new_dual[None])


def solution(mesh):
    return jax.shard_map(
        local,
        mesh=mesh,
        in_specs=(
            P("con", None, None, "slab", None),
            P("con", None, None, "slab", None),
            P("con", None, None, "slab", None),
            P(None, None, None, "slab", None),
            P("con", "slab", None),
        ),
        out_specs=(P("con", None, None, "slab", None), P("con", None, None, "slab", None)),
        check_vma=False,
    )
```

profile of v0, /device:TPU:1, one launch (start us, length us, event | category | flops | bytes accessed | tf_op | source)
XLA Modules:
  0.0 117.4 jit_solution(1260307144695304998)
XLA Ops:
  0.6 0.0 copy-start.6
  0.6 0.8 copy.44.image_ref
  1.5 1.0 copy.46.sens_ref
  2.5 0.0 copy-done.6
  2.5 0.0 copy-start.7
  2.5 1.0 copy-done.7
  3.5 0.0 copy-start.8
  3.5 1.0 copy-done.8
  4.5 0.0 copy-start.9
  4.5 1.0 copy-done.9
  5.6 0.0 copy-start.3
  5.6 2.3 %first.1 = (f32[832,128]{1,0:T(8,128)}, f32[160,320]{1,0:T(8,128)S(1)}) custom-call(f32[1,2,2,5,320]{4,3,2,1,0:T(8,128)S(1)} %copy.44.image_ref, f32[8,2,2,5,320]{4,3,2,1,0:T(8,128)S(1)} %copy.46.sens_ref, bf16[640,320]{1,0:T(8,128)(2,1)S(1)} %copy-done.6, bf16[640,320]{1,0:T(8,128)(2,1)S(1)} %copy-done.7, bf16[640,320]{1,0:T(8,128)(2,1)S(1)} %copy-done.8, ...), custom_call_target="tpu_custom_call" | custom-call | tf_op jit(solution)/shard_map/first/pallas_call | solution.py:220
  7.8 0.0 copy-start.2
  7.8 0.0 copy-start.14
  7.8 19.7 %all-to-all-start = ((f32[64,1,1664]{2,1,0:T(1,128)}), f32[64,1,1664]{2,1,0:T(1,128)S(1)}, u32[]{:S(2)}, u32[]{:S(2)}) async-start(f32[64,1,1664]{2,1,0:T(1,128)} %bitcast.1), calls=%async_computation | async-start | bytes 851968 | tf_op jit(solution)/shard_map/all_to_all | solution.py:214
  27.6 0.0 copy-done.14
  27.6 0.0 copy-start.10
  27.6 29.8 %all-to-all-done = f32[64,1,1664]{2,1,0:T(1,128)S(1)} async-done(((f32[64,1,1664]{2,1,0:T(1,128)}), f32[64,1,1664]{2,1,0:T(1,128)S(1)}, u32[]{:S(2)}, u32[]{:S(2)}) %all-to-all-start) | async-done | bytes 426016 | tf_op jit(solution)/shard_map/all_to_all | solution.py:214
  57.5 0.0 copy-done.3
  57.5 0.0 copy-done.2
  57.5 0.0 copy-done.10
  57.5 0.0 copy-start.4
  57.5 1.1 copy-done.4
  58.6 0.0 copy-start.5
  58.6 1.1 copy-done.5
  59.8 0.0 copy-start.11
  59.8 0.0 copy-start.1
  59.8 4.7 %second.1 = f32[832,128]{1,0:T(8,128)} custom-call(f32[832,128]{1,0:T(8,128)S(1)} %bitcast.37, f32[1,10,640]{2,1,0:T(8,128)S(1)} %copy.48.kern_ref, bf16[640,640]{1,0:T(8,128)(2,1)S(1)} %copy-done.2, bf16[640,640]{1,0:T(8,128)(2,1)S(1)} %copy-done.3, bf16[640,640]{1,0:T(8,128)(2,1)S(1)} %copy-done.4, bf16[640,640]{1,0:T(8,128)(2,1)S(1)} %copy-done.5, ...), custom_call_target="tpu_custom_call" | custom-call | tf_op jit(solution)/shard_map/second/pallas_call | solution.py:226
  64.4 0.0 copy-start
  64.4 5.1 %all-to-all-start.1 = ((f32[64,1,1664]{2,1,0:T(1,128)}), f32[64,1,1664]{2,1,0:T(1,128)S(1)}, u32[]{:S(2)}, u32[]{:S(2)}) async-start(f32[64,1,1664]{2,1,0:T(1,128)} %bitcast.3), calls=%async_computation.1 | async-start | bytes 851968 | tf_op jit(solution)/shard_map/all_to_all | solution.py:214
  69.5 0.0 copy-done.11
  69.6 3.5 %collective-permute-start = (f32[2,2,1,320]{3,2,1,0:T(1,128)S(1)}, f32[2,2,1,320]{3,2,1,0:T(1,128)S(1)}, u32[]{:S(2)}, u32[]{:S(2)}) collective-permute-start(f32[2,2,1,320]{3,2,1,0:T(1,128)S(1)} %slice.64), channel_id=1, source_target_pairs={{0,1},{1,2},{2,3},{3,4},{4,5},{5,6},{6,7},{7,8},{8,9},{9,10},{10,1... | collective-permute-start | bytes 15368 | tf_op jit(solution)/shard_map/ppermute | solution.py:240
  73.2 0.1 fusion.7
  73.3 26.1 %all-to-all-done.1 = f32[64,1,1664]{2,1,0:T(1,128)S(1)} async-done(((f32[64,1,1664]{2,1,0:T(1,128)}), f32[64,1,1664]{2,1,0:T(1,128)S(1)}, u32[]{:S(2)}, u32[]{:S(2)}) %all-to-all-start.1) | async-done | bytes 426016 | tf_op jit(solution)/shard_map/all_to_all | solution.py:214
  99.4 0.0 copy-done.1
  99.4 0.0 copy-done
  99.4 0.0 copy-start.12
  99.4 0.0 copy-start.13
  99.4 1.6 %third.1 = f32[2,2,5,320]{3,2,1,0:T(8,128)S(1)} custom-call(f32[832,128]{1,0:T(8,128)S(1)} %bitcast.38, f32[160,320]{1,0:T(8,128)S(1)} %get-tuple-element.5.rows_ref, bf16[768,640]{1,0:T(8,128)(2,1)S(1)} %copy-done, bf16[768,640]{1,0:T(8,128)(2,1)S(1)} %copy-done.1), custom_call_target="tpu_custom_call" | custom-call | tf_op jit(solution)/shard_map/third/pallas_call | solution.py:229
  101.0 0.0 collective-permute-done
  101.0 0.0 copy-done.12
  101.0 0.0 copy-done.13
  101.0 0.1 bitcast_subtract_fusion.1
  101.1 0.1 slice_subtract_fusion
  101.2 1.9 %collective-permute-start.1 = (f32[2,2,1,320]{3,2,1,0:T(1,128)S(1)}, f32[2,2,1,320]{3,2,1,0:T(1,128)S(1)}, u32[]{:S(2)}, u32[]{:S(2)}) collective-permute-start(f32[2,2,1,320]{3,2,1,0:T(1,128)S(1)} %slice.72), channel_id=1, source_target_pairs={{1,0},{2,1},{3,2},{4,3},{5,4},{6,5},{7,6},{8,7},{9,8},{10,9},{11,1... | collective-permute-start | bytes 15368 | tf_op jit(solution)/shard_map/ppermute | solution.py:240
  103.2 3.0 %collective-permute-done.1 = f32[2,2,1,320]{3,2,1,0:T(1,128)S(1)} collective-permute-done((f32[2,2,1,320]{3,2,1,0:T(1,128)S(1)}, f32[2,2,1,320]{3,2,1,0:T(1,128)S(1)}, u32[]{:S(2)}, u32[]{:S(2)}) %collective-permute-start.1) | collective-permute-done | bytes 5152 | tf_op jit(solution)/shard_map/ppermute | solution.py:240
  106.2 0.1 fusion.13
  106.3 0.7 broadcast_in_dim.5
  107.0 4.2 %all-to-all-start.2 = ((f32[8,2,5,320]{3,1,2,0:T(2,128)}), f32[8,2,5,320]{3,1,2,0:T(2,128)S(1)}, u32[]{:S(2)}, u32[]{:S(2)}) async-start(f32[8,2,5,320]{3,1,2,0:T(2,128)} %broadcast_in_dim.5), calls=%async_computation.2 | async-start | bytes 245760 | tf_op jit(solution)/shard_map/all_to_all | solution.py:266
  111.2 0.6 copy.58
  111.8 4.8 %all-to-all-done.2 = f32[8,2,5,320]{3,1,2,0:T(2,128)S(1)} async-done(((f32[8,2,5,320]{3,1,2,0:T(2,128)}), f32[8,2,5,320]{3,1,2,0:T(2,128)S(1)}, u32[]{:S(2)}, u32[]{:S(2)}) %all-to-all-start.2) | async-done | bytes 102432 | tf_op jit(solution)/shard_map/all_to_all | solution.py:266
  116.6 0.1 reduce_sum.19
  116.7 0.7 copy.59
  (17 shorter events, 0.2 us)
Async XLA Ops:
  0.6 1.8 %copy-start.6 = (bf16[640,320]{1,0:T(8,128)(2,1)S(1)}, bf16[640,320]{1,0:T(8,128)(2,1)}, u32[]{:S(2)}) copy-start(bf16[640,320]{1,0:T(8,128)(2,1)} %constant.19.clone.ch_ref) | copy-start | bytes 1228804
  2.5 1.0 copy-start.7
  3.5 1.0 copy-start.8
  4.5 1.0 copy-start.9
  5.6 51.9 %copy-start.3 = (bf16[640,640]{1,0:T(8,128)(2,1)S(1)}, bf16[640,640]{1,0:T(8,128)(2,1)}, u32[]{:S(2)}) copy-start(bf16[640,640]{1,0:T(8,128)(2,1)} %constant.53.clone.fl_ref) | copy-start | bytes 2457604
  7.8 49.6 %copy-start.2 = (bf16[640,640]{1,0:T(8,128)(2,1)S(1)}, bf16[640,640]{1,0:T(8,128)(2,1)}, u32[]{:S(2)}) copy-start(bf16[640,640]{1,0:T(8,128)(2,1)} %constant.52.clone.fh_ref) | copy-start | bytes 2457604
  7.8 19.8 %copy-start.14 = (f32[1,10,640]{2,0,1:T(1,128)S(1)}, f32[1,10,640]{2,0,1:T(1,128)}, u32[]{:S(2)}) copy-start(f32[1,10,640]{2,0,1:T(1,128)} %param.20) | copy-start | bytes 76804
  7.8 49.6 %all-to-all-start = ((f32[64,1,1664]{2,1,0:T(1,128)}), f32[64,1,1664]{2,1,0:T(1,128)S(1)}, u32[]{:S(2)}, u32[]{:S(2)}) async-start(f32[64,1,1664]{2,1,0:T(1,128)} %bitcast.1), calls=%async_computation | async-start | bytes 851968 | tf_op jit(solution)/shard_map/all_to_all | solution.py:214
  27.6 29.9 %copy-start.10 = (bf16[10,384]{1,0:T(8,128)(2,1)S(1)}, bf16[10,384]{1,0:T(8,128)(2,1)}, u32[]{:S(2)}) copy-start(bf16[10,384]{1,0:T(8,128)(2,1)} %constant.56.clone.spread_ref) | copy-start | bytes 23044
  57.5 1.1 copy-start.4
  58.6 1.1 copy-start.5
  59.8 9.7 %copy-start.11 = (f32[1,6,2,5,320]{4,2,3,1,0:T(2,128)S(1)}, f32[1,6,2,5,320]{4,2,3,1,0:T(2,128)}, u32[]{:S(2)}) copy-start(f32[1,6,2,5,320]{4,2,3,1,0:T(2,128)} %param.17) | copy-start | bytes 230404
  59.8 39.6 %copy-start.1 = (bf16[768,640]{1,0:T(8,128)(2,1)S(1)}, bf16[768,640]{1,0:T(8,128)(2,1)}, u32[]{:S(2)}) copy-start(bf16[768,640]{1,0:T(8,128)(2,1)} %constant.58.clone.tl_ref) | copy-start | bytes 2949124
  64.4 35.0 %copy-start = (bf16[768,640]{1,0:T(8,128)(2,1)S(1)}, bf16[768,640]{1,0:T(8,128)(2,1)}, u32[]{:S(2)}) copy-start(bf16[768,640]{1,0:T(8,128)(2,1)} %constant.57.clone.th_ref) | copy-start | bytes 2949124
  64.4 35.0 %all-to-all-start.1 = ((f32[64,1,1664]{2,1,0:T(1,128)}), f32[64,1,1664]{2,1,0:T(1,128)S(1)}, u32[]{:S(2)}, u32[]{:S(2)}) async-start(f32[64,1,1664]{2,1,0:T(1,128)} %bitcast.3), calls=%async_computation.1 | async-start | bytes 851968 | tf_op jit(solution)/shard_map/all_to_all | solution.py:214
  69.6 31.4 %collective-permute-start = (f32[2,2,1,320]{3,2,1,0:T(1,128)S(1)}, f32[2,2,1,320]{3,2,1,0:T(1,128)S(1)}, u32[]{:S(2)}, u32[]{:S(2)}) collective-permute-start(f32[2,2,1,320]{3,2,1,0:T(1,128)S(1)} %slice.64), channel_id=1, source_target_pairs={{0,1},{1,2},{2,3},{3,4},{4,5},{5,6},{6,7},{7,8},{8,9},{9,10},{10,1... | collective-permute-start | bytes 15368 | tf_op jit(solution)/shard_map/ppermute | solution.py:240
  99.4 1.6 %copy-start.12 = (f32[1,2,2,5,320]{4,2,3,1,0:T(2,128)S(1)}, f32[1,2,2,5,320]{4,2,3,1,0:T(2,128)}, u32[]{:S(2)}) copy-start(f32[1,2,2,5,320]{4,2,3,1,0:T(2,128)} %param.16) | copy-start | bytes 76804
  99.4 1.6 %copy-start.13 = (f32[1,2,2,5,320]{4,2,3,1,0:T(2,128)S(1)}, f32[1,2,2,5,320]{4,2,3,1,0:T(2,128)}, u32[]{:S(2)}) copy-start(f32[1,2,2,5,320]{4,2,3,1,0:T(2,128)} %param.18) | copy-start | bytes 76804
  101.2 4.9 %collective-permute-start.1 = (f32[2,2,1,320]{3,2,1,0:T(1,128)S(1)}, f32[2,2,1,320]{3,2,1,0:T(1,128)S(1)}, u32[]{:S(2)}, u32[]{:S(2)}) collective-permute-start(f32[2,2,1,320]{3,2,1,0:T(1,128)S(1)} %slice.72), channel_id=1, source_target_pairs={{1,0},{2,1},{3,2},{4,3},{5,4},{6,5},{7,6},{8,7},{9,8},{10,9},{11,1... | collective-permute-start | bytes 15368 | tf_op jit(solution)/shard_map/ppermute | solution.py:240
  107.0 9.6 %all-to-all-start.2 = ((f32[8,2,5,320]{3,1,2,0:T(2,128)}), f32[8,2,5,320]{3,1,2,0:T(2,128)S(1)}, u32[]{:S(2)}, u32[]{:S(2)}) async-start(f32[8,2,5,320]{3,1,2,0:T(2,128)} %broadcast_in_dim.5), calls=%async_computation.2 | async-start | bytes 245760 | tf_op jit(solution)/shard_map/all_to_all | solution.py:266
where the time goes:
time: 118 us; the launch traced here: 117 us
  waiting for transfers between devices  63.7 us (54%)
  starting transfers between devices  34.5 us (29%)
  local copies, waits for them, and re-layouts  9.31 us (8%)
  Pallas kernels  8.5 us (7%)
    all_to_all x2, waiting for transfers between devices, exchange(): lax.all_to_all(blocks, 'slab', 0, 0, tiled=True)  56 us
    all_to_all x2, starting transfers between devices, exchange(): lax.all_to_all(blocks, 'slab', 0, 0, tiled=True)  24.8 us
    unnamed x36, local copies, waits for them, and re-layouts  8.56 us
    ppermute x2, starting transfers between devices, shifted(): return lax.ppermute(value, axis, pairs)  5.46 us
    all_to_all x1, waiting for transfers between devices, total_over(): return jnp.sum(lax.all_to_all(copies, axis, 0, 0, tiled=True), axis=0)  4.76 us
    pallas_call x1, Pallas kernels, normal_image(): pl.pallas_call(second_kernel, out_shape=block, compiler_params=PARAMS, na...  4.65 us
    all_to_all x1, starting transfers between devices, total_over(): return jnp.sum(lax.all_to_all(copies, axis, 0, 0, tiled=True), axis=0)  4.22 us
    ppermute x2, waiting for transfers between devices, shifted(): return lax.ppermute(value, axis, pairs)  2.98 us
  transfers between devices with their start and end apart: 5, of which 4 were waited for; matrix products, arithmetic and copies ran while one was open for 1% of the time, Pallas kernels for 1%

commit v1 on v0

v1 whole, which is shorter than its diff:
```python
import functools
import math

import jax
import jax.numpy as jnp
import ml_dtypes
import numpy as np
from jax import lax
from jax.experimental import pallas as pl
from jax.experimental.pallas import tpu as pltpu
from jax.sharding import PartitionSpec as P

FULL = 320
PADDED = 640
QUARTER = 160
SLABS = 64
ROWS = 5
BAND = 10
COILS = 8
PLANES = 2
PIECE = 2 * PLANES * COILS
TILES = 13
LANES = 128


def tile_of(x, b):
    if b < 8:
        return 2 * x + b // 4, b % 4
    return 10 + x // 2, (x % 2) * 2 + b - 8


def split(value):
    high = value.astype(jnp.bfloat16)
    return high, (value - high.astype(jnp.float32)).astype(jnp.bfloat16)


def np_split(value):
    high = value.astype(np.float32).astype(ml_dtypes.bfloat16)
    low = (value - high.astype(np.float64)).astype(np.float32).astype(ml_dtypes.bfloat16)
    return high, low


@functools.cache
def tables():
    low = np.arange(QUARTER)
    by_band = (np.arange(BAND)[:, None] + BAND * np.arange(16)[None, :]).reshape(-1)
    points_y = [4 * np.arange(80) + r for r in range(4)]
    points_x = []
    for r in range(4):
        order = [5 * (4 * u + (r - x) % 4) + x for x in range(ROWS) for u in range(16)]
        points_x.append(np.array(order))

    def stack(points, k):
        result = []
        for point in points:
            angle = 2 * np.pi * (k[:, None] * point[None, :] % PADDED) / PADDED
            result.append(np.concatenate([np.cos(angle), np.sin(angle)], axis=1))
        return np.stack(result)

    along_y = stack(points_y, by_band)
    along_x = stack(points_x, low)
    back_x = along_x.transpose(0, 2, 1)
    back_y = along_y.transpose(0, 2, 1) / PADDED**2
    spread = np.zeros((BAND, 384), np.float32)
    for b in range(BAND):
        spread[b, b * PIECE : (b + 1) * PIECE] = 1.0
    first = np.stack(np_split(along_y))
    second = np.stack(np_split(along_x) + np_split(back_x))
    third = np.stack(np_split(back_y))
    return first, second, third, spread.astype(ml_dtypes.bfloat16)


def dot(left, right):
    return jnp.dot(left, right, preferred_element_type=jnp.float32)


def dot3(left_high, left_low, right):
    high, low = split(right)
    return dot(left_high, high) + dot(left_high, low) + dot(left_low, high)


def turn(value, shift):
    shift %= LANES
    return value if shift == 0 else pltpu.roll(value, shift, 1)


def gather_pieces(sources, groups):
    result = None
    for at, source in enumerate(sources):
        if source is None:
            continue
        moved = turn(source[0], 32 * (at - source[1]))
        result = moved if result is None else jnp.where(groups == at, moved, result)
    return result


def times_minus_i(value):
    rows = value.shape[0]
    is_real = lax.broadcasted_iota(jnp.int32, (rows, LANES), 1) % 32 < 16
    parts = []
    for at in range(0, value.shape[1], LANES):
        tile = value[:, at : at + LANES]
        parts.append(jnp.where(is_real, turn(tile, -16), -turn(tile, 16)))
    return jnp.concatenate(parts, axis=1)


def butterfly(a0, a1, a2, a3):
    even, odd = a0 + a2, a1 + a3
    apart, turned = a0 - a2, times_minus_i(a1 - a3)
    return even + odd, apart + turned, even - odd, apart - turned


def forward(high_ref_of, low_ref_of, residues):
    parts = []
    for r in range(4):
        data = jnp.concatenate([residues[r], times_minus_i(residues[r])], axis=0)
        parts.append(dot3(high_ref_of(r), low_ref_of(r), data))
    return butterfly(*parts)


def backward(high_ref_of, low_ref_of, quarters):
    sums = butterfly(*quarters)
    result = []
    for r, at in enumerate((0, 3, 2, 1)):
        both = dot3(high_ref_of(r), low_ref_of(r), sums[at])
        result.append(both[:80] - times_minus_i(both[80:]))
    return result


def first_kernel(image_hbm, sens_hbm, table_hbm, out_ref, rows_ref, image_ref, sens_ref, table_ref, flat_ref, sems):
    copies = [
        pltpu.make_async_copy(sens_hbm, sens_ref, sems.at[0]),
        pltpu.make_async_copy(image_hbm, image_ref, sems.at[1]),
        pltpu.make_async_copy(table_hbm.at[0], table_ref.at[0], sems.at[2]),
        pltpu.make_async_copy(table_hbm.at[1], table_ref.at[1], sems.at[3]),
    ]
    for copy in copies:
        copy.start()
    copies[0].wait()
    for x in range(ROWS):
        for part in range(2):
            for j in range(COILS):
                row = x * PIECE + part * 16 + 2 * j
                rows_ref[row : row + 2, :] = sens_ref[j, part, x]
    copies[1].wait()
    coil = []
    for x in range(ROWS):
        sr = rows_ref[x * PIECE : x * PIECE + 16, :]
        si = rows_ref[x * PIECE + 16 : x * PIECE + 32, :]
        ur = jnp.concatenate([image_ref[0, 0, x]] * 8, axis=0)
        ui = jnp.concatenate([image_ref[0, 1, x]] * 8, axis=0)
        coil += [sr * ur - si * ui, sr * ui + si * ur]
    coil = jnp.concatenate(coil + [jnp.zeros((256 - ROWS * PIECE, FULL), jnp.float32)], axis=0)
    coil = jnp.concatenate([coil, jnp.zeros((256, 384 - FULL), jnp.float32)], axis=1).T
    flat_ref[0] = coil[:, :LANES]
    flat_ref[1] = coil[:, LANES:]
    residues = []
    for r in range(4):
        columns = [flat_ref[column, pl.ds(r, 80, stride=4), :] for column in range(2)]
        residues.append(jnp.concatenate(columns, axis=1))
    copies[2].wait()
    copies[3].wait()
    bands = forward(lambda r: table_ref[0, r], lambda r: table_ref[1, r], residues)
    groups = lax.broadcasted_iota(jnp.int32, (16, LANES), 1) // 32
    for q in range(4):
        wanted = [[None] * 4 for _ in range(TILES)]
        for x in range(ROWS):
            for b in range(BAND):
                tile, at = tile_of(x, b)
                column = x // 4 * LANES
                value = bands[q][b * 16 : (b + 1) * 16, column : column + LANES]
                wanted[tile][at] = (value, x % 4)
        for tile in range(TILES):
            out_ref[pl.ds(16 * q * TILES + tile, 16, stride=TILES), :] = gather_pieces(
                wanted[tile], groups
            )


def weight_kernel(kern_ref, spread_ref, out_ref):
    form = (((0,), (0,)), ((), ()))
    high, low = split(kern_ref[0])
    out_ref[...] = lax.dot_general(
        high, spread_ref[...], form, preferred_element_type=jnp.float32
    ) + lax.dot_general(low, spread_ref[...], form, preferred_element_type=jnp.float32)


def second_kernel(in_ref, weight_ref, table_ref, out_ref):
    def place(x, r, t):
        return pl.ds((r - x) % 4 * TILES + t, 16, stride=4 * TILES)

    residues = []
    for r in range(4):
        rows = []
        for x in range(ROWS):
            rest = turn(in_ref[place(x, r, 10 + x // 2), :], -64 * (x % 2))
            whole = [in_ref[place(x, r, 2 * x), :], in_ref[place(x, r, 2 * x + 1), :]]
            rows.append(jnp.concatenate(whole + [rest], axis=1))
        residues.append(jnp.concatenate(rows, axis=0))
    spectrum = forward(lambda r: table_ref[0, r], lambda r: table_ref[1, r], residues)
    weighted = [
        part * weight_ref[q * QUARTER : (q + 1) * QUARTER, :] for q, part in enumerate(spectrum)
    ]
    result = backward(lambda r: table_ref[2, r], lambda r: table_ref[3, r], weighted)
    for r in range(4):
        for x in range(ROWS):
            for g in range(2):
                out_ref[place(x, r, 2 * x + g), :] = result[r][
                    x * 16 : (x + 1) * 16, g * LANES : (g + 1) * LANES
                ]
    lower = lax.broadcasted_iota(jnp.int32, (16, LANES), 1) < 64
    for s in range(4):
        for pair in range(3):
            x = 2 * pair
            rest = result[(s + x) % 4][x * 16 : (x + 1) * 16, 256:384]
            if pair < 2:
                other = result[(s + x + 1) % 4][(x + 1) * 16 : (x + 2) * 16, 256:384]
                rest = jnp.where(lower, rest, turn(other, 64))
            out_ref[place(x, s + x, 10 + pair), :] = rest


def third_kernel(in_ref, rows_ref, table_ref, normal_ref, flat_ref):
    groups = lax.broadcasted_iota(jnp.int32, (16, LANES), 1) // 32
    quarters = []
    for q in range(4):
        tiles = [in_ref[pl.ds(16 * q * TILES + t, 16, stride=TILES), :] for t in range(TILES)]
        bands = []
        for b in range(BAND):
            pieces = []
            for x in range(ROWS):
                t, at = tile_of(x, b)
                pieces.append((tiles[t], at))
            columns = [gather_pieces(pieces[:4], groups), gather_pieces(pieces[4:], groups)]
            bands.append(jnp.concatenate(columns, axis=1))
        quarters.append(jnp.concatenate(bands, axis=0))
    back = backward(lambda r: table_ref[0, r], lambda r: table_ref[1, r], quarters)
    flat_ref[:, FULL:, :] = jnp.zeros((2, 384 - FULL, LANES), jnp.float32)
    for r in range(4):
        for column in range(2):
            flat_ref[column, pl.ds(r, 80, stride=4), :] = back[r][
                :, column * LANES : (column + 1) * LANES
            ]
    back = jnp.concatenate([flat_ref[0].T, flat_ref[1].T], axis=0)[:, :FULL]

    def over_coils(value):
        half = value[:8] + value[8:]
        quarter = half[:4] + half[4:]
        return quarter[:2] + quarter[2:]

    for x in range(ROWS):
        at = x * PIECE
        sr, si = rows_ref[at : at + 16, :], rows_ref[at + 16 : at + 32, :]
        br, bi = back[at : at + 16], back[at + 16 : at + 32]
        normal_ref[0, x] = over_coils(sr * br + si * bi)
        normal_ref[1, x] = over_coils(sr * bi - si * br)


PARAMS = pltpu.CompilerParams(vmem_limit_bytes=32 * 2**20)


def exchange(value):
    blocks = value.reshape(SLABS, 1, TILES * LANES)
    return lax.all_to_all(blocks, "slab", 0, 0, tiled=True).reshape(SLABS * TILES, LANES)


def normal_image(image, sens, kern):
    first, second, third, spread = tables()
    block = jax.ShapeDtypeStruct((SLABS * TILES, LANES), jnp.float32)
    weight = pl.pallas_call(
        weight_kernel,
        out_shape=jax.ShapeDtypeStruct((PADDED, 384), jnp.float32),
        compiler_params=PARAMS,
        name="weights",
    )(kern, spread)
    whole = pl.BlockSpec(memory_space=pltpu.HBM)
    bands, sens_rows = pl.pallas_call(
        first_kernel,
        in_specs=[whole] * 3,
        out_shape=(block, jax.ShapeDtypeStruct((ROWS * PIECE, FULL), jnp.float32)),
        scratch_shapes=[
            pltpu.VMEM(image.shape, jnp.float32),
            pltpu.VMEM(sens.shape, jnp.float32),
            pltpu.VMEM(first.shape, jnp.bfloat16),
            pltpu.VMEM((2, 384, LANES), jnp.float32),
            pltpu.SemaphoreType.DMA((4,)),
        ],
        compiler_params=pltpu.CompilerParams(vmem_limit_bytes=56*2**20),
        name="first",
    )(image, sens, first)
    returned = pl.pallas_call(
        second_kernel, out_shape=block, compiler_params=PARAMS, name="second"
    )(exchange(bands), weight, second)
    return pl.pallas_call(
        third_kernel,
        out_shape=jax.ShapeDtypeStruct((2, ROWS, PLANES, FULL), jnp.float32),
        scratch_shapes=[pltpu.VMEM((2, 384, LANES), jnp.float32)],
        compiler_params=PARAMS,
        name="third",
    )(exchange(returned), sens_rows, third)


def shifted(value, axis, by):
    count = lax.axis_size(axis)
    pairs = [(i, i + by) for i in range(count) if 0 <= i + by < count]
    return lax.ppermute(value, axis, pairs)


def local_forward(field, axis):
    length = field.shape[axis]
    steps_along = lax.slice_in_dim(field, 1, length, axis=axis) - lax.slice_in_dim(
        field, 0, length - 1, axis=axis
    )
    edge = jnp.zeros_like(lax.slice_in_dim(field, 0, 1, axis=axis))
    return jnp.concatenate([steps_along, edge], axis=axis)


def local_adjoint(field, axis):
    length = field.shape[axis]
    shape = [1] * field.ndim
    shape[axis] = length
    inner = (jnp.arange(length) < length - 1).astype(jnp.float32).reshape(shape)
    masked = field * inner
    edge = jnp.zeros_like(lax.slice_in_dim(field, 0, 1, axis=axis))
    before = jnp.concatenate([edge, lax.slice_in_dim(masked, 0, length - 1, axis=axis)], axis=axis)
    return before - masked


def total_over(value, axis):
    count = lax.axis_size(axis)
    copies = jnp.broadcast_to(value[None], (count, *value.shape))
    return jnp.sum(lax.all_to_all(copies, axis, 0, 0, tiled=True), axis=0)


def local(image, dual, adjoint_data, sens, kern):
    image, dual, adjoint_data, sens = (
        jnp.swapaxes(value, 2, 3) for value in (image, dual, adjoint_data, sens)
    )
    field = image[0]
    dual_now = dual[0]
    measured = adjoint_data[0]
    slab_count = lax.axis_size("slab")
    local_x = field.shape[1]
    full_x = local_x * slab_count
    global_x = lax.axis_index("slab") * local_x + jnp.arange(local_x, dtype=jnp.int32)
    inner_x = (global_x < full_x - 1).astype(jnp.float32)[None, :, None, None]
    rim_dual = shifted(dual_now[0:2, local_x - 1 :], "slab", 1)
    masked_x = dual_now[0:2] * inner_x
    adjoint_x = jnp.concatenate([rim_dual, masked_x[:, : local_x - 1]], axis=1) - masked_x
    adjoint_grad = adjoint_x + local_adjoint(dual_now[2:4], 3) + local_adjoint(dual_now[4:6], 2)
    normal = normal_image(image, sens, kern)
    new_field = field - 0.2 * (normal - measured + adjoint_grad)
    extra = 2.0 * new_field - field
    rim_image = shifted(extra[:, :1], "slab", -1)
    grad_x = (jnp.concatenate([extra[:, 1:], rim_image], axis=1) - extra) * inner_x
    grads = jnp.concatenate([grad_x, local_forward(extra, 3), local_forward(extra, 2)], axis=0)
    moved = dual_now + 0.5 * grads
    energy = total_over(jnp.sum(moved * moved, axis=0), "con")
    contrasts = lax.axis_size("con") * image.shape[0]
    limit = 0.9 * math.sqrt(6.0 * contrasts)
    factor = jnp.maximum(1.0, jnp.sqrt(energy) / limit)
    new_dual = moved / factor[None]
    return (jnp.swapaxes(new_field[None], 2, 3), jnp.swapaxes(new_dual[None], 2, 3))


def solution(mesh):
    return jax.shard_map(
        local,
        mesh=mesh,
        in_specs=(
            P("con", None, None, "slab", None),
            P("con", None, None, "slab", None),
            P("con", None, None, "slab", None),
            P(None, None, None, "slab", None),
            P("con", "slab", None),
        ),
        out_specs=(P("con", None, None, "slab", None), P("con", None, None, "slab", None)),
        check_vma=False,
    )
```

time: 118 us -> 109 us (0.924)
  blocking collectives: 0 us -> 9.41 us
  local copies, waits for them, and re-layouts: 9.31 us -> 0.14 us
  waiting for transfers between devices: 63.7 us -> 58.5 us
  starting transfers between devices: 34.5 us -> 30.2 us
  other arithmetic: 0.5 us -> 1.92 us
  Pallas kernels: 8.5 us -> 7.25 us
    all_to_all x0 -> x1, blocking collectives: none -> 9.41 us  [total_over(): return jnp.sum(lax.all_to_all(copies, axis, 0, 0, tiled=True), axis=0)]
    unnamed x36 -> x17, local copies, waits for them, and re-layouts: 8.56 us -> 0.04 us
    all_to_all x1 -> x0, waiting for transfers between devices: 4.76 us -> none  [total_over(): return jnp.sum(lax.all_to_all(copies, axis, 0, 0, tiled=True), axis=0)]
    all_to_all x1 -> x0, starting transfers between devices: 4.22 us -> none  [total_over(): return jnp.sum(lax.all_to_all(copies, axis, 0, 0, tiled=True), axis=0)]
    pallas_call x1, Pallas kernels: 4.65 us -> 2.58 us  [normal_image(): pl.pallas_call(second_kernel, out_shape=block, compiler_params=PARAMS, na...]
    pallas_call x2 -> x3, Pallas kernels: 3.85 us -> 4.67 us  [the longest x1 3.08 us: normal_image(): pl.pallas_call(first_kernel, in_specs=[whole] * 3, out_shape=(block, jax....]
  transfers between devices with their start and end apart: 5 -> 4, of which waited for: 4 -> 3; matrix products, arithmetic and copies ran while one was open for 1% -> 0% of each run, Pallas kernels for 1% -> 1%
where the time goes in v1:
time: 109 us; the launch traced here: 108 us
  waiting for transfers between devices  58.5 us (54%)
  starting transfers between devices  30.2 us (28%)
  blocking collectives  9.41 us (9%)
  Pallas kernels  7.25 us (7%)
  other arithmetic  1.92 us (2%)
    all_to_all x2, waiting for transfers between devices, exchange(): lax.all_to_all(blocks, 'slab', 0, 0, tiled=True)  55.5 us
    all_to_all x2, starting transfers between devices, exchange(): lax.all_to_all(blocks, 'slab', 0, 0, tiled=True)  24.7 us
    all_to_all x1, blocking collectives, total_over(): return jnp.sum(lax.all_to_all(copies, axis, 0, 0, tiled=True), axis=0)  9.41 us
    ppermute x2, starting transfers between devices, shifted(): return lax.ppermute(value, axis, pairs)  5.46 us
    pallas_call x1, Pallas kernels, normal_image(): pl.pallas_call(first_kernel, in_specs=[whole] * 3, out_shape=(block, jax....  3.08 us
    ppermute x2, waiting for transfers between devices, shifted(): return lax.ppermute(value, axis, pairs)  2.96 us
    pallas_call x1, Pallas kernels, normal_image(): pl.pallas_call(second_kernel, out_shape=block, compiler_params=PARAMS, na...  2.58 us
  transfers between devices with their start and end apart: 4, of which 3 were waited for; matrix products, arithmetic and copies ran while one was open for 0% of the time, Pallas kernels for 1%

profile of v1, /device:TPU:1, one launch (start us, length us, event | category | flops | bytes accessed | tf_op | source)
XLA Modules:
  0.0 108.2 jit_solution(14973054540048827520)
XLA Ops:
  0.6 0.0 copy-start.3
  0.6 0.0 copy-start.7
  0.7 0.0 copy-start
  0.7 3.1 %first.1 = (f32[832,128]{1,0:T(8,128)}, f32[160,320]{1,0:T(8,128)}) custom-call(f32[1,2,5,2,320]{4,3,2,1,0:T(2,128)} %bitcast.56, f32[8,2,5,2,320]{4,3,2,1,0:T(2,128)} %bitcast.55, bf16[2,4,160,160]{3,2,1,0:T(8,128)(2,1)} %constant.13.clone.table_hbm), custom_call_target="tpu_custom_call" | custom-call | tf_op jit(solution)/shard_map/first/pallas_call | solution.py:275
  3.8 19.6 %all-to-all-start = ((f32[64,1,1664]{2,1,0:T(1,128)}), f32[64,1,1664]{2,1,0:T(1,128)S(1)}, u32[]{:S(2)}, u32[]{:S(2)}) async-start(f32[64,1,1664]{2,1,0:T(1,128)} %bitcast.52), calls=%async_computation | async-start | bytes 851968 | tf_op jit(solution)/shard_map/all_to_all | solution.py:262
  23.4 0.0 copy-done.7
  23.4 0.0 copy-done.3
  23.4 0.5 weights.1.weight_ref
  23.9 29.4 %all-to-all-done = f32[64,1,1664]{2,1,0:T(1,128)S(1)} async-done(((f32[64,1,1664]{2,1,0:T(1,128)}), f32[64,1,1664]{2,1,0:T(1,128)S(1)}, u32[]{:S(2)}, u32[]{:S(2)}) %all-to-all-start) | async-done | bytes 426016 | tf_op jit(solution)/shard_map/all_to_all | solution.py:262
  53.3 0.0 copy-done
  53.3 0.0 copy-start.4
  53.3 2.6 %second.1 = f32[832,128]{1,0:T(8,128)} custom-call(f32[832,128]{1,0:T(8,128)S(1)} %bitcast.48, f32[640,384]{1,0:T(8,128)S(1)} %weights.1.weight_ref, bf16[4,4,160,160]{3,2,1,0:T(8,128)(2,1)S(1)} %copy-done), custom_call_target="tpu_custom_call" | custom-call | tf_op jit(solution)/shard_map/second/pallas_call | solution.py:289
  55.9 0.0 copy-start.1
  55.9 0.0 copy-start.2
  55.9 0.0 copy-start.5
  55.9 0.0 copy-start.6
  55.9 5.1 %all-to-all-start.1 = ((f32[64,1,1664]{2,1,0:T(1,128)}), f32[64,1,1664]{2,1,0:T(1,128)S(1)}, u32[]{:S(2)}, u32[]{:S(2)}) async-start(f32[64,1,1664]{2,1,0:T(1,128)} %bitcast.5), calls=%async_computation.1 | async-start | bytes 851968 | tf_op jit(solution)/shard_map/all_to_all | solution.py:262
  61.0 0.0 copy-done.4
  61.0 3.5 %collective-permute-start = (f32[2,1,2,320]{3,2,1,0:T(2,128)S(1)}, f32[2,1,2,320]{3,2,1,0:T(2,128)S(1)}, u32[]{:S(2)}, u32[]{:S(2)}) collective-permute-start(f32[2,1,2,320]{3,2,1,0:T(2,128)S(1)} %slice.64), channel_id=1, source_target_pairs={{0,1},{1,2},{2,3},{3,4},{4,5},{5,6},{6,7},{7,8},{8,9},{9,10},{10,1... | collective-permute-start | bytes 15368 | tf_op jit(solution)/shard_map/ppermute | solution.py:304
  64.6 0.1 fusion.8
  64.7 26.1 %all-to-all-done.1 = f32[64,1,1664]{2,1,0:T(1,128)S(1)} async-done(((f32[64,1,1664]{2,1,0:T(1,128)}), f32[64,1,1664]{2,1,0:T(1,128)S(1)}, u32[]{:S(2)}, u32[]{:S(2)}) %all-to-all-start.1) | async-done | bytes 426016 | tf_op jit(solution)/shard_map/all_to_all | solution.py:262
  90.8 0.0 copy-done.1
  90.8 0.0 copy-done.2
  90.8 1.1 %third.1 = f32[2,5,2,320]{3,2,1,0:T(2,128)S(1)} custom-call(f32[832,128]{1,0:T(8,128)S(1)} %bitcast.49, f32[160,320]{1,0:T(8,128)S(1)} %copy-done.2, bf16[2,4,160,160]{3,2,1,0:T(8,128)(2,1)S(1)} %copy-done.1), custom_call_target="tpu_custom_call" | custom-call | tf_op jit(solution)/shard_map/third/pallas_call | solution.py:292
  92.0 0.0 collective-permute-done
  92.0 0.0 copy-done.5
  92.0 0.0 copy-done.6
  92.0 0.7 bitcast_subtract_fusion.1
  92.7 0.1 slice_subtract_fusion
  92.9 1.9 %collective-permute-start.1 = (f32[2,1,2,320]{3,2,1,0:T(2,128)S(1)}, f32[2,1,2,320]{3,2,1,0:T(2,128)S(1)}, u32[]{:S(2)}, u32[]{:S(2)}) collective-permute-start(f32[2,1,2,320]{3,2,1,0:T(2,128)S(1)} %slice.72), channel_id=1, source_target_pairs={{1,0},{2,1},{3,2},{4,3},{5,4},{6,5},{7,6},{8,7},{9,8},{10,9},{11,1... | collective-permute-start | bytes 15368 | tf_op jit(solution)/shard_map/ppermute | solution.py:304
  94.9 3.0 %collective-permute-done.1 = f32[2,1,2,320]{3,2,1,0:T(2,128)S(1)} collective-permute-done((f32[2,1,2,320]{3,2,1,0:T(2,128)S(1)}, f32[2,1,2,320]{3,2,1,0:T(2,128)S(1)}, u32[]{:S(2)}, u32[]{:S(2)}) %collective-permute-start.1) | collective-permute-done | bytes 5152 | tf_op jit(solution)/shard_map/ppermute | solution.py:304
  97.8 0.1 fusion.12
  97.9 0.1 fusion.5
  98.0 9.4 %all_to_all.15 = f32[8,5,2,320]{3,2,1,0:T(2,128)S(1)} all-to-all(f32[8,5,2,320]{3,2,1,0:T(2,128)S(1)} %broadcast_in_dim.5), channel_id=1, replica_groups=mesh['con'=8,'slab'=64] {'con'}, dimensions={0} | all-to-all | bytes 204800 | tf_op jit(solution)/shard_map/all_to_all | solution.py:330
  107.4 0.1 reduce_sum.19
  107.5 0.7 fusion.4
  (13 shorter events, 0.2 us)
Async XLA Ops:
  0.6 22.8 %copy-start.3 = (bf16[10,384]{1,0:T(8,128)(2,1)S(1)}, bf16[10,384]{1,0:T(8,128)(2,1)}, u32[]{:S(2)}) copy-start(bf16[10,384]{1,0:T(8,128)(2,1)} %constant.12.clone.spread_ref) | copy-start | bytes 23044
  0.6 22.7 %copy-start.7 = (f32[1,10,640]{2,0,1:T(1,128)S(1)}, f32[1,10,640]{2,0,1:T(1,128)}, u32[]{:S(2)}) copy-start(f32[1,10,640]{2,0,1:T(1,128)} %param.13) | copy-start | bytes 76804
  0.7 52.6 %copy-start = (bf16[4,4,160,160]{3,2,1,0:T(8,128)(2,1)S(1)}, bf16[4,4,160,160]{3,2,1,0:T(8,128)(2,1)}, u32[]{:S(2)}) copy-start(bf16[4,4,160,160]{3,2,1,0:T(8,128)(2,1)} %constant.36.clone.table_ref) | copy-start | bytes 2457604
  3.8 49.5 %all-to-all-start = ((f32[64,1,1664]{2,1,0:T(1,128)}), f32[64,1,1664]{2,1,0:T(1,128)S(1)}, u32[]{:S(2)}, u32[]{:S(2)}) async-start(f32[64,1,1664]{2,1,0:T(1,128)} %bitcast.52), calls=%async_computation | async-start | bytes 851968 | tf_op jit(solution)/shard_map/all_to_all | solution.py:262
  53.3 7.7 %copy-start.4 = (f32[1,6,2,5,320]{4,2,3,1,0:T(2,128)S(1)}, f32[1,6,2,5,320]{4,2,3,1,0:T(2,128)}, u32[]{:S(2)}) copy-start(f32[1,6,2,5,320]{4,2,3,1,0:T(2,128)} %param.10) | copy-start | bytes 230404
  55.9 35.0 %copy-start.1 = (bf16[2,4,160,160]{3,2,1,0:T(8,128)(2,1)S(1)}, bf16[2,4,160,160]{3,2,1,0:T(8,128)(2,1)}, u32[]{:S(2)}) copy-start(bf16[2,4,160,160]{3,2,1,0:T(8,128)(2,1)} %constant.37.clone.table_ref) | copy-start | bytes 1228804
  55.9 35.0 %copy-start.2 = (f32[160,320]{1,0:T(8,128)S(1)}, f32[160,320]{1,0:T(8,128)}, u32[]{:S(2)}) copy-start(f32[160,320]{1,0:T(8,128)} %get-tuple-element.5.rows_ref) | copy-start | bytes 614404
  55.9 36.1 %copy-start.5 = (f32[1,2,2,5,320]{4,2,3,1,0:T(2,128)S(1)}, f32[1,2,2,5,320]{4,2,3,1,0:T(2,128)}, u32[]{:S(2)}) copy-start(f32[1,2,2,5,320]{4,2,3,1,0:T(2,128)} %param.9) | copy-start | bytes 76804
  55.9 36.1 %copy-start.6 = (f32[1,2,2,5,320]{4,2,3,1,0:T(2,128)S(1)}, f32[1,2,2,5,320]{4,2,3,1,0:T(2,128)}, u32[]{:S(2)}) copy-start(f32[1,2,2,5,320]{4,2,3,1,0:T(2,128)} %param.11) | copy-start | bytes 76804
  55.9 35.0 %all-to-all-start.1 = ((f32[64,1,1664]{2,1,0:T(1,128)}), f32[64,1,1664]{2,1,0:T(1,128)S(1)}, u32[]{:S(2)}, u32[]{:S(2)}) async-start(f32[64,1,1664]{2,1,0:T(1,128)} %bitcast.5), calls=%async_computation.1 | async-start | bytes 851968 | tf_op jit(solution)/shard_map/all_to_all | solution.py:262
  61.0 31.0 %collective-permute-start = (f32[2,1,2,320]{3,2,1,0:T(2,128)S(1)}, f32[2,1,2,320]{3,2,1,0:T(2,128)S(1)}, u32[]{:S(2)}, u32[]{:S(2)}) collective-permute-start(f32[2,1,2,320]{3,2,1,0:T(2,128)S(1)} %slice.64), channel_id=1, source_target_pairs={{0,1},{1,2},{2,3},{3,4},{4,5},{5,6},{6,7},{7,8},{8,9},{9,10},{10,1... | collective-permute-start | bytes 15368 | tf_op jit(solution)/shard_map/ppermute | solution.py:304
  92.9 4.9 %collective-permute-start.1 = (f32[2,1,2,320]{3,2,1,0:T(2,128)S(1)}, f32[2,1,2,320]{3,2,1,0:T(2,128)S(1)}, u32[]{:S(2)}, u32[]{:S(2)}) collective-permute-start(f32[2,1,2,320]{3,2,1,0:T(2,128)S(1)} %slice.72), channel_id=1, source_target_pairs={{1,0},{2,1},{3,2},{4,3},{5,4},{6,5},{7,6},{8,7},{9,8},{10,9},{11,1... | collective-permute-start | bytes 15368 | tf_op jit(solution)/shard_map/ppermute | solution.py:304

commit v2 on v1

--- a/solution.py
+++ b/solution.py
@@ -20,13 +20,15 @@
 PLANES = 2
 PIECE = 2 * PLANES * COILS
 TILES = 13
+BACK_TILES = 15
 LANES = 128
-
-
-def tile_of(x, b):
+WIDE = 384
+
+
+def tile_of(x, b, rows):
     if b < 8:
         return 2 * x + b // 4, b % 4
-    return 10 + x // 2, (x % 2) * 2 + b - 8
+    return 2 * rows + x // 2, (x % 2) * 2 + b - 8
 
 
 def split(value):
@@ -61,7 +63,7 @@
     along_x = stack(points_x, low)
     back_x = along_x.transpose(0, 2, 1)
     back_y = along_y.transpose(0, 2, 1) / PADDED**2
-    spread = np.zeros((BAND, 384), np.float32)
+    spread = np.zeros((BAND, WIDE), np.float32)
     for b in range(BAND):
         spread[b, b * PIECE : (b + 1) * PIECE] = 1.0
     first = np.stack(np_split(along_y))
@@ -166,7 +168,7 @@
         wanted = [[None] * 4 for _ in range(TILES)]
         for x in range(ROWS):
             for b in range(BAND):
-                tile, at = tile_of(x, b)
+                tile, at = tile_of(x, b, ROWS)
                 column = x // 4 * LANES
                 value = bands[q][b * 16 : (b + 1) * 16, column : column + LANES]
                 wanted[tile][at] = (value, x % 4)
@@ -182,6 +184,17 @@
     out_ref[...] = lax.dot_general(
         high, spread_ref[...], form, preferred_element_type=jnp.float32
     ) + lax.dot_general(low, spread_ref[...], form, preferred_element_type=jnp.float32)
+
+
+def edge_kernel(image_ref, measured_ref, dual_ref, sens_ref, edge_ref, rim_ref):
+    for at, count, source in ((0, 2, image_ref), (2, 2, measured_ref), (4, 6, dual_ref)):
+        for channel in range(count):
+            edge_ref[at + channel, 0] = source[0, channel, 0]
+    for j in range(COILS):
+        for part in range(2):
+            edge_ref[10 + 2 * j + part, 0] = sens_ref[j, part, 0]
+    for part in range(2):
+        rim_ref[part, 0] = dual_ref[0, part, ROWS - 1]
 
 
 def second_kernel(in_ref, weight_ref, table_ref, out_ref):
@@ -201,39 +214,43 @@
         part * weight_ref[q * QUARTER : (q + 1) * QUARTER, :] for q, part in enumerate(spectrum)
     ]
     result = backward(lambda r: table_ref[2, r], lambda r: table_ref[3, r], weighted)
-    for r in range(4):
-        for x in range(ROWS):
-            for g in range(2):
-                out_ref[place(x, r, 2 * x + g), :] = result[r][
-                    x * 16 : (x + 1) * 16, g * LANES : (g + 1) * LANES
-                ]
     lower = lax.broadcasted_iota(jnp.int32, (16, LANES), 1) < 64
     for s in range(4):
+
+        def put(t, value):
+            out_ref[pl.ds(s * BACK_TILES + t, 16, stride=4 * BACK_TILES), :] = value
+
+        rows = [result[(s + x) % 4][x * 16 : (x + 1) * 16] for x in range(ROWS)]
+        following = result[(s + 1) % 4][:16]
+        rows.append(pltpu.roll(following, 15, 0) if s == 3 else following)
+        for x in range(ROWS + 1):
+            for g in range(2):
+                put(2 * x + g, rows[x][:, g * LANES : (g + 1) * LANES])
         for pair in range(3):
-            x = 2 * pair
-            rest = result[(s + x) % 4][x * 16 : (x + 1) * 16, 256:384]
-            if pair < 2:
-                other = result[(s + x + 1) % 4][(x + 1) * 16 : (x + 2) * 16, 256:384]
-                rest = jnp.where(lower, rest, turn(other, 64))
-            out_ref[place(x, s + x, 10 + pair), :] = rest
-
-
-def third_kernel(in_ref, rows_ref, table_ref, normal_ref, flat_ref):
+            left, right = rows[2 * pair][:, 256:384], rows[2 * pair + 1][:, 256:384]
+            put(12 + pair, jnp.where(lower, left, turn(right, 64)))
+
+
+def third_kernel(
+    last_ref, in_ref, rows_ref, table_ref, image_ref, measured_ref, dual_ref, edge_ref, rim_ref,
+    new_ref, moved_ref, energy_ref, flat_ref, next_ref, plain_ref,
+):
     groups = lax.broadcasted_iota(jnp.int32, (16, LANES), 1) // 32
     quarters = []
     for q in range(4):
-        tiles = [in_ref[pl.ds(16 * q * TILES + t, 16, stride=TILES), :] for t in range(TILES)]
+        start = 16 * q * BACK_TILES
+        tiles = [in_ref[pl.ds(start + t, 16, stride=BACK_TILES), :] for t in range(BACK_TILES)]
         bands = []
         for b in range(BAND):
             pieces = []
-            for x in range(ROWS):
-                t, at = tile_of(x, b)
+            for x in range(ROWS + 1):
+                t, at = tile_of(x, b, ROWS + 1)
                 pieces.append((tiles[t], at))
             columns = [gather_pieces(pieces[:4], groups), gather_pieces(pieces[4:], groups)]
             bands.append(jnp.concatenate(columns, axis=1))
         quarters.append(jnp.concatenate(bands, axis=0))
     back = backward(lambda r: table_ref[0, r], lambda r: table_ref[1, r], quarters)
-    flat_ref[:, FULL:, :] = jnp.zeros((2, 384 - FULL, LANES), jnp.float32)
+    flat_ref[:, FULL:, :] = jnp.zeros((2, WIDE - FULL, LANES), jnp.float32)
     for r in range(4):
         for column in range(2):
             flat_ref[column, pl.ds(r, 80, stride=4), :] = back[r][
@@ -246,28 +263,98 @@
         quarter = half[:4] + half[4:]
         return quarter[:2] + quarter[2:]
 
-    for x in range(ROWS):
+    for part in range(2):
+        plain_ref[12 + part, :2, :FULL] = rim_ref[part, 0]
+        for j in range(COILS):
+            row = part * 16 + 2 * j
+            next_ref[row : row + 2, :] = edge_ref[10 + 2 * j + part, 0]
+    for source, at, count in ((image_ref, 0, 2), (measured_ref, 2, 2), (dual_ref, 4, 6)):
+        for channel in range(count):
+            for x in range(ROWS):
+                plain_ref[at + channel, 2 * x : 2 * x + 2, :FULL] = source[0, channel, x]
+            plain_ref[at + channel, 2 * ROWS : 2 * ROWS + 2, :FULL] = edge_ref[at + channel, 0]
+    for x in range(ROWS + 1):
         at = x * PIECE
-        sr, si = rows_ref[at : at + 16, :], rows_ref[at + 16 : at + 32, :]
+        if x < ROWS:
+            sr, si = rows_ref[at : at + 16, :], rows_ref[at + 16 : at + 32, :]
+        else:
+            sr, si = next_ref[:16, :], next_ref[16:, :]
         br, bi = back[at : at + 16], back[at + 16 : at + 32]
-        normal_ref[0, x] = over_coils(sr * br + si * bi)
-        normal_ref[1, x] = over_coils(sr * bi - si * br)
+        plain_ref[10, 2 * x : 2 * x + 2, :FULL] = over_coils(sr * br + si * bi)
+        plain_ref[11, 2 * x : 2 * x + 2, :FULL] = over_coils(sr * bi - si * br)
+
+    row = lax.broadcasted_iota(jnp.int32, (16, WIDE), 0)
+    lane = lax.broadcasted_iota(jnp.int32, (16, WIDE), 1)
+    known = (lane < FULL) & (row < 2 * ROWS + 2)
+    inner_y = lane < FULL - 1
+    inner_z = row % 2 == 0
+    inner_x = row < jnp.where(last_ref[0] > 0, 2 * ROWS - 2, 16)
+
+    def field(at):
+        return jnp.where(known, plain_ref[at], 0.0)
+
+    moved = [None] * 6
+    for part in range(2):
+        own, across, through = field(4 + part), field(6 + part), field(8 + part)
+        masked_x = jnp.where(inner_x, own, 0.0)
+        masked_y = jnp.where(inner_y, across, 0.0)
+        masked_z = jnp.where(inner_z, through, 0.0)
+        before = jnp.where(row < 2, field(12 + part), pltpu.roll(masked_x, 2, 0))
+        adjoint = (before - masked_x) + (pltpu.roll(masked_y, 1, 1) - masked_y)
+        adjoint = adjoint + (pltpu.roll(masked_z, 1, 0) - masked_z)
+        now = field(part)
+        new = now - 0.2 * (field(10 + part) - field(2 + part) + adjoint)
+        extra = 2.0 * new - now
+        grad_x = jnp.where(inner_x, pltpu.roll(extra, 14, 0) - extra, 0.0)
+        grad_y = jnp.where(inner_y, pltpu.roll(extra, WIDE - 1, 1) - extra, 0.0)
+        grad_z = jnp.where(inner_z, pltpu.roll(extra, 15, 0) - extra, 0.0)
+        moved[part] = own + 0.5 * grad_x
+        moved[2 + part] = across + 0.5 * grad_y
+        moved[4 + part] = through + 0.5 * grad_z
+        for x in range(ROWS):
+            new_ref[0, part, x] = new[2 * x : 2 * x + 2, :FULL]
+    energy = sum(value * value for value in moved)
+    for channel in range(6):
+        moved_ref[channel] = moved[channel]
+    for copy in range(energy_ref.shape[0]):
+        energy_ref[copy] = energy
+
+
+def last_kernel(limit, energy_ref, moved_ref, out_ref):
+    energy = energy_ref[0]
+    for at in range(1, energy_ref.shape[0]):
+        energy = energy + energy_ref[at]
+    factor = jnp.maximum(1.0, jnp.sqrt(energy) / limit)
+    for channel in range(6):
+        value = moved_ref[channel] / factor
+        for x in range(ROWS):
+            out_ref[0, channel, x] = value[2 * x : 2 * x + 2, :FULL]
 
 
 PARAMS = pltpu.CompilerParams(vmem_limit_bytes=32 * 2**20)
 
 
 def exchange(value):
-    blocks = value.reshape(SLABS, 1, TILES * LANES)
-    return lax.all_to_all(blocks, "slab", 0, 0, tiled=True).reshape(SLABS * TILES, LANES)
-
-
-def normal_image(image, sens, kern):
+    tiles = value.shape[0] // SLABS
+    blocks = value.reshape(SLABS, 1, tiles * LANES)
+    return lax.all_to_all(blocks, "slab", 0, 0, tiled=True).reshape(SLABS * tiles, LANES)
+
+
+def shifted(value, axis, by):
+    count = lax.axis_size(axis)
+    pairs = [(i, i + by) for i in range(count) if 0 <= i + by < count]
+    return lax.ppermute(value, axis, pairs)
+
+
+def local(image, dual, adjoint_data, sens, kern):
+    image, dual, adjoint_data, sens = (
+        jnp.swapaxes(value, 2, 3) for value in (image, dual, adjoint_data, sens)
+    )
     first, second, third, spread = tables()
-    block = jax.ShapeDtypeStruct((SLABS * TILES, LANES), jnp.float32)
+    contrasts = lax.axis_size("con")
     weight = pl.pallas_call(
         weight_kernel,
-        out_shape=jax.ShapeDtypeStruct((PADDED, 384), jnp.float32),
+        out_shape=jax.ShapeDtypeStruct((PADDED, WIDE), jnp.float32),
         compiler_params=PARAMS,
         name="weights",
     )(kern, spread)
@@ -275,90 +362,63 @@
     bands, sens_rows = pl.pallas_call(
         first_kernel,
         in_specs=[whole] * 3,
-        out_shape=(block, jax.ShapeDtypeStruct((ROWS * PIECE, FULL), jnp.float32)),
+        out_shape=(
+            jax.ShapeDtypeStruct((SLABS * TILES, LANES), jnp.float32),
+            jax.ShapeDtypeStruct((ROWS * PIECE, FULL), jnp.float32),
+        ),
         scratch_shapes=[
             pltpu.VMEM(image.shape, jnp.float32),
             pltpu.VMEM(sens.shape, jnp.float32),
             pltpu.VMEM(first.shape, jnp.bfloat16),
-            pltpu.VMEM((2, 384, LANES), jnp.float32),
+            pltpu.VMEM((2, WIDE, LANES), jnp.float32),
             pltpu.SemaphoreType.DMA((4,)),
         ],
-        compiler_params=pltpu.CompilerParams(vmem_limit_bytes=56*2**20),
+        compiler_params=pltpu.CompilerParams(vmem_limit_bytes=56 * 2**20),
         name="first",
     )(image, sens, first)
+    edge, rim = pl.pallas_call(
+        edge_kernel,
+        out_shape=(
+            jax.ShapeDtypeStruct((10 + 2 * COILS, 1, PLANES, FULL), jnp.float32),
+            jax.ShapeDtypeStruct((2, 1, PLANES, FULL), jnp.float32),
+        ),
+        compiler_params=PARAMS,
+        name="edge",
+    )(image, adjoint_data, dual, sens)
+    edge = shifted(edge, "slab", -1)
+    rim = shifted(rim, "slab", 1)
     returned = pl.pallas_call(
-        second_kernel, out_shape=block, compiler_params=PARAMS, name="second"
+        second_kernel,
+        out_shape=jax.ShapeDtypeStruct((SLABS * BACK_TILES, LANES), jnp.float32),
+        compiler_params=PARAMS,
+        name="second",
     )(exchange(bands), weight, second)
-    return pl.pallas_call(
+    is_last = (lax.axis_index("slab") == SLABS - 1).astype(jnp.int32).reshape(1)
+    plain = jax.ShapeDtypeStruct((6, 16, WIDE), jnp.float32)
+    new_image, moved, energy = pl.pallas_call(
         third_kernel,
-        out_shape=jax.ShapeDtypeStruct((2, ROWS, PLANES, FULL), jnp.float32),
-        scratch_shapes=[pltpu.VMEM((2, 384, LANES), jnp.float32)],
+        in_specs=[pl.BlockSpec(memory_space=pltpu.SMEM)]
+        + [pl.BlockSpec(memory_space=pltpu.VMEM)] * 8,
+        out_shape=(
+            jax.ShapeDtypeStruct(image.shape, jnp.float32),
+            plain,
+            jax.ShapeDtypeStruct((contrasts, 16, WIDE), jnp.float32),
+        ),
+        scratch_shapes=[
+            pltpu.VMEM((2, WIDE, LANES), jnp.float32),
+            pltpu.VMEM((PIECE, FULL), jnp.float32),
+            pltpu.VMEM((14, 16, WIDE), jnp.float32),
+        ],
         compiler_params=PARAMS,
         name="third",
-    )(exchange(returned), sens_rows, third)
-
-
-def shifted(value, axis, by):
-    count = lax.axis_size(axis)
-    pairs = [(i, i + by) for i in range(count) if 0 <= i + by < count]
-    return lax.ppermute(value, axis, pairs)
-
-
-def local_forward(field, axis):
-    length = field.shape[axis]
-    steps_along = lax.slice_in_dim(field, 1, length, axis=axis) - lax.slice_in_dim(
-        field, 0, length - 1, axis=axis
-    )
-    edge = jnp.zeros_like(lax.slice_in_dim(field, 0, 1, axis=axis))
-    return jnp.concatenate([steps_along, edge], axis=axis)
-
-
-def local_adjoint(field, axis):
-    length = field.shape[axis]
-    shape = [1] * field.ndim
-    shape[axis] = length
-    inner = (jnp.arange(length) < length - 1).astype(jnp.float32).reshape(shape)
-    masked = field * inner
-    edge = jnp.zeros_like(lax.slice_in_dim(field, 0, 1, axis=axis))
-    before = jnp.concatenate([edge, lax.slice_in_dim(masked, 0, length - 1, axis=axis)], axis=axis)
-    return before - masked
-
-
-def total_over(value, axis):
-    count = lax.axis_size(axis)
-    copies = jnp.broadcast_to(value[None], (count, *value.shape))
-    return jnp.sum(lax.all_to_all(copies, axis, 0, 0, tiled=True), axis=0)
-
-
-def local(image, dual, adjoint_data, sens, kern):
-    image, dual, adjoint_data, sens = (
-        jnp.swapaxes(value, 2, 3) for value in (image, dual, adjoint_data, sens)
-    )
-    field = image[0]
-    dual_now = dual[0]
-    measured = adjoint_data[0]
-    slab_count = lax.axis_size("slab")
-    local_x = field.shape[1]
-    full_x = local_x * slab_count
-    global_x = lax.axis_index("slab") * local_x + jnp.arange(local_x, dtype=jnp.int32)
-    inner_x = (global_x < full_x - 1).astype(jnp.float32)[None, :, None, None]
-    rim_dual = shifted(dual_now[0:2, local_x - 1 :], "slab", 1)
-    masked_x = dual_now[0:2] * inner_x
-    adjoint_x = jnp.concatenate([rim_dual, masked_x[:, : local_x - 1]], axis=1) - masked_x
-    adjoint_grad = adjoint_x + local_adjoint(dual_now[2:4], 3) + local_adjoint(dual_now[4:6], 2)
-    normal = normal_image(image, sens, kern)
-    new_field = field - 0.2 * (normal - measured + adjoint_grad)
-    extra = 2.0 * new_field - field
-    rim_image = shifted(extra[:, :1], "slab", -1)
-    grad_x = (jnp.concatenate([extra[:, 1:], rim_image], axis=1) - extra) * inner_x
-    grads = jnp.concatenate([grad_x, local_forward(extra, 3), local_forward(extra, 2)], axis=0)
-    moved = dual_now + 0.5 * grads
-    energy = total_over(jnp.sum(moved * moved, axis=0), "con")
-    contrasts = lax.axis_size("con") * image.shape[0]
-    limit = 0.9 * math.sqrt(6.0 * contrasts)
-    factor = jnp.maximum(1.0, jnp.sqrt(energy) / limit)
-    new_dual = moved / factor[None]
-    return (jnp.swapaxes(new_field[None], 2, 3), jnp.swapaxes(new_dual[None], 2, 3))
+    )(is_last, exchange(returned), sens_rows, third, image, adjoint_data, dual, edge, rim)
+    new_dual = pl.pallas_call(
+        functools.partial(last_kernel, 0.9 * math.sqrt(6.0 * contrasts)),
+        out_shape=jax.ShapeDtypeStruct(dual.shape, jnp.float32),
+        compiler_params=PARAMS,
+        name="last",
+    )(lax.all_to_all(energy, "con", 0, 0, tiled=True), moved)
+    return jnp.swapaxes(new_image, 2, 3), jnp.swapaxes(new_dual, 2, 3)
 
 
 def solution(mesh):

time: 109 us -> 106 us (0.972)
  waiting for transfers between devices: 58.5 us -> 55.8 us
  other arithmetic: 1.92 us -> 0 us
  Pallas kernels: 7.25 us -> 8.72 us
    all_to_all x2, waiting for transfers between devices: 55.5 us -> 38 us  [exchange(): lax.all_to_all(blocks, 'slab', 0, 0, tiled=True)]
    ppermute x2, waiting for transfers between devices: 2.96 us -> 17.8 us  [shifted(): return lax.ppermute(value, axis, pairs)]
    pallas_call x4 -> x6, Pallas kernels: 7.25 us -> 8.72 us  [the longest x1 3.08 us: local(): pl.pallas_call(first_kernel, in_specs=[whole] * 3, out_shape=(jax.ShapeDt...]
  transfers between devices with their start and end apart: 4 -> 4, of which waited for: 3 -> 4; matrix products, arithmetic and copies ran while one was open for 0% -> 0% of each run, Pallas kernels for 1% -> 0%
where the time goes in v2:
time: 106 us
  waiting for transfers between devices  55.8 us (53%)
  starting transfers between devices  30.3 us (29%)
  blocking collectives  10.1 us (10%)
  Pallas kernels  8.72 us (8%)
    all_to_all x2, waiting for transfers between devices, exchange(): lax.all_to_all(blocks, 'slab', 0, 0, tiled=True)  38 us
    all_to_all x2, starting transfers between devices, exchange(): lax.all_to_all(blocks, 'slab', 0, 0, tiled=True)  24.7 us
    ppermute x2, waiting for transfers between devices, shifted(): return lax.ppermute(value, axis, pairs)  17.8 us
    all_to_all x1, blocking collectives, local(): lax.all_to_all(energy, 'con', 0, 0, tiled=True)  10.1 us
    ppermute x2, starting transfers between devices, shifted(): return lax.ppermute(value, axis, pairs)  5.56 us
    pallas_call x1, Pallas kernels, local(): pl.pallas_call(first_kernel, in_specs=[whole] * 3, out_shape=(jax.ShapeDt...  3.08 us
    pallas_call x1, Pallas kernels, local(): pl.pallas_call(second_kernel, out_shape=jax.ShapeDtypeStruct((SLABS * BAC...  2.61 us
  transfers between devices with their start and end apart: 4, of which 4 were waited for; matrix products, arithmetic and copies ran while one was open for 0% of the time, Pallas kernels for 0%

profile of v2, /device:TPU:1, one launch (start us, length us, event | category | flops | bytes accessed | tf_op | source)
XLA Modules:
  0.0 105.7 jit_solution(2317211917490796584)
XLA Ops:
  0.6 0.0 copy-start.7
  0.6 0.0 copy-start.8
  0.7 0.0 copy-start
  0.7 3.1 %first.1 = (f32[832,128]{1,0:T(8,128)}, f32[160,320]{1,0:T(8,128)}) custom-call(f32[1,2,5,2,320]{4,3,2,1,0:T(2,128)} %bitcast.17, f32[8,2,5,2,320]{4,3,2,1,0:T(2,128)} %bitcast.13, bf16[2,4,160,160]{3,2,1,0:T(8,128)(2,1)} %constant.15.clone.table_hbm), custom_call_target="tpu_custom_call" | custom-call | tf_op jit(solution)/shard_map/first/pallas_call | solution.py:362
  3.8 19.6 %all-to-all-start = ((f32[64,1,1664]{2,1,0:T(1,128)}), f32[64,1,1664]{2,1,0:T(1,128)S(1)}, u32[]{:S(2)}, u32[]{:S(2)}) async-start(f32[64,1,1664]{2,1,0:T(1,128)} %bitcast.22), calls=%async_computation | async-start | bytes 851968 | tf_op jit(solution)/shard_map/all_to_all | solution.py:340
  23.4 0.0 copy-done.8
  23.4 0.0 copy-done.7
  23.4 0.5 weights.1.weight_ref
  23.9 29.4 %all-to-all-done = f32[64,1,1664]{2,1,0:T(1,128)S(1)} async-done(((f32[64,1,1664]{2,1,0:T(1,128)}), f32[64,1,1664]{2,1,0:T(1,128)S(1)}, u32[]{:S(2)}, u32[]{:S(2)}) %all-to-all-start) | async-done | bytes 426016 | tf_op jit(solution)/shard_map/all_to_all | solution.py:340
  53.3 0.0 copy-done
  53.3 0.0 copy-start.1
  53.3 0.0 copy-start.3
  53.3 0.0 copy-start.4
  53.3 0.0 copy-start.6
  53.3 2.6 %second.1 = f32[960,128]{1,0:T(8,128)} custom-call(f32[832,128]{1,0:T(8,128)S(1)} %bitcast.12, f32[640,384]{1,0:T(8,128)S(1)} %weights.1.weight_ref, bf16[4,4,160,160]{3,2,1,0:T(8,128)(2,1)S(1)} %copy-done), custom_call_target="tpu_custom_call" | custom-call | tf_op jit(solution)/shard_map/second/pallas_call | solution.py:390
  55.9 0.0 copy-start.2
  55.9 0.0 copy-start.5
  55.9 5.1 %all-to-all-start.1 = ((f32[64,1,1920]{2,1,0:T(1,128)}), f32[64,1,1920]{2,1,0:T(1,128)S(1)}, u32[]{:S(2)}, u32[]{:S(2)}) async-start(f32[64,1,1920]{2,1,0:T(1,128)} %bitcast.5), calls=%async_computation.1 | async-start | bytes 983040 | tf_op jit(solution)/shard_map/all_to_all | solution.py:340
  61.0 0.0 copy-done.1
  61.0 0.0 copy-done.3
  61.0 0.0 copy-done.4
  61.0 0.0 copy-done.6
  61.0 2.4 %collective-permute-start = (f32[26,1,2,320]{3,2,1,0:T(2,128)S(1)}, f32[26,1,2,320]{3,2,1,0:T(2,128)S(1)}, u32[]{:S(2)}, u32[]{:S(2)}) collective-permute-start(f32[26,1,2,320]{3,2,1,0:T(2,128)S(1)} %get-tuple-element.11), channel_id=1, source_target_pairs={{1,0},{2,1},{3,2},{4,3},{5,4},{6,5},{7,6},{8,7},{9,8},{10,9},{11,1... | collective-permute-start | bytes 199688 | tf_op jit(solution)/shard_map/ppermute | solution.py:346
  63.4 3.2 %collective-permute-start.1 = (f32[2,1,2,320]{3,2,1,0:T(2,128)S(1)}, f32[2,1,2,320]{3,2,1,0:T(2,128)S(1)}, u32[]{:S(2)}, u32[]{:S(2)}) collective-permute-start(f32[2,1,2,320]{3,2,1,0:T(2,128)S(1)} %get-tuple-element.12), channel_id=1, source_target_pairs={{0,1},{1,2},{2,3},{3,4},{4,5},{5,6},{6,7},{7,8},{8,9},{9,10},{10,1... | collective-permute-start | bytes 15368 | tf_op jit(solution)/shard_map/ppermute | solution.py:346
  66.6 8.9 %collective-permute-done.1.rim_ref = f32[2,1,2,320]{3,2,1,0:T(2,128)S(1)} collective-permute-done((f32[2,1,2,320]{3,2,1,0:T(2,128)S(1)}, f32[2,1,2,320]{3,2,1,0:T(2,128)S(1)}, u32[]{:S(2)}, u32[]{:S(2)}) %collective-permute-start.1) | collective-permute-done | bytes 5152 | tf_op jit(solution)/shard_map/ppermute | solution.py:346
  75.5 8.9 %collective-permute-done.edge_ref = f32[26,1,2,320]{3,2,1,0:T(2,128)S(1)} collective-permute-done((f32[26,1,2,320]{3,2,1,0:T(2,128)S(1)}, f32[26,1,2,320]{3,2,1,0:T(2,128)S(1)}, u32[]{:S(2)}, u32[]{:S(2)}) %collective-permute-start) | collective-permute-done | bytes 66592 | tf_op jit(solution)/shard_map/ppermute | solution.py:346
  84.4 8.6 %all-to-all-done.1 = f32[64,1,1920]{2,1,0:T(1,128)S(1)} async-done(((f32[64,1,1920]{2,1,0:T(1,128)}), f32[64,1,1920]{2,1,0:T(1,128)S(1)}, u32[]{:S(2)}, u32[]{:S(2)}) %all-to-all-start.1) | async-done | bytes 491552 | tf_op jit(solution)/shard_map/all_to_all | solution.py:340
  93.0 0.0 copy-done.2
  93.0 0.0 copy-done.5
  93.0 1.9 %third.1 = (f32[1,2,5,2,320]{4,3,2,1,0:T(2,128)}, f32[6,16,384]{2,1,0:T(8,128)S(1)}, f32[8,16,384]{2,1,0:T(8,128)S(1)}) custom-call(s32[1]{0:T(128)} %bitcast.last_ref, f32[960,128]{1,0:T(8,128)S(1)} %bitcast.11, f32[160,320]{1,0:T(8,128)S(1)} %copy-done.5, bf16[2,4,160,160]{3,2,1,0:T(8,128)(2,1)S(1)} %copy-done.2, f32[1,2,5,2,320]{4,3,2,1,0:T(2,128)S(1)} %bitcast.19, ...), custom_call_target="tpu_custom_call" | custom-call | tf_op jit(solution)/shard_map/third/pallas_call | solution.py:398
  94.9 10.1 %all_to_all.15.energy_ref = f32[8,16,384]{2,1,0:T(8,128)S(1)} all-to-all(f32[8,16,384]{2,1,0:T(8,128)S(1)} %get-tuple-element.14), channel_id=1, replica_groups=mesh['con'=8,'slab'=64] {'con'}, dimensions={0} | all-to-all | bytes 393216 | tf_op jit(solution)/shard_map/all_to_all | solution.py:420
  105.0 0.7 last.1
  (2 shorter events, 0.0 us)
Async XLA Ops:
  0.6 22.8 %copy-start.7 = (bf16[10,384]{1,0:T(8,128)(2,1)S(1)}, bf16[10,384]{1,0:T(8,128)(2,1)}, u32[]{:S(2)}) copy-start(bf16[10,384]{1,0:T(8,128)(2,1)} %constant.14.clone.spread_ref) | copy-start | bytes 23044
  0.6 22.7 %copy-start.8 = (f32[1,10,640]{2,0,1:T(1,128)S(1)}, f32[1,10,640]{2,0,1:T(1,128)}, u32[]{:S(2)}) copy-start(f32[1,10,640]{2,0,1:T(1,128)} %param.13) | copy-start | bytes 76804
  0.7 52.6 %copy-start = (bf16[4,4,160,160]{3,2,1,0:T(8,128)(2,1)S(1)}, bf16[4,4,160,160]{3,2,1,0:T(8,128)(2,1)}, u32[]{:S(2)}) copy-start(bf16[4,4,160,160]{3,2,1,0:T(8,128)(2,1)} %constant.16.clone.table_ref) | copy-start | bytes 2457604
  3.8 49.5 %all-to-all-start = ((f32[64,1,1664]{2,1,0:T(1,128)}), f32[64,1,1664]{2,1,0:T(1,128)S(1)}, u32[]{:S(2)}, u32[]{:S(2)}) async-start(f32[64,1,1664]{2,1,0:T(1,128)} %bitcast.22), calls=%async_computation | async-start | bytes 851968 | tf_op jit(solution)/shard_map/all_to_all | solution.py:340
  53.3 7.7 %copy-start.1 = (f32[8,2,2,5,320]{4,2,3,1,0:T(2,128)S(1)}, f32[8,2,2,5,320]{4,2,3,1,0:T(2,128)}, u32[]{:S(2)}) copy-start(f32[8,2,2,5,320]{4,2,3,1,0:T(2,128)} %param.12) | copy-start | bytes 614404
  53.3 7.7 %copy-start.3 = (f32[1,6,2,5,320]{4,2,3,1,0:T(2,128)S(1)}, f32[1,6,2,5,320]{4,2,3,1,0:T(2,128)}, u32[]{:S(2)}) copy-start(f32[1,6,2,5,320]{4,2,3,1,0:T(2,128)} %param.10) | copy-start | bytes 230404
  53.3 7.7 %copy-start.4 = (f32[1,2,2,5,320]{4,2,3,1,0:T(2,128)S(1)}, f32[1,2,2,5,320]{4,2,3,1,0:T(2,128)}, u32[]{:S(2)}) copy-start(f32[1,2,2,5,320]{4,2,3,1,0:T(2,128)} %param.9) | copy-start | bytes 76804
  53.3 7.7 %copy-start.6 = (f32[1,2,2,5,320]{4,2,3,1,0:T(2,128)S(1)}, f32[1,2,2,5,320]{4,2,3,1,0:T(2,128)}, u32[]{:S(2)}) copy-start(f32[1,2,2,5,320]{4,2,3,1,0:T(2,128)} %param.11) | copy-start | bytes 76804
  55.9 37.1 %copy-start.2 = (bf16[2,4,160,160]{3,2,1,0:T(8,128)(2,1)S(1)}, bf16[2,4,160,160]{3,2,1,0:T(8,128)(2,1)}, u32[]{:S(2)}) copy-start(bf16[2,4,160,160]{3,2,1,0:T(8,128)(2,1)} %constant.17.clone.table_ref) | copy-start | bytes 1228804
  55.9 37.1 %copy-start.5 = (f32[160,320]{1,0:T(8,128)S(1)}, f32[160,320]{1,0:T(8,128)}, u32[]{:S(2)}) copy-start(f32[160,320]{1,0:T(8,128)} %get-tuple-element.10.rows_ref) | copy-start | bytes 614404
  55.9 37.1 %all-to-all-start.1 = ((f32[64,1,1920]{2,1,0:T(1,128)}), f32[64,1,1920]{2,1,0:T(1,128)S(1)}, u32[]{:S(2)}, u32[]{:S(2)}) async-start(f32[64,1,1920]{2,1,0:T(1,128)} %bitcast.5), calls=%async_computation.1 | async-start | bytes 983040 | tf_op jit(solution)/shard_map/all_to_all | solution.py:340
  61.0 23.4 %collective-permute-start = (f32[26,1,2,320]{3,2,1,0:T(2,128)S(1)}, f32[26,1,2,320]{3,2,1,0:T(2,128)S(1)}, u32[]{:S(2)}, u32[]{:S(2)}) collective-permute-start(f32[26,1,2,320]{3,2,1,0:T(2,128)S(1)} %get-tuple-element.11), channel_id=1, source_target_pairs={{1,0},{2,1},{3,2},{4,3},{5,4},{6,5},{7,6},{8,7},{9,8},{10,9},{11,1... | collective-permute-start | bytes 199688 | tf_op jit(solution)/shard_map/ppermute | solution.py:346
  63.4 12.1 %collective-permute-start.1 = (f32[2,1,2,320]{3,2,1,0:T(2,128)S(1)}, f32[2,1,2,320]{3,2,1,0:T(2,128)S(1)}, u32[]{:S(2)}, u32[]{:S(2)}) collective-permute-start(f32[2,1,2,320]{3,2,1,0:T(2,128)S(1)} %get-tuple-element.12), channel_id=1, source_target_pairs={{0,1},{1,2},{2,3},{3,4},{4,5},{5,6},{6,7},{7,8},{8,9},{9,10},{10,1... | collective-permute-start | bytes 15368 | tf_op jit(solution)/shard_map/ppermute | solution.py:346

commit v3 on v2

--- a/solution.py
+++ b/solution.py
@@ -18,7 +18,7 @@
 BAND = 10
 COILS = 8
 PLANES = 2
-PIECE = 2 * PLANES * COILS
+PIECE = PLANES * COILS
 TILES = 13
 BACK_TILES = 15
 LANES = 128
@@ -65,9 +65,11 @@
     back_y = along_y.transpose(0, 2, 1) / PADDED**2
     spread = np.zeros((BAND, WIDE), np.float32)
     for b in range(BAND):
-        spread[b, b * PIECE : (b + 1) * PIECE] = 1.0
-    first = np.stack(np_split(along_y))
-    second = np.stack(np_split(along_x) + np_split(back_x))
+        for part in range(2):
+            at = b // 4 * LANES + part * 64 + b % 4 * PIECE
+            spread[b, at : at + PIECE] = 1.0
+    first = np.stack(np_split(along_y), axis=1)
+    second = np.stack([np.concatenate([h, h, l], axis=2) for h, l in (np_split(along_x), np_split(back_x))])
     third = np.stack(np_split(back_y))
     return first, second, third, spread.astype(ml_dtypes.bfloat16)
 
@@ -78,6 +80,8 @@
 
 def dot3(left_high, left_low, right):
     high, low = split(right)
+    if right.shape[1] > 256:
+        return dot(left_high, jnp.concatenate([high, low, high], axis=0))
     return dot(left_high, high) + dot(left_high, low) + dot(left_low, high)
 
 
@@ -86,23 +90,38 @@
     return value if shift == 0 else pltpu.roll(value, shift, 1)
 
 
-def gather_pieces(sources, groups):
+def slot_of_lane(rows):
+    return lax.broadcasted_iota(jnp.int32, (rows, LANES), 1) % 64 // PIECE
+
+
+def gather_pieces(sources, slots):
     result = None
     for at, source in enumerate(sources):
         if source is None:
             continue
-        moved = turn(source[0], 32 * (at - source[1]))
-        result = moved if result is None else jnp.where(groups == at, moved, result)
+        moved = turn(source[0], PIECE * (at - source[1]))
+        result = moved if result is None else jnp.where(slots == at, moved, result)
+    return result
+
+
+def transpose_pieces(tiles, slots):
+    result = list(tiles)
+    for step in (1, 2):
+        low = slots // step % 2 == 0
+        for at in (0, 1) if step == 2 else (0, 2):
+            left, right = result[at], result[at + step]
+            result[at] = jnp.where(low, left, turn(right, PIECE * step))
+            result[at + step] = jnp.where(low, turn(left, -PIECE * step), right)
     return result
 
 
 def times_minus_i(value):
     rows = value.shape[0]
-    is_real = lax.broadcasted_iota(jnp.int32, (rows, LANES), 1) % 32 < 16
+    is_real = lax.broadcasted_iota(jnp.int32, (rows, LANES), 1) < 64
     parts = []
     for at in range(0, value.shape[1], LANES):
-        tile = value[:, at : at + LANES]
-        parts.append(jnp.where(is_real, turn(tile, -16), -turn(tile, 16)))
+        turned = turn(value[:, at : at + LANES], 64)
+        parts.append(jnp.where(is_real, turned, -turned))
     return jnp.concatenate(parts, axis=1)
 
 
@@ -129,53 +148,71 @@
     return result
 
 
-def first_kernel(image_hbm, sens_hbm, table_hbm, out_ref, rows_ref, image_ref, sens_ref, table_ref, flat_ref, sems):
+def gather_rows(sens_ref, rows_ref):
+    for x in range(ROWS):
+        for part in range(2):
+            for j in range(COILS):
+                row = (2 * x + part) * PIECE + 2 * j
+                rows_ref[row : row + 2, :] = sens_ref[j, part, x]
+
+
+def first_kernel(
+    image_hbm, sens_hbm, table_hbm, out_ref,
+    image_ref, sens_ref, table_ref, flat_ref, rows_ref, sems,
+):
     copies = [
         pltpu.make_async_copy(sens_hbm, sens_ref, sems.at[0]),
         pltpu.make_async_copy(image_hbm, image_ref, sems.at[1]),
-        pltpu.make_async_copy(table_hbm.at[0], table_ref.at[0], sems.at[2]),
-        pltpu.make_async_copy(table_hbm.at[1], table_ref.at[1], sems.at[3]),
     ]
+    for r in range(4):
+        copies.append(pltpu.make_async_copy(table_hbm.at[r], table_ref.at[r], sems.at[2 + r]))
     for copy in copies:
         copy.start()
     copies[0].wait()
+    gather_rows(sens_ref, rows_ref)
+    copies[1].wait()
+    real, imag = [], []
     for x in range(ROWS):
-        for part in range(2):
-            for j in range(COILS):
-                row = x * PIECE + part * 16 + 2 * j
-                rows_ref[row : row + 2, :] = sens_ref[j, part, x]
-    copies[1].wait()
-    coil = []
-    for x in range(ROWS):
-        sr = rows_ref[x * PIECE : x * PIECE + 16, :]
-        si = rows_ref[x * PIECE + 16 : x * PIECE + 32, :]
-        ur = jnp.concatenate([image_ref[0, 0, x]] * 8, axis=0)
-        ui = jnp.concatenate([image_ref[0, 1, x]] * 8, axis=0)
-        coil += [sr * ur - si * ui, sr * ui + si * ur]
-    coil = jnp.concatenate(coil + [jnp.zeros((256 - ROWS * PIECE, FULL), jnp.float32)], axis=0)
-    coil = jnp.concatenate([coil, jnp.zeros((256, 384 - FULL), jnp.float32)], axis=1).T
+        sr = rows_ref[2 * x * PIECE : (2 * x + 1) * PIECE, :]
+        si = rows_ref[(2 * x + 1) * PIECE : (2 * x + 2) * PIECE, :]
+        ur = jnp.concatenate([image_ref[0, 0, x]] * COILS, axis=0)
+        ui = jnp.concatenate([image_ref[0, 1, x]] * COILS, axis=0)
+        real.append(sr * ur - si * ui)
+        imag.append(sr * ui + si * ur)
+    rest = [jnp.zeros((3 * PIECE, FULL), jnp.float32)]
+    coil = jnp.concatenate(real[:4] + imag[:4] + real[4:] + rest + imag[4:] + rest, axis=0)
+    coil = jnp.concatenate([coil, jnp.zeros((256, WIDE - FULL), jnp.float32)], axis=1).T
     flat_ref[0] = coil[:, :LANES]
     flat_ref[1] = coil[:, LANES:]
     residues = []
     for r in range(4):
         columns = [flat_ref[column, pl.ds(r, 80, stride=4), :] for column in range(2)]
         residues.append(jnp.concatenate(columns, axis=1))
-    copies[2].wait()
-    copies[3].wait()
-    bands = forward(lambda r: table_ref[0, r], lambda r: table_ref[1, r], residues)
-    groups = lax.broadcasted_iota(jnp.int32, (16, LANES), 1) // 32
+
+    for r in range(4):
+        copies[2 + r].wait()
+
+    def table(r, level):
+        return table_ref[r, level]
+
+    bands = forward(lambda r: table(r, 0), lambda r: table(r, 1), residues)
+    slots = slot_of_lane(16)
     for q in range(4):
-        wanted = [[None] * 4 for _ in range(TILES)]
-        for x in range(ROWS):
-            for b in range(BAND):
-                tile, at = tile_of(x, b, ROWS)
-                column = x // 4 * LANES
-                value = bands[q][b * 16 : (b + 1) * 16, column : column + LANES]
-                wanted[tile][at] = (value, x % 4)
-        for tile in range(TILES):
-            out_ref[pl.ds(16 * q * TILES + tile, 16, stride=TILES), :] = gather_pieces(
-                wanted[tile], groups
-            )
+        start = 16 * q * TILES
+
+        def put(t, value):
+            out_ref[pl.ds(start + t, 16, stride=TILES), :] = value
+
+        near = [bands[q][b * 16 : (b + 1) * 16, :LANES] for b in range(BAND)]
+        far = [bands[q][b * 16 : (b + 1) * 16, LANES:] for b in range(BAND)]
+        for g in range(2):
+            for x, value in enumerate(transpose_pieces(near[4 * g : 4 * g + 4], slots)):
+                put(2 * x + g, value)
+            put(8 + g, gather_pieces([(far[4 * g + i], 0) for i in range(4)], slots))
+        for pair in range(2):
+            pieces = [(near[8 + i], 2 * pair + x) for x in range(2) for i in range(2)]
+            put(10 + pair, gather_pieces(pieces, slots))
+        put(12, gather_pieces([(far[8], 0), (far[9], 0)], slots))
 
 
 def weight_kernel(kern_ref, spread_ref, out_ref):
@@ -186,7 +223,8 @@
     ) + lax.dot_general(low, spread_ref[...], form, preferred_element_type=jnp.float32)
 
 
-def edge_kernel(image_ref, measured_ref, dual_ref, sens_ref, edge_ref, rim_ref):
+def edge_kernel(image_ref, measured_ref, dual_ref, sens_ref, edge_ref, rim_ref, rows_ref):
+    gather_rows(sens_ref, rows_ref)
     for at, count, source in ((0, 2, image_ref), (2, 2, measured_ref), (4, 6, dual_ref)):
         for channel in range(count):
             edge_ref[at + channel, 0] = source[0, channel, 0]
@@ -205,16 +243,16 @@
     for r in range(4):
         rows = []
         for x in range(ROWS):
-            rest = turn(in_ref[place(x, r, 10 + x // 2), :], -64 * (x % 2))
+            rest = turn(in_ref[place(x, r, 10 + x // 2), :], -2 * PIECE * (x % 2))
             whole = [in_ref[place(x, r, 2 * x), :], in_ref[place(x, r, 2 * x + 1), :]]
             rows.append(jnp.concatenate(whole + [rest], axis=1))
         residues.append(jnp.concatenate(rows, axis=0))
-    spectrum = forward(lambda r: table_ref[0, r], lambda r: table_ref[1, r], residues)
+    spectrum = forward(lambda r: table_ref[0, r], lambda r: None, residues)
     weighted = [
         part * weight_ref[q * QUARTER : (q + 1) * QUARTER, :] for q, part in enumerate(spectrum)
     ]
-    result = backward(lambda r: table_ref[2, r], lambda r: table_ref[3, r], weighted)
-    lower = lax.broadcasted_iota(jnp.int32, (16, LANES), 1) < 64
+    result = backward(lambda r: table_ref[1, r], lambda r: None, weighted)
+    lower = slot_of_lane(16) < 2
     for s in range(4):
 
         def put(t, value):
@@ -227,28 +265,28 @@
             for g in range(2):
                 put(2 * x + g, rows[x][:, g * LANES : (g + 1) * LANES])
         for pair in range(3):
-            left, right = rows[2 * pair][:, 256:384], rows[2 * pair + 1][:, 256:384]
-            put(12 + pair, jnp.where(lower, left, turn(right, 64)))
+            left, right = rows[2 * pair][:, 2 * LANES :], rows[2 * pair + 1][:, 2 * LANES :]
+            put(12 + pair, jnp.where(lower, left, turn(right, 2 * PIECE)))
 
 
 def third_kernel(
     last_ref, in_ref, rows_ref, table_ref, image_ref, measured_ref, dual_ref, edge_ref, rim_ref,
-    new_ref, moved_ref, energy_ref, flat_ref, next_ref, plain_ref,
+    moved_ref, energy_ref, flat_ref, next_ref, plain_ref,
 ):
-    groups = lax.broadcasted_iota(jnp.int32, (16, LANES), 1) // 32
+    slots = slot_of_lane(16)
     quarters = []
     for q in range(4):
         start = 16 * q * BACK_TILES
         tiles = [in_ref[pl.ds(start + t, 16, stride=BACK_TILES), :] for t in range(BACK_TILES)]
-        bands = []
-        for b in range(BAND):
-            pieces = []
-            for x in range(ROWS + 1):
-                t, at = tile_of(x, b, ROWS + 1)
-                pieces.append((tiles[t], at))
-            columns = [gather_pieces(pieces[:4], groups), gather_pieces(pieces[4:], groups)]
-            bands.append(jnp.concatenate(columns, axis=1))
-        quarters.append(jnp.concatenate(bands, axis=0))
+        near, far = [], []
+        for g in range(2):
+            near += transpose_pieces([tiles[2 * x + g] for x in range(4)], slots)
+            far += [gather_pieces([(tiles[8 + g], i), (tiles[10 + g], i)], slots) for i in range(4)]
+        for i in range(2):
+            near.append(gather_pieces([(tiles[12 + x // 2], x % 2 * 2 + i) for x in range(4)], slots))
+            far.append(gather_pieces([(tiles[14], i), (tiles[14], 2 + i)], slots))
+        columns = [jnp.concatenate(near, axis=0), jnp.concatenate(far, axis=0)]
+        quarters.append(jnp.concatenate(columns, axis=1))
     back = backward(lambda r: table_ref[0, r], lambda r: table_ref[1, r], quarters)
     flat_ref[:, FULL:, :] = jnp.zeros((2, WIDE - FULL, LANES), jnp.float32)
     for r in range(4):
@@ -266,7 +304,7 @@
     for part in range(2):
         plain_ref[12 + part, :2, :FULL] = rim_ref[part, 0]
         for j in range(COILS):
-            row = part * 16 + 2 * j
+            row = part * PIECE + 2 * j
             next_ref[row : row + 2, :] = edge_ref[10 + 2 * j + part, 0]
     for source, at, count in ((image_ref, 0, 2), (measured_ref, 2, 2), (dual_ref, 4, 6)):
         for channel in range(count):
@@ -274,12 +312,13 @@
                 plain_ref[at + channel, 2 * x : 2 * x + 2, :FULL] = source[0, channel, x]
             plain_ref[at + channel, 2 * ROWS : 2 * ROWS + 2, :FULL] = edge_ref[at + channel, 0]
     for x in range(ROWS + 1):
-        at = x * PIECE
         if x < ROWS:
-            sr, si = rows_ref[at : at + 16, :], rows_ref[at + 16 : at + 32, :]
+            at = 2 * x * PIECE
+            sr, si = rows_ref[at : at + PIECE, :], rows_ref[at + PIECE : at + 2 * PIECE, :]
         else:
-            sr, si = next_ref[:16, :], next_ref[16:, :]
-        br, bi = back[at : at + 16], back[at + 16 : at + 32]
+            sr, si = next_ref[:PIECE, :], next_ref[PIECE:, :]
+        at = x // 4 * LANES + x % 4 * PIECE
+        br, bi = back[at : at + PIECE], back[at + 64 : at + 64 + PIECE]
         plain_ref[10, 2 * x : 2 * x + 2, :FULL] = over_coils(sr * br + si * bi)
         plain_ref[11, 2 * x : 2 * x + 2, :FULL] = over_coils(sr * bi - si * br)
 
@@ -311,24 +350,28 @@
         moved[part] = own + 0.5 * grad_x
         moved[2 + part] = across + 0.5 * grad_y
         moved[4 + part] = through + 0.5 * grad_z
-        for x in range(ROWS):
-            new_ref[0, part, x] = new[2 * x : 2 * x + 2, :FULL]
+        moved_ref[6 + part] = new
     energy = sum(value * value for value in moved)
     for channel in range(6):
         moved_ref[channel] = moved[channel]
     for copy in range(energy_ref.shape[0]):
-        energy_ref[copy] = energy
-
-
-def last_kernel(limit, energy_ref, moved_ref, out_ref):
+        for t in range(3):
+            energy_ref[copy, 10 * t : 10 * t + 10, :] = energy[:10, t * LANES : (t + 1) * LANES]
+
+
+def last_kernel(limit, energy_ref, moved_ref, new_ref, out_ref):
     energy = energy_ref[0]
     for at in range(1, energy_ref.shape[0]):
         energy = energy + energy_ref[at]
-    factor = jnp.maximum(1.0, jnp.sqrt(energy) / limit)
+    scale = 1.0 / jnp.maximum(1.0, jnp.sqrt(energy) / limit)
+    scale = jnp.concatenate([scale[10 * t : 10 * t + 10] for t in range(3)], axis=1)
     for channel in range(6):
-        value = moved_ref[channel] / factor
+        value = moved_ref[channel][:10] * scale
         for x in range(ROWS):
             out_ref[0, channel, x] = value[2 * x : 2 * x + 2, :FULL]
+    for part in range(2):
+        for x in range(ROWS):
+            new_ref[0, part, x] = moved_ref[6 + part, 2 * x : 2 * x + 2, :FULL]
 
 
 PARAMS = pltpu.CompilerParams(vmem_limit_bytes=32 * 2**20)
@@ -359,28 +402,27 @@
         name="weights",
     )(kern, spread)
     whole = pl.BlockSpec(memory_space=pltpu.HBM)
-    bands, sens_rows = pl.pallas_call(
+    bands = pl.pallas_call(
         first_kernel,
         in_specs=[whole] * 3,
-        out_shape=(
-            jax.ShapeDtypeStruct((SLABS * TILES, LANES), jnp.float32),
-            jax.ShapeDtypeStruct((ROWS * PIECE, FULL), jnp.float32),
-        ),
+        out_shape=jax.ShapeDtypeStruct((SLABS * TILES, LANES), jnp.float32),
         scratch_shapes=[
             pltpu.VMEM(image.shape, jnp.float32),
             pltpu.VMEM(sens.shape, jnp.float32),
             pltpu.VMEM(first.shape, jnp.bfloat16),
             pltpu.VMEM((2, WIDE, LANES), jnp.float32),
-            pltpu.SemaphoreType.DMA((4,)),
+            pltpu.VMEM((2 * ROWS * PIECE, FULL), jnp.float32),
+            pltpu.SemaphoreType.DMA((6,)),
         ],
         compiler_params=pltpu.CompilerParams(vmem_limit_bytes=56 * 2**20),
         name="first",
     )(image, sens, first)
-    edge, rim = pl.pallas_call(
+    edge, rim, sens_rows = pl.pallas_call(
         edge_kernel,
         out_shape=(
             jax.ShapeDtypeStruct((10 + 2 * COILS, 1, PLANES, FULL), jnp.float32),
             jax.ShapeDtypeStruct((2, 1, PLANES, FULL), jnp.float32),
+            jax.ShapeDtypeStruct((2 * ROWS * PIECE, FULL), jnp.float32),
         ),
         compiler_params=PARAMS,
         name="edge",
@@ -394,27 +436,28 @@
         name="second",
     )(exchange(bands), weight, second)
     is_last = (lax.axis_index("slab") == SLABS - 1).astype(jnp.int32).reshape(1)
-    plain = jax.ShapeDtypeStruct((6, 16, WIDE), jnp.float32)
-    new_image, moved, energy = pl.pallas_call(
+    moved, energy = pl.pallas_call(
         third_kernel,
         in_specs=[pl.BlockSpec(memory_space=pltpu.SMEM)]
         + [pl.BlockSpec(memory_space=pltpu.VMEM)] * 8,
         out_shape=(
-            jax.ShapeDtypeStruct(image.shape, jnp.float32),
-            plain,
-            jax.ShapeDtypeStruct((contrasts, 16, WIDE), jnp.float32),
+            jax.ShapeDtypeStruct((8, 16, WIDE), jnp.float32),
+            jax.ShapeDtypeStruct((contrasts, 30, LANES), jnp.float32),
         ),
         scratch_shapes=[
             pltpu.VMEM((2, WIDE, LANES), jnp.float32),
-            pltpu.VMEM((PIECE, FULL), jnp.float32),
+            pltpu.VMEM((2 * PIECE, FULL), jnp.float32),
             pltpu.VMEM((14, 16, WIDE), jnp.float32),
         ],
         compiler_params=PARAMS,
         name="third",
     )(is_last, exchange(returned), sens_rows, third, image, adjoint_data, dual, edge, rim)
-    new_dual = pl.pallas_call(
+    new_image, new_dual = pl.pallas_call(
         functools.partial(last_kernel, 0.9 * math.sqrt(6.0 * contrasts)),
-        out_shape=jax.ShapeDtypeStruct(dual.shape, jnp.float32),
+        out_shape=(
+            jax.ShapeDtypeStruct(image.shape, jnp.float32),
+            jax.ShapeDtypeStruct(dual.shape, jnp.float32),
+        ),
         compiler_params=PARAMS,
         name="last",
     )(lax.all_to_all(energy, "con", 0, 0, tiled=True), moved)

time: 106 us -> 104 us (0.981)
  Pallas kernels: 8.72 us -> 7.58 us
  transfers between devices with their start and end apart: 4 -> 4, of which waited for: 4 -> 4; matrix products, arithmetic and copies ran while one was open for 0% -> 0% of each run, Pallas kernels for 0% -> 1%
where the time goes in v3:
time: 104 us
  waiting for transfers between devices  55.7 us (54%)
  starting transfers between devices  30.4 us (29%)
  blocking collectives  9.61 us (9%)
  Pallas kernels  7.58 us (7%)
    all_to_all x2, waiting for transfers between devices, exchange(): lax.all_to_all(blocks, 'slab', 0, 0, tiled=True)  38 us
    all_to_all x2, starting transfers between devices, exchange(): lax.all_to_all(blocks, 'slab', 0, 0, tiled=True)  24.8 us
    ppermute x2, waiting for transfers between devices, shifted(): return lax.ppermute(value, axis, pairs)  17.7 us
    all_to_all x1, blocking collectives, local(): lax.all_to_all(energy, 'con', 0, 0, tiled=True)  9.61 us
    ppermute x2, starting transfers between devices, shifted(): return lax.ppermute(value, axis, pairs)  5.56 us
    pallas_call x1, Pallas kernels, local(): pl.pallas_call(first_kernel, in_specs=[whole] * 3, out_shape=jax.ShapeDty...  2.91 us
    pallas_call x1, Pallas kernels, local(): pl.pallas_call(second_kernel, out_shape=jax.ShapeDtypeStruct((SLABS * BAC...  2.22 us
  transfers between devices with their start and end apart: 4, of which 4 were waited for; matrix products, arithmetic and copies ran while one was open for 0% of the time, Pallas kernels for 1%

profile of v3, /device:TPU:1, one launch (start us, length us, event | category | flops | bytes accessed | tf_op | source)
XLA Modules:
  0.0 104.1 jit_solution(5138886350158076429)
XLA Ops:
  0.6 0.0 copy-start.6
  0.6 0.0 copy-start.7
  0.7 2.9 %first.1 = f32[832,128]{1,0:T(8,128)} custom-call(f32[1,2,5,2,320]{4,3,2,1,0:T(2,128)} %bitcast.17, f32[8,2,5,2,320]{4,3,2,1,0:T(2,128)} %bitcast.13, bf16[4,2,160,160]{3,2,1,0:T(8,128)(2,1)} %constant.15.clone.table_hbm), custom_call_target="tpu_custom_call" | custom-call | tf_op jit(solution)/shard_map/first/pallas_call | solution.py:405
  3.6 0.0 copy-start
  3.6 19.8 %all-to-all-start = ((f32[64,1,1664]{2,1,0:T(1,128)}), f32[64,1,1664]{2,1,0:T(1,128)S(1)}, u32[]{:S(2)}, u32[]{:S(2)}) async-start(f32[64,1,1664]{2,1,0:T(1,128)} %bitcast.22), calls=%async_computation | async-start | bytes 851968 | tf_op jit(solution)/shard_map/all_to_all | solution.py:383
  23.3 0.0 copy-done.7
  23.4 0.0 copy-done.6
  23.4 0.5 weights.1.weight_ref
  23.8 29.4 %all-to-all-done = f32[64,1,1664]{2,1,0:T(1,128)S(1)} async-done(((f32[64,1,1664]{2,1,0:T(1,128)}), f32[64,1,1664]{2,1,0:T(1,128)S(1)}, u32[]{:S(2)}, u32[]{:S(2)}) %all-to-all-start) | async-done | bytes 426016 | tf_op jit(solution)/shard_map/all_to_all | solution.py:383
  53.2 0.0 copy-done
  53.2 0.0 copy-start.1
  53.2 0.0 copy-start.3
  53.2 0.0 copy-start.4
  53.2 0.0 copy-start.5
  53.3 2.2 %second.1 = f32[960,128]{1,0:T(8,128)} custom-call(f32[832,128]{1,0:T(8,128)S(1)} %bitcast.12, f32[640,384]{1,0:T(8,128)S(1)} %weights.1.weight_ref, bf16[2,4,160,480]{3,2,1,0:T(8,128)(2,1)S(1)} %copy-done), custom_call_target="tpu_custom_call" | custom-call | tf_op jit(solution)/shard_map/second/pallas_call | solution.py:432
  55.5 0.0 copy-start.2
  55.5 5.1 %all-to-all-start.1 = ((f32[64,1,1920]{2,1,0:T(1,128)}), f32[64,1,1920]{2,1,0:T(1,128)S(1)}, u32[]{:S(2)}, u32[]{:S(2)}) async-start(f32[64,1,1920]{2,1,0:T(1,128)} %bitcast.5), calls=%async_computation.1 | async-start | bytes 983040 | tf_op jit(solution)/shard_map/all_to_all | solution.py:383
  60.6 0.0 copy-done.1
  60.6 0.0 copy-done.3
  60.6 0.0 copy-done.4
  60.6 0.0 copy-done.5
  60.6 0.1 edge.1
  60.7 2.4 %collective-permute-start = (f32[26,1,2,320]{3,2,1,0:T(2,128)S(1)}, f32[26,1,2,320]{3,2,1,0:T(2,128)S(1)}, u32[]{:S(2)}, u32[]{:S(2)}) collective-permute-start(f32[26,1,2,320]{3,2,1,0:T(2,128)S(1)} %get-tuple-element.10), channel_id=1, source_target_pairs={{1,0},{2,1},{3,2},{4,3},{5,4},{6,5},{7,6},{8,7},{9,8},{10,9},{11,1... | collective-permute-start | bytes 199688 | tf_op jit(solution)/shard_map/ppermute | solution.py:389
  63.1 3.2 %collective-permute-start.1 = (f32[2,1,2,320]{3,2,1,0:T(2,128)S(1)}, f32[2,1,2,320]{3,2,1,0:T(2,128)S(1)}, u32[]{:S(2)}, u32[]{:S(2)}) collective-permute-start(f32[2,1,2,320]{3,2,1,0:T(2,128)S(1)} %get-tuple-element.11), channel_id=1, source_target_pairs={{0,1},{1,2},{2,3},{3,4},{4,5},{5,6},{6,7},{7,8},{8,9},{9,10},{10,1... | collective-permute-start | bytes 15368 | tf_op jit(solution)/shard_map/ppermute | solution.py:389
  66.3 8.8 %collective-permute-done.1.rim_ref = f32[2,1,2,320]{3,2,1,0:T(2,128)S(1)} collective-permute-done((f32[2,1,2,320]{3,2,1,0:T(2,128)S(1)}, f32[2,1,2,320]{3,2,1,0:T(2,128)S(1)}, u32[]{:S(2)}, u32[]{:S(2)}) %collective-permute-start.1) | collective-permute-done | bytes 5152 | tf_op jit(solution)/shard_map/ppermute | solution.py:389
  75.1 8.9 %collective-permute-done.edge_ref = f32[26,1,2,320]{3,2,1,0:T(2,128)S(1)} collective-permute-done((f32[26,1,2,320]{3,2,1,0:T(2,128)S(1)}, f32[26,1,2,320]{3,2,1,0:T(2,128)S(1)}, u32[]{:S(2)}, u32[]{:S(2)}) %collective-permute-start) | collective-permute-done | bytes 66592 | tf_op jit(solution)/shard_map/ppermute | solution.py:389
  84.0 8.6 %all-to-all-done.1 = f32[64,1,1920]{2,1,0:T(1,128)S(1)} async-done(((f32[64,1,1920]{2,1,0:T(1,128)}), f32[64,1,1920]{2,1,0:T(1,128)S(1)}, u32[]{:S(2)}, u32[]{:S(2)}) %all-to-all-start.1) | async-done | bytes 491552 | tf_op jit(solution)/shard_map/all_to_all | solution.py:383
  92.6 0.0 copy-done.2
  92.6 1.2 %third.1 = (f32[8,16,384]{2,1,0:T(8,128)S(1)}, f32[8,30,128]{2,1,0:T(8,128)S(1)}) custom-call(s32[1]{0:T(128)} %bitcast.last_ref, f32[960,128]{1,0:T(8,128)S(1)} %bitcast.11, f32[160,320]{1,0:T(8,128)S(1)} %get-tuple-element.9.rows_ref, bf16[2,4,160,160]{3,2,1,0:T(8,128)(2,1)S(1)} %copy-done.2, f32[1,2,5,2,320]{4,3,2,1,0:T(2,128)S(1)} %bitcast.19, ...), custom_call_target="tpu_custom_call" | custom-call | tf_op jit(solution)/shard_map/third/pallas_call | solution.py:439
  93.8 9.6 %all_to_all.15.energy_ref = f32[8,30,128]{2,1,0:T(8,128)S(1)} all-to-all(f32[8,30,128]{2,1,0:T(8,128)S(1)} %get-tuple-element.12), channel_id=1, replica_groups=mesh['con'=8,'slab'=64] {'con'}, dimensions={0} | all-to-all | bytes 245760 | tf_op jit(solution)/shard_map/all_to_all | solution.py:463
  103.4 0.7 last.1
  (1 shorter events, 0.0 us)
Async XLA Ops:
  0.6 22.7 %copy-start.6 = (bf16[10,384]{1,0:T(8,128)(2,1)S(1)}, bf16[10,384]{1,0:T(8,128)(2,1)}, u32[]{:S(2)}) copy-start(bf16[10,384]{1,0:T(8,128)(2,1)} %constant.14.clone.spread_ref) | copy-start | bytes 23044
  0.6 22.7 %copy-start.7 = (f32[1,10,640]{2,0,1:T(1,128)S(1)}, f32[1,10,640]{2,0,1:T(1,128)}, u32[]{:S(2)}) copy-start(f32[1,10,640]{2,0,1:T(1,128)} %param.13) | copy-start | bytes 76804
  3.6 49.7 %copy-start = (bf16[2,4,160,480]{3,2,1,0:T(8,128)(2,1)S(1)}, bf16[2,4,160,480]{3,2,1,0:T(8,128)(2,1)}, u32[]{:S(2)}) copy-start(bf16[2,4,160,480]{3,2,1,0:T(8,128)(2,1)} %constant.16.clone.table_ref) | copy-start | bytes 3686404
  3.6 49.6 %all-to-all-start = ((f32[64,1,1664]{2,1,0:T(1,128)}), f32[64,1,1664]{2,1,0:T(1,128)S(1)}, u32[]{:S(2)}, u32[]{:S(2)}) async-start(f32[64,1,1664]{2,1,0:T(1,128)} %bitcast.22), calls=%async_computation | async-start | bytes 851968 | tf_op jit(solution)/shard_map/all_to_all | solution.py:383
  53.2 7.3 %copy-start.1 = (f32[8,2,2,5,320]{4,2,3,1,0:T(2,128)S(1)}, f32[8,2,2,5,320]{4,2,3,1,0:T(2,128)}, u32[]{:S(2)}) copy-start(f32[8,2,2,5,320]{4,2,3,1,0:T(2,128)} %param.12) | copy-start | bytes 614404
  53.2 7.3 %copy-start.3 = (f32[1,6,2,5,320]{4,2,3,1,0:T(2,128)S(1)}, f32[1,6,2,5,320]{4,2,3,1,0:T(2,128)}, u32[]{:S(2)}) copy-start(f32[1,6,2,5,320]{4,2,3,1,0:T(2,128)} %param.10) | copy-start | bytes 230404
  53.2 7.3 %copy-start.4 = (f32[1,2,2,5,320]{4,2,3,1,0:T(2,128)S(1)}, f32[1,2,2,5,320]{4,2,3,1,0:T(2,128)}, u32[]{:S(2)}) copy-start(f32[1,2,2,5,320]{4,2,3,1,0:T(2,128)} %param.9) | copy-start | bytes 76804
  53.2 7.3 %copy-start.5 = (f32[1,2,2,5,320]{4,2,3,1,0:T(2,128)S(1)}, f32[1,2,2,5,320]{4,2,3,1,0:T(2,128)}, u32[]{:S(2)}) copy-start(f32[1,2,2,5,320]{4,2,3,1,0:T(2,128)} %param.11) | copy-start | bytes 76804
  55.5 37.1 %copy-start.2 = (bf16[2,4,160,160]{3,2,1,0:T(8,128)(2,1)S(1)}, bf16[2,4,160,160]{3,2,1,0:T(8,128)(2,1)}, u32[]{:S(2)}) copy-start(bf16[2,4,160,160]{3,2,1,0:T(8,128)(2,1)} %constant.17.clone.table_ref) | copy-start | bytes 1228804
  55.5 37.1 %all-to-all-start.1 = ((f32[64,1,1920]{2,1,0:T(1,128)}), f32[64,1,1920]{2,1,0:T(1,128)S(1)}, u32[]{:S(2)}, u32[]{:S(2)}) async-start(f32[64,1,1920]{2,1,0:T(1,128)} %bitcast.5), calls=%async_computation.1 | async-start | bytes 983040 | tf_op jit(solution)/shard_map/all_to_all | solution.py:383
  60.7 23.3 %collective-permute-start = (f32[26,1,2,320]{3,2,1,0:T(2,128)S(1)}, f32[26,1,2,320]{3,2,1,0:T(2,128)S(1)}, u32[]{:S(2)}, u32[]{:S(2)}) collective-permute-start(f32[26,1,2,320]{3,2,1,0:T(2,128)S(1)} %get-tuple-element.10), channel_id=1, source_target_pairs={{1,0},{2,1},{3,2},{4,3},{5,4},{6,5},{7,6},{8,7},{9,8},{10,9},{11,1... | collective-permute-start | bytes 199688 | tf_op jit(solution)/shard_map/ppermute | solution.py:389
  63.1 12.0 %collective-permute-start.1 = (f32[2,1,2,320]{3,2,1,0:T(2,128)S(1)}, f32[2,1,2,320]{3,2,1,0:T(2,128)S(1)}, u32[]{:S(2)}, u32[]{:S(2)}) collective-permute-start(f32[2,1,2,320]{3,2,1,0:T(2,128)S(1)} %get-tuple-element.11), channel_id=1, source_target_pairs={{0,1},{1,2},{2,3},{3,4},{4,5},{5,6},{6,7},{7,8},{8,9},{9,10},{10,1... | collective-permute-start | bytes 15368 | tf_op jit(solution)/shard_map/ppermute | solution.py:389

commit v4 on v3

--- a/solution.py
+++ b/solution.py
@@ -215,10 +215,10 @@
         put(12, gather_pieces([(far[8], 0), (far[9], 0)], slots))
 
 
-def weight_kernel(kern_ref, spread_ref, out_ref):
+def weights(kern_ref, spread_ref):
     form = (((0,), (0,)), ((), ()))
-    high, low = split(kern_ref[0])
-    out_ref[...] = lax.dot_general(
+    high, low = split(kern_ref[:, 0])
+    return lax.dot_general(
         high, spread_ref[...], form, preferred_element_type=jnp.float32
     ) + lax.dot_general(low, spread_ref[...], form, preferred_element_type=jnp.float32)
 
@@ -235,7 +235,9 @@
         rim_ref[part, 0] = dual_ref[0, part, ROWS - 1]
 
 
-def second_kernel(in_ref, weight_ref, table_ref, out_ref):
+def second_kernel(in_ref, kern_ref, spread_ref, table_ref, out_ref):
+    weight = weights(kern_ref, spread_ref)
+
     def place(x, r, t):
         return pl.ds((r - x) % 4 * TILES + t, 16, stride=4 * TILES)
 
@@ -249,7 +251,7 @@
         residues.append(jnp.concatenate(rows, axis=0))
     spectrum = forward(lambda r: table_ref[0, r], lambda r: None, residues)
     weighted = [
-        part * weight_ref[q * QUARTER : (q + 1) * QUARTER, :] for q, part in enumerate(spectrum)
+        part * weight[q * QUARTER : (q + 1) * QUARTER, :] for q, part in enumerate(spectrum)
     ]
     result = backward(lambda r: table_ref[1, r], lambda r: None, weighted)
     lower = slot_of_lane(16) < 2
@@ -395,12 +397,6 @@
     )
     first, second, third, spread = tables()
     contrasts = lax.axis_size("con")
-    weight = pl.pallas_call(
-        weight_kernel,
-        out_shape=jax.ShapeDtypeStruct((PADDED, WIDE), jnp.float32),
-        compiler_params=PARAMS,
-        name="weights",
-    )(kern, spread)
     whole = pl.BlockSpec(memory_space=pltpu.HBM)
     bands = pl.pallas_call(
         first_kernel,
@@ -414,9 +410,16 @@
             pltpu.VMEM((2 * ROWS * PIECE, FULL), jnp.float32),
             pltpu.SemaphoreType.DMA((6,)),
         ],
-        compiler_params=pltpu.CompilerParams(vmem_limit_bytes=56 * 2**20),
+        compiler_params=pltpu.CompilerParams(vmem_limit_bytes=53 * 2**20),
         name="first",
     )(image, sens, first)
+    returned = pl.pallas_call(
+        second_kernel,
+        out_shape=jax.ShapeDtypeStruct((SLABS * BACK_TILES, LANES), jnp.float32),
+        compiler_params=PARAMS,
+        name="second",
+    )(exchange(bands), kern.reshape(BAND, 1, PADDED), spread, second)
+    *late, returned = lax.optimization_barrier((image, adjoint_data, dual, sens, returned))
     edge, rim, sens_rows = pl.pallas_call(
         edge_kernel,
         out_shape=(
@@ -426,15 +429,9 @@
         ),
         compiler_params=PARAMS,
         name="edge",
-    )(image, adjoint_data, dual, sens)
+    )(*late)
     edge = shifted(edge, "slab", -1)
     rim = shifted(rim, "slab", 1)
-    returned = pl.pallas_call(
-        second_kernel,
-        out_shape=jax.ShapeDtypeStruct((SLABS * BACK_TILES, LANES), jnp.float32),
-        compiler_params=PARAMS,
-        name="second",
-    )(exchange(bands), weight, second)
     is_last = (lax.axis_index("slab") == SLABS - 1).astype(jnp.int32).reshape(1)
     moved, energy = pl.pallas_call(
         third_kernel,

time: 104 us -> 105 us (level)
  blocking collectives: 9.61 us -> 58.9 us
  waiting for transfers between devices: 55.7 us -> 26.3 us
  starting transfers between devices: 30.4 us -> 10.5 us
  local copies, waits for them, and re-layouts: 0.04 us -> 1.84 us
    all_to_all x0 -> x1, blocking collectives: none -> 49.3 us  [exchange(): lax.all_to_all(blocks, 'slab', 0, 0, tiled=True)]
    all_to_all x2 -> x1, waiting for transfers between devices: 38 us -> 8.59 us  [exchange(): lax.all_to_all(blocks, 'slab', 0, 0, tiled=True)]
    all_to_all x2 -> x1, starting transfers between devices: 24.8 us -> 4.94 us  [exchange(): lax.all_to_all(blocks, 'slab', 0, 0, tiled=True)]
    unnamed x17 -> x20, local copies, waits for them, and re-layouts: 0.04 us -> 1.84 us
  transfers between devices with their start and end apart: 4 -> 3, of which waited for: 4 -> 3; matrix products, arithmetic and copies ran while one was open for 0% -> 0% of each run, Pallas kernels for 1% -> 0%
where the time goes in v4:
time: 105 us
  blocking collectives  58.9 us (56%)
  waiting for transfers between devices  26.3 us (25%)
  starting transfers between devices  10.5 us (10%)
  Pallas kernels  6.73 us (6%)
  local copies, waits for them, and re-layouts  1.84 us (2%)
    all_to_all x1, blocking collectives, exchange(): lax.all_to_all(blocks, 'slab', 0, 0, tiled=True)  49.3 us
    ppermute x2, waiting for transfers between devices, shifted(): return lax.ppermute(value, axis, pairs)  17.7 us
    all_to_all x1, blocking collectives, local(): lax.all_to_all(energy, 'con', 0, 0, tiled=True)  9.61 us
    all_to_all x1, waiting for transfers between devices, exchange(): lax.all_to_all(blocks, 'slab', 0, 0, tiled=True)  8.59 us
    ppermute x2, starting transfers between devices, shifted(): return lax.ppermute(value, axis, pairs)  5.56 us
    all_to_all x1, starting transfers between devices, exchange(): lax.all_to_all(blocks, 'slab', 0, 0, tiled=True)  4.94 us
    pallas_call x1, Pallas kernels, local(): pl.pallas_call(second_kernel, out_shape=jax.ShapeDtypeStruct((SLABS * BAC...  2.4 us
    pallas_call x1, Pallas kernels, local(): pl.pallas_call(first_kernel, in_specs=[whole] * 3, out_shape=jax.ShapeDty...  2.36 us
  transfers between devices with their start and end apart: 3, of which 3 were waited for; matrix products, arithmetic and copies ran while one was open for 0% of the time, Pallas kernels for 0%

profile of v4, /device:TPU:1, one launch (start us, length us, event | category | flops | bytes accessed | tf_op | source)
XLA Modules:
  0.0 105.1 jit_solution(11862095279062393994)
XLA Ops:
  0.6 0.0 copy-start
  0.6 0.0 copy-start.1
  0.7 1.0 copy-done.1
  1.7 0.0 copy-start.5
  1.7 0.8 copy-done.5
  2.4 0.0 copy-start.8
  2.4 0.0 copy-start.9
  2.4 2.4 %first.1 = f32[832,128]{1,0:T(8,128)S(1)} custom-call(f32[1,2,5,2,320]{4,3,2,1,0:T(2,128)S(1)} %bitcast.19, f32[8,2,5,2,320]{4,3,2,1,0:T(2,128)S(1)} %bitcast.15, bf16[4,2,160,160]{3,2,1,0:T(8,128)(2,1)} %constant.14.clone.table_hbm), custom_call_target="tpu_custom_call" | custom-call | tf_op jit(solution)/shard_map/first/pallas_call | solution.py:401
  4.8 49.3 %all_to_all.15 = f32[64,1,1664]{2,1,0:T(1,128)S(1)} all-to-all(f32[64,1,1664]{2,1,0:T(1,128)S(1)} %bitcast.14), channel_id=1, replica_groups=mesh['con'=8,'slab'=64] {'slab'}, dimensions={0} | all-to-all | bytes 851968 | tf_op jit(solution)/shard_map/all_to_all | solution.py:385
  54.1 0.0 copy-done
  54.1 0.0 copy-done.8
  54.1 0.0 copy-done.9
  54.1 0.0 copy-start.2
  54.1 0.0 copy-start.4
  54.1 0.0 copy-start.6
  54.2 0.0 copy-start.7
  54.2 0.0 copy-start.3
  54.2 2.4 %second.1 = f32[960,128]{1,0:T(8,128)} custom-call(f32[832,128]{1,0:T(8,128)S(1)} %bitcast.13, f32[10,1,640]{2,1,0:T(1,128)S(1)} %bitcast.24, bf16[10,384]{1,0:T(8,128)(2,1)S(1)} %copy-done.9, bf16[2,4,160,480]{3,2,1,0:T(8,128)(2,1)S(1)} %copy-done), custom_call_target="tpu_custom_call" | custom-call | tf_op jit(solution)/shard_map/second/pallas_call | solution.py:416
  56.6 4.9 %all-to-all-start.1 = ((f32[64,1,1920]{2,1,0:T(1,128)}), f32[64,1,1920]{2,1,0:T(1,128)S(1)}, u32[]{:S(2)}, u32[]{:S(2)}) async-start(f32[64,1,1920]{2,1,0:T(1,128)} %bitcast.8), calls=%async_computation.1 | async-start | bytes 983040 | tf_op jit(solution)/shard_map/all_to_all | solution.py:385
  61.5 0.0 copy-done.2
  61.5 0.0 copy-done.4
  61.5 0.0 copy-done.6
  61.6 0.0 copy-done.7
  61.6 0.1 edge.1
  61.7 2.4 %collective-permute-start = (f32[26,1,2,320]{3,2,1,0:T(2,128)S(1)}, f32[26,1,2,320]{3,2,1,0:T(2,128)S(1)}, u32[]{:S(2)}, u32[]{:S(2)}) collective-permute-start(f32[26,1,2,320]{3,2,1,0:T(2,128)S(1)} %get-tuple-element.20), channel_id=1, source_target_pairs={{1,0},{2,1},{3,2},{4,3},{5,4},{6,5},{7,6},{8,7},{9,8},{10,9},{11,1... | collective-permute-start | bytes 199688 | tf_op jit(solution)/shard_map/ppermute | solution.py:391
  64.0 3.2 %collective-permute-start.1 = (f32[2,1,2,320]{3,2,1,0:T(2,128)S(1)}, f32[2,1,2,320]{3,2,1,0:T(2,128)S(1)}, u32[]{:S(2)}, u32[]{:S(2)}) collective-permute-start(f32[2,1,2,320]{3,2,1,0:T(2,128)S(1)} %get-tuple-element.21), channel_id=1, source_target_pairs={{0,1},{1,2},{2,3},{3,4},{4,5},{5,6},{6,7},{7,8},{8,9},{9,10},{10,1... | collective-permute-start | bytes 15368 | tf_op jit(solution)/shard_map/ppermute | solution.py:391
  67.2 8.8 %collective-permute-done.1.rim_ref = f32[2,1,2,320]{3,2,1,0:T(2,128)S(1)} collective-permute-done((f32[2,1,2,320]{3,2,1,0:T(2,128)S(1)}, f32[2,1,2,320]{3,2,1,0:T(2,128)S(1)}, u32[]{:S(2)}, u32[]{:S(2)}) %collective-permute-start.1) | collective-permute-done | bytes 5152 | tf_op jit(solution)/shard_map/ppermute | solution.py:391
  76.1 8.9 %collective-permute-done.edge_ref = f32[26,1,2,320]{3,2,1,0:T(2,128)S(1)} collective-permute-done((f32[26,1,2,320]{3,2,1,0:T(2,128)S(1)}, f32[26,1,2,320]{3,2,1,0:T(2,128)S(1)}, u32[]{:S(2)}, u32[]{:S(2)}) %collective-permute-start) | collective-permute-done | bytes 66592 | tf_op jit(solution)/shard_map/ppermute | solution.py:391
  85.0 8.6 %all-to-all-done.1 = f32[64,1,1920]{2,1,0:T(1,128)S(1)} async-done(((f32[64,1,1920]{2,1,0:T(1,128)}), f32[64,1,1920]{2,1,0:T(1,128)S(1)}, u32[]{:S(2)}, u32[]{:S(2)}) %all-to-all-start.1) | async-done | bytes 491552 | tf_op jit(solution)/shard_map/all_to_all | solution.py:385
  93.6 0.0 copy-done.3
  93.6 1.2 %third.1 = (f32[8,16,384]{2,1,0:T(8,128)S(1)}, f32[8,30,128]{2,1,0:T(8,128)S(1)}) custom-call(s32[1]{0:T(128)} %bitcast.last_ref, f32[960,128]{1,0:T(8,128)S(1)} %bitcast.12, f32[160,320]{1,0:T(8,128)S(1)} %get-tuple-element.19.rows_ref, bf16[2,4,160,160]{3,2,1,0:T(8,128)(2,1)S(1)} %copy-done.3, f32[1,2,5,2,320]{4,3,2,1,0:T(2,128)S(1)} %bitcast.21, ...), custom_call_target="tpu_custom_call" | custom-call | tf_op jit(solution)/shard_map/third/pallas_call | solution.py:436
  94.8 9.6 %all_to_all.16.energy_ref = f32[8,30,128]{2,1,0:T(8,128)S(1)} all-to-all(f32[8,30,128]{2,1,0:T(8,128)S(1)} %get-tuple-element.22), channel_id=1, replica_groups=mesh['con'=8,'slab'=64] {'con'}, dimensions={0} | all-to-all | bytes 245760 | tf_op jit(solution)/shard_map/all_to_all | solution.py:460
  104.4 0.7 last.1
Async XLA Ops:
  0.6 53.5 %copy-start = (bf16[2,4,160,480]{3,2,1,0:T(8,128)(2,1)S(1)}, bf16[2,4,160,480]{3,2,1,0:T(8,128)(2,1)}, u32[]{:S(2)}) copy-start(bf16[2,4,160,480]{3,2,1,0:T(8,128)(2,1)} %constant.16.clone.table_ref) | copy-start | bytes 3686404
  0.6 1.0 copy-start.1
  1.7 0.8 copy-start.5
  2.4 51.7 %copy-start.8 = (f32[1,10,640]{2,0,1:T(1,128)S(1)}, f32[1,10,640]{2,0,1:T(1,128)}, u32[]{:S(2)}) copy-start(f32[1,10,640]{2,0,1:T(1,128)} %param.13) | copy-start | bytes 76804
  2.4 51.7 %copy-start.9 = (bf16[10,384]{1,0:T(8,128)(2,1)S(1)}, bf16[10,384]{1,0:T(8,128)(2,1)}, u32[]{:S(2)}) copy-start(bf16[10,384]{1,0:T(8,128)(2,1)} %constant.15.clone.spread_ref) | copy-start | bytes 23044
  54.1 7.4 %copy-start.2 = (f32[8,2,2,5,320]{4,2,3,1,0:T(2,128)S(1)}, f32[8,2,2,5,320]{4,2,3,1,0:T(2,128)}, u32[]{:S(2)}) copy-start(f32[8,2,2,5,320]{4,2,3,1,0:T(2,128)} %param.12) | copy-start | bytes 614404
  54.1 7.4 %copy-start.4 = (f32[1,6,2,5,320]{4,2,3,1,0:T(2,128)S(1)}, f32[1,6,2,5,320]{4,2,3,1,0:T(2,128)}, u32[]{:S(2)}) copy-start(f32[1,6,2,5,320]{4,2,3,1,0:T(2,128)} %param.10) | copy-start | bytes 230404
  54.1 7.4 %copy-start.6 = (f32[1,2,2,5,320]{4,2,3,1,0:T(2,128)S(1)}, f32[1,2,2,5,320]{4,2,3,1,0:T(2,128)}, u32[]{:S(2)}) copy-start(f32[1,2,2,5,320]{4,2,3,1,0:T(2,128)} %param.9) | copy-start | bytes 76804
  54.2 7.4 %copy-start.7 = (f32[1,2,2,5,320]{4,2,3,1,0:T(2,128)S(1)}, f32[1,2,2,5,320]{4,2,3,1,0:T(2,128)}, u32[]{:S(2)}) copy-start(f32[1,2,2,5,320]{4,2,3,1,0:T(2,128)} %param.11) | copy-start | bytes 76804
  54.2 39.4 %copy-start.3 = (bf16[2,4,160,160]{3,2,1,0:T(8,128)(2,1)S(1)}, bf16[2,4,160,160]{3,2,1,0:T(8,128)(2,1)}, u32[]{:S(2)}) copy-start(bf16[2,4,160,160]{3,2,1,0:T(8,128)(2,1)} %constant.17.clone.table_ref) | copy-start | bytes 1228804
  56.6 37.0 %all-to-all-start.1 = ((f32[64,1,1920]{2,1,0:T(1,128)}), f32[64,1,1920]{2,1,0:T(1,128)S(1)}, u32[]{:S(2)}, u32[]{:S(2)}) async-start(f32[64,1,1920]{2,1,0:T(1,128)} %bitcast.8), calls=%async_computation.1 | async-start | bytes 983040 | tf_op jit(solution)/shard_map/all_to_all | solution.py:385
  61.7 23.3 %collective-permute-start = (f32[26,1,2,320]{3,2,1,0:T(2,128)S(1)}, f32[26,1,2,320]{3,2,1,0:T(2,128)S(1)}, u32[]{:S(2)}, u32[]{:S(2)}) collective-permute-start(f32[26,1,2,320]{3,2,1,0:T(2,128)S(1)} %get-tuple-element.20), channel_id=1, source_target_pairs={{1,0},{2,1},{3,2},{4,3},{5,4},{6,5},{7,6},{8,7},{9,8},{10,9},{11,1... | collective-permute-start | bytes 199688 | tf_op jit(solution)/shard_map/ppermute | solution.py:391
  64.0 12.0 %collective-permute-start.1 = (f32[2,1,2,320]{3,2,1,0:T(2,128)S(1)}, f32[2,1,2,320]{3,2,1,0:T(2,128)S(1)}, u32[]{:S(2)}, u32[]{:S(2)}) collective-permute-start(f32[2,1,2,320]{3,2,1,0:T(2,128)S(1)} %get-tuple-element.21), channel_id=1, source_target_pairs={{0,1},{1,2},{2,3},{3,4},{4,5},{5,6},{6,7},{7,8},{8,9},{9,10},{10,1... | collective-permute-start | bytes 15368 | tf_op jit(solution)/shard_map/ppermute | solution.py:391

commit v5 on v3

--- a/solution.py
+++ b/solution.py
@@ -414,9 +414,9 @@
             pltpu.VMEM((2 * ROWS * PIECE, FULL), jnp.float32),
             pltpu.SemaphoreType.DMA((6,)),
         ],
-        compiler_params=pltpu.CompilerParams(vmem_limit_bytes=56 * 2**20),
+        compiler_params=PARAMS,
         name="first",
-    )(image, sens, first)
+    )(*(pltpu.with_memory_space_constraint(v, pltpu.HBM) for v in (image, sens, first)))
     edge, rim, sens_rows = pl.pallas_call(
         edge_kernel,
         out_shape=(
@@ -429,13 +429,16 @@
     )(image, adjoint_data, dual, sens)
     edge = shifted(edge, "slab", -1)
     rim = shifted(rim, "slab", 1)
+    is_last = (lax.axis_index("slab") == SLABS - 1).astype(jnp.int32).reshape(1)
+    bands, edge, rim, is_last, sens_rows = lax.optimization_barrier(
+        (exchange(bands), edge, rim, is_last, sens_rows)
+    )
     returned = pl.pallas_call(
         second_kernel,
         out_shape=jax.ShapeDtypeStruct((SLABS * BACK_TILES, LANES), jnp.float32),
         compiler_params=PARAMS,
         name="second",
-    )(exchange(bands), weight, second)
-    is_last = (lax.axis_index("slab") == SLABS - 1).astype(jnp.int32).reshape(1)
+    )(bands, weight, second)
     moved, energy = pl.pallas_call(
         third_kernel,
         in_specs=[pl.BlockSpec(memory_space=pltpu.SMEM)]

time: 104 us -> 104 us (level)
  blocking collectives: 9.61 us -> 46.7 us
  waiting for transfers between devices: 55.7 us -> 23.7 us
  starting transfers between devices: 30.4 us -> 25.3 us
    all_to_all x0 -> x1, blocking collectives: none -> 37.1 us  [exchange(): lax.all_to_all(blocks, 'slab', 0, 0, tiled=True)]
    all_to_all x2 -> x1, waiting for transfers between devices: 38 us -> 9.19 us  [exchange(): lax.all_to_all(blocks, 'slab', 0, 0, tiled=True)]
    all_to_all x2 -> x1, starting transfers between devices: 24.8 us -> 19.8 us  [exchange(): lax.all_to_all(blocks, 'slab', 0, 0, tiled=True)]
    ppermute x2, waiting for transfers between devices: 17.7 us -> 14.5 us  [shifted(): return lax.ppermute(value, axis, pairs)]
  transfers between devices with their start and end apart: 4 -> 3, of which waited for: 4 -> 3; matrix products, arithmetic and copies ran while one was open for 0% -> 0% of each run, Pallas kernels for 1% -> 1%
where the time goes in v5:
time: 104 us; the launch traced here: 103 us
  blocking collectives  46.7 us (45%)
  starting transfers between devices  25.3 us (24%)
  waiting for transfers between devices  23.7 us (23%)
  Pallas kernels  6.81 us (7%)
    all_to_all x1, blocking collectives, exchange(): lax.all_to_all(blocks, 'slab', 0, 0, tiled=True)  37.1 us
    all_to_all x1, starting transfers between devices, exchange(): lax.all_to_all(blocks, 'slab', 0, 0, tiled=True)  19.8 us
    ppermute x2, waiting for transfers between devices, shifted(): return lax.ppermute(value, axis, pairs)  14.5 us
    all_to_all x1, blocking collectives, local(): lax.all_to_all(energy, 'con', 0, 0, tiled=True)  9.62 us
    all_to_all x1, waiting for transfers between devices, exchange(): lax.all_to_all(blocks, 'slab', 0, 0, tiled=True)  9.19 us
    ppermute x2, starting transfers between devices, shifted(): return lax.ppermute(value, axis, pairs)  5.56 us
    pallas_call x1, Pallas kernels, local(): pl.pallas_call(first_kernel, in_specs=[whole] * 3, out_shape=jax.ShapeDty...  2.98 us
  transfers between devices with their start and end apart: 3, of which 3 were waited for; matrix products, arithmetic and copies ran while one was open for 0% of the time, Pallas kernels for 1%

profile of v5, /device:TPU:1, one launch (start us, length us, event | category | flops | bytes accessed | tf_op | source)
XLA Modules:
  0.0 103.4 jit_solution(5520614795252119247)
XLA Ops:
  0.6 0.0 copy-start.1
  0.6 0.0 copy-start.4
  0.7 0.0 copy-start.5
  0.7 0.0 copy-start.3
  0.7 0.0 copy-start.7
  0.7 0.0 copy-start.6
  0.7 3.0 %first.1 = f32[832,128]{1,0:T(8,128)} custom-call(f32[1,2,5,2,320]{4,3,2,1,0:T(2,128)} %bitcast.18, f32[8,2,5,2,320]{4,3,2,1,0:T(2,128)} %bitcast.14, bf16[4,2,160,160]{3,2,1,0:T(8,128)(2,1)} %constant.15.clone.table_hbm), custom_call_target="tpu_custom_call" | custom-call | tf_op jit(solution)/shard_map/first/pallas_call | solution.py:405
  3.7 0.0 copy-start
  3.7 19.8 %all-to-all-start = ((f32[64,1,1664]{2,1,0:T(1,128)}), f32[64,1,1664]{2,1,0:T(1,128)S(1)}, u32[]{:S(2)}, u32[]{:S(2)}) async-start(f32[64,1,1664]{2,1,0:T(1,128)} %bitcast.2), calls=%async_computation | async-start | bytes 851968 | tf_op jit(solution)/shard_map/all_to_all | solution.py:383
  23.5 0.0 copy-done.1
  23.5 0.0 copy-done.4
  23.5 0.0 copy-done.5
  23.5 0.0 copy-done.3
  23.5 0.1 edge.1
  23.6 2.4 %collective-permute-start = (f32[26,1,2,320]{3,2,1,0:T(2,128)S(1)}, f32[26,1,2,320]{3,2,1,0:T(2,128)S(1)}, u32[]{:S(2)}, u32[]{:S(2)}) collective-permute-start(f32[26,1,2,320]{3,2,1,0:T(2,128)S(1)} %get-tuple-element.14), channel_id=1, source_target_pairs={{1,0},{2,1},{3,2},{4,3},{5,4},{6,5},{7,6},{8,7},{9,8},{10,9},{11,1... | collective-permute-start | bytes 199688 | tf_op jit(solution)/shard_map/ppermute | solution.py:389
  26.0 3.2 %collective-permute-start.1 = (f32[2,1,2,320]{3,2,1,0:T(2,128)S(1)}, f32[2,1,2,320]{3,2,1,0:T(2,128)S(1)}, u32[]{:S(2)}, u32[]{:S(2)}) collective-permute-start(f32[2,1,2,320]{3,2,1,0:T(2,128)S(1)} %get-tuple-element.15), channel_id=1, source_target_pairs={{0,1},{1,2},{2,3},{3,4},{4,5},{5,6},{6,7},{7,8},{8,9},{9,10},{10,1... | collective-permute-start | bytes 15368 | tf_op jit(solution)/shard_map/ppermute | solution.py:389
  29.2 0.0 copy-done.7
  29.2 0.0 copy-done.6
  29.2 0.5 weights.1.weight_ref
  29.7 5.7 %collective-permute-done.1.rim_ref = f32[2,1,2,320]{3,2,1,0:T(2,128)S(1)} collective-permute-done((f32[2,1,2,320]{3,2,1,0:T(2,128)S(1)}, f32[2,1,2,320]{3,2,1,0:T(2,128)S(1)}, u32[]{:S(2)}, u32[]{:S(2)}) %collective-permute-start.1) | collective-permute-done | bytes 5152 | tf_op jit(solution)/shard_map/ppermute | solution.py:389
  35.3 8.8 %collective-permute-done.edge_ref = f32[26,1,2,320]{3,2,1,0:T(2,128)S(1)} collective-permute-done((f32[26,1,2,320]{3,2,1,0:T(2,128)S(1)}, f32[26,1,2,320]{3,2,1,0:T(2,128)S(1)}, u32[]{:S(2)}, u32[]{:S(2)}) %collective-permute-start) | collective-permute-done | bytes 66592 | tf_op jit(solution)/shard_map/ppermute | solution.py:389
  44.1 9.2 %all-to-all-done = f32[64,1,1664]{2,1,0:T(1,128)S(1)} async-done(((f32[64,1,1664]{2,1,0:T(1,128)}), f32[64,1,1664]{2,1,0:T(1,128)S(1)}, u32[]{:S(2)}, u32[]{:S(2)}) %all-to-all-start) | async-done | bytes 426016 | tf_op jit(solution)/shard_map/all_to_all | solution.py:383
  53.3 0.0 copy-done
  53.3 0.0 copy-start.2
  53.3 1.4 %second.1 = f32[960,128]{1,0:T(8,128)S(1)} custom-call(f32[832,128]{1,0:T(8,128)S(1)} %bitcast.13, f32[640,384]{1,0:T(8,128)S(1)} %weights.1.weight_ref, bf16[2,4,160,480]{3,2,1,0:T(8,128)(2,1)S(1)} %copy-done), custom_call_target="tpu_custom_call" | custom-call | tf_op jit(solution)/shard_map/second/pallas_call | solution.py:436
  54.7 37.1 %all_to_all.15 = f32[64,1,1920]{2,1,0:T(1,128)S(1)} all-to-all(f32[64,1,1920]{2,1,0:T(1,128)S(1)} %bitcast.11), channel_id=1, replica_groups=mesh['con'=8,'slab'=64] {'slab'}, dimensions={0} | all-to-all | bytes 983040 | tf_op jit(solution)/shard_map/all_to_all | solution.py:383
  91.9 0.0 copy-done.2
  91.9 1.2 %third.1 = (f32[8,16,384]{2,1,0:T(8,128)S(1)}, f32[8,30,128]{2,1,0:T(8,128)S(1)}) custom-call(s32[1]{0:T(128)} %bitcast.6.last_ref, f32[960,128]{1,0:T(8,128)S(1)} %bitcast.12, f32[160,320]{1,0:T(8,128)S(1)} %get-tuple-element.19.rows_ref, bf16[2,4,160,160]{3,2,1,0:T(8,128)(2,1)S(1)} %copy-done.2, f32[1,2,5,2,320]{4,3,2,1,0:T(2,128)S(1)} %bitcast.20, ...), custom_call_target="tpu_custom_call" | custom-call | tf_op jit(solution)/shard_map/third/pallas_call | solution.py:442
  93.1 9.6 %all_to_all.16.energy_ref = f32[8,30,128]{2,1,0:T(8,128)S(1)} all-to-all(f32[8,30,128]{2,1,0:T(8,128)S(1)} %get-tuple-element.22), channel_id=1, replica_groups=mesh['con'=8,'slab'=64] {'con'}, dimensions={0} | all-to-all | bytes 245760 | tf_op jit(solution)/shard_map/all_to_all | solution.py:466
  102.7 0.7 last.1
  (1 shorter events, 0.0 us)
Async XLA Ops:
  0.6 22.8 %copy-start.1 = (f32[8,2,2,5,320]{4,2,3,1,0:T(2,128)S(1)}, f32[8,2,2,5,320]{4,2,3,1,0:T(2,128)}, u32[]{:S(2)}) copy-start(f32[8,2,2,5,320]{4,2,3,1,0:T(2,128)} %param.12) | copy-start | bytes 614404
  0.6 22.8 %copy-start.4 = (f32[1,2,2,5,320]{4,2,3,1,0:T(2,128)S(1)}, f32[1,2,2,5,320]{4,2,3,1,0:T(2,128)}, u32[]{:S(2)}) copy-start(f32[1,2,2,5,320]{4,2,3,1,0:T(2,128)} %param.9) | copy-start | bytes 76804
  0.7 22.8 %copy-start.5 = (f32[1,2,2,5,320]{4,2,3,1,0:T(2,128)S(1)}, f32[1,2,2,5,320]{4,2,3,1,0:T(2,128)}, u32[]{:S(2)}) copy-start(f32[1,2,2,5,320]{4,2,3,1,0:T(2,128)} %param.11) | copy-start | bytes 76804
  0.7 22.8 %copy-start.3 = (f32[1,6,2,5,320]{4,2,3,1,0:T(2,128)S(1)}, f32[1,6,2,5,320]{4,2,3,1,0:T(2,128)}, u32[]{:S(2)}) copy-start(f32[1,6,2,5,320]{4,2,3,1,0:T(2,128)} %param.10) | copy-start | bytes 230404
  0.7 28.5 %copy-start.7 = (f32[1,10,640]{2,0,1:T(1,128)S(1)}, f32[1,10,640]{2,0,1:T(1,128)}, u32[]{:S(2)}) copy-start(f32[1,10,640]{2,0,1:T(1,128)} %param.13) | copy-start | bytes 76804
  0.7 28.5 %copy-start.6 = (bf16[10,384]{1,0:T(8,128)(2,1)S(1)}, bf16[10,384]{1,0:T(8,128)(2,1)}, u32[]{:S(2)}) copy-start(bf16[10,384]{1,0:T(8,128)(2,1)} %constant.14.clone.spread_ref) | copy-start | bytes 23044
  3.7 49.7 %copy-start = (bf16[2,4,160,480]{3,2,1,0:T(8,128)(2,1)S(1)}, bf16[2,4,160,480]{3,2,1,0:T(8,128)(2,1)}, u32[]{:S(2)}) copy-start(bf16[2,4,160,480]{3,2,1,0:T(8,128)(2,1)} %constant.16.clone.table_ref) | copy-start | bytes 3686404
  3.7 49.6 %all-to-all-start = ((f32[64,1,1664]{2,1,0:T(1,128)}), f32[64,1,1664]{2,1,0:T(1,128)S(1)}, u32[]{:S(2)}, u32[]{:S(2)}) async-start(f32[64,1,1664]{2,1,0:T(1,128)} %bitcast.2), calls=%async_computation | async-start | bytes 851968 | tf_op jit(solution)/shard_map/all_to_all | solution.py:383
  23.6 20.6 %collective-permute-start = (f32[26,1,2,320]{3,2,1,0:T(2,128)S(1)}, f32[26,1,2,320]{3,2,1,0:T(2,128)S(1)}, u32[]{:S(2)}, u32[]{:S(2)}) collective-permute-start(f32[26,1,2,320]{3,2,1,0:T(2,128)S(1)} %get-tuple-element.14), channel_id=1, source_target_pairs={{1,0},{2,1},{3,2},{4,3},{5,4},{6,5},{7,6},{8,7},{9,8},{10,9},{11,1... | collective-permute-start | bytes 199688 | tf_op jit(solution)/shard_map/ppermute | solution.py:389
  26.0 9.4 %collective-permute-start.1 = (f32[2,1,2,320]{3,2,1,0:T(2,128)S(1)}, f32[2,1,2,320]{3,2,1,0:T(2,128)S(1)}, u32[]{:S(2)}, u32[]{:S(2)}) collective-permute-start(f32[2,1,2,320]{3,2,1,0:T(2,128)S(1)} %get-tuple-element.15), channel_id=1, source_target_pairs={{0,1},{1,2},{2,3},{3,4},{4,5},{5,6},{6,7},{7,8},{8,9},{9,10},{10,1... | collective-permute-start | bytes 15368 | tf_op jit(solution)/shard_map/ppermute | solution.py:389
  53.3 38.5 %copy-start.2 = (bf16[2,4,160,160]{3,2,1,0:T(8,128)(2,1)S(1)}, bf16[2,4,160,160]{3,2,1,0:T(8,128)(2,1)}, u32[]{:S(2)}) copy-start(bf16[2,4,160,160]{3,2,1,0:T(8,128)(2,1)} %constant.17.clone.table_ref) | copy-start | bytes 1228804

commit v6 on v5

--- a/solution.py
+++ b/solution.py
@@ -42,6 +42,11 @@
     return high, low
 
 
+def stack_depth(value):
+    high, low = np_split(value)
+    return np.concatenate([high, high, low], axis=-1)
+
+
 @functools.cache
 def tables():
     low = np.arange(QUARTER)
@@ -68,21 +73,18 @@
         for part in range(2):
             at = b // 4 * LANES + part * 64 + b % 4 * PIECE
             spread[b, at : at + PIECE] = 1.0
-    first = np.stack(np_split(along_y), axis=1)
-    second = np.stack([np.concatenate([h, h, l], axis=2) for h, l in (np_split(along_x), np_split(back_x))])
-    third = np.stack(np_split(back_y))
-    return first, second, third, spread.astype(ml_dtypes.bfloat16)
+    first, back_y = stack_depth(along_y), stack_depth(back_y)
+    second = np.stack([stack_depth(along_x), stack_depth(back_x)])
+    return first, second, back_y, spread.astype(ml_dtypes.bfloat16)
 
 
 def dot(left, right):
     return jnp.dot(left, right, preferred_element_type=jnp.float32)
 
 
-def dot3(left_high, left_low, right):
+def dot3(left, right):
     high, low = split(right)
-    if right.shape[1] > 256:
-        return dot(left_high, jnp.concatenate([high, low, high], axis=0))
-    return dot(left_high, high) + dot(left_high, low) + dot(left_low, high)
+    return dot(left, jnp.concatenate([high, low, high], axis=0))
 
 
 def turn(value, shift):
@@ -104,15 +106,18 @@
     return result
 
 
+def trade(left, right, step, slots):
+    low = slots // step % 2 == 0
+    shift = PIECE * step
+    return jnp.where(low, left, turn(right, shift)), jnp.where(low, turn(left, -shift), right)
+
+
 def transpose_pieces(tiles, slots):
-    result = list(tiles)
-    for step in (1, 2):
-        low = slots // step % 2 == 0
-        for at in (0, 1) if step == 2 else (0, 2):
-            left, right = result[at], result[at + step]
-            result[at] = jnp.where(low, left, turn(right, PIECE * step))
-            result[at + step] = jnp.where(low, turn(left, -PIECE * step), right)
-    return result
+    a0, a1 = trade(tiles[0], tiles[1], 1, slots)
+    a2, a3 = trade(tiles[2], tiles[3], 1, slots)
+    b0, b2 = trade(a0, a2, 2, slots)
+    b1, b3 = trade(a1, a3, 2, slots)
+    return b0, b1, b2, b3
 
 
 def times_minus_i(value):
@@ -131,19 +136,19 @@
     return even + odd, apart + turned, even - odd, apart - turned
 
 
-def forward(high_ref_of, low_ref_of, residues):
+def forward(table, residues):
     parts = []
     for r in range(4):
         data = jnp.concatenate([residues[r], times_minus_i(residues[r])], axis=0)
-        parts.append(dot3(high_ref_of(r), low_ref_of(r), data))
+        parts.append(dot3(table[r], data))
     return butterfly(*parts)
 
 
-def backward(high_ref_of, low_ref_of, quarters):
+def backward(table, quarters):
     sums = butterfly(*quarters)
     result = []
     for r, at in enumerate((0, 3, 2, 1)):
-        both = dot3(high_ref_of(r), low_ref_of(r), sums[at])
+        both = dot3(table[r], sums[at])
         result.append(both[:80] - times_minus_i(both[80:]))
     return result
 
@@ -191,11 +196,7 @@
 
     for r in range(4):
         copies[2 + r].wait()
-
-    def table(r, level):
-        return table_ref[r, level]
-
-    bands = forward(lambda r: table(r, 0), lambda r: table(r, 1), residues)
+    bands = forward(table_ref, residues)
     slots = slot_of_lane(16)
     for q in range(4):
         start = 16 * q * TILES
@@ -209,9 +210,8 @@
             for x, value in enumerate(transpose_pieces(near[4 * g : 4 * g + 4], slots)):
                 put(2 * x + g, value)
             put(8 + g, gather_pieces([(far[4 * g + i], 0) for i in range(4)], slots))
-        for pair in range(2):
-            pieces = [(near[8 + i], 2 * pair + x) for x in range(2) for i in range(2)]
-            put(10 + pair, gather_pieces(pieces, slots))
+        for pair, value in enumerate(trade(*trade(near[8], near[9], 1, slots), 2, slots)):
+            put(10 + pair, value)
         put(12, gather_pieces([(far[8], 0), (far[9], 0)], slots))
 
 
@@ -247,11 +247,11 @@
             whole = [in_ref[place(x, r, 2 * x), :], in_ref[place(x, r, 2 * x + 1), :]]
             rows.append(jnp.concatenate(whole + [rest], axis=1))
         residues.append(jnp.concatenate(rows, axis=0))
-    spectrum = forward(lambda r: table_ref[0, r], lambda r: None, residues)
+    spectrum = forward(table_ref.at[0], residues)
     weighted = [
         part * weight_ref[q * QUARTER : (q + 1) * QUARTER, :] for q, part in enumerate(spectrum)
     ]
-    result = backward(lambda r: table_ref[1, r], lambda r: None, weighted)
+    result = backward(table_ref.at[1], weighted)
     lower = slot_of_lane(16) < 2
     for s in range(4):
 
@@ -281,13 +281,13 @@
         near, far = [], []
         for g in range(2):
             near += transpose_pieces([tiles[2 * x + g] for x in range(4)], slots)
-            far += [gather_pieces([(tiles[8 + g], i), (tiles[10 + g], i)], slots) for i in range(4)]
-        for i in range(2):
-            near.append(gather_pieces([(tiles[12 + x // 2], x % 2 * 2 + i) for x in range(4)], slots))
-            far.append(gather_pieces([(tiles[14], i), (tiles[14], 2 + i)], slots))
+            pairs = trade(tiles[8 + g], tiles[10 + g], 1, slots)
+            far += [*pairs, *(turn(value, -2 * PIECE) for value in pairs)]
+        near += trade(*trade(tiles[12], tiles[13], 2, slots), 1, slots)
+        far += trade(tiles[14], turn(tiles[14], -2 * PIECE), 1, slots)
         columns = [jnp.concatenate(near, axis=0), jnp.concatenate(far, axis=0)]
         quarters.append(jnp.concatenate(columns, axis=1))
-    back = backward(lambda r: table_ref[0, r], lambda r: table_ref[1, r], quarters)
+    back = backward(table_ref, quarters)
     flat_ref[:, FULL:, :] = jnp.zeros((2, WIDE - FULL, LANES), jnp.float32)
     for r in range(4):
         for column in range(2):

time: 104 us -> 104 us (level)
  no operation moved by 1% of the time
where the time goes in v6:
time: 104 us; the launch traced here: 103 us
  blocking collectives  46.7 us (45%)
  starting transfers between devices  25.3 us (24%)
  waiting for transfers between devices  23.7 us (23%)
  Pallas kernels  6.66 us (6%)
    all_to_all x1, blocking collectives, exchange(): lax.all_to_all(blocks, 'slab', 0, 0, tiled=True)  37.1 us
    all_to_all x1, starting transfers between devices, exchange(): lax.all_to_all(blocks, 'slab', 0, 0, tiled=True)  19.8 us
    ppermute x2, waiting for transfers between devices, shifted(): return lax.ppermute(value, axis, pairs)  14.5 us
    all_to_all x1, blocking collectives, local(): lax.all_to_all(energy, 'con', 0, 0, tiled=True)  9.61 us
    all_to_all x1, waiting for transfers between devices, exchange(): lax.all_to_all(blocks, 'slab', 0, 0, tiled=True)  9.19 us
    ppermute x2, starting transfers between devices, shifted(): return lax.ppermute(value, axis, pairs)  5.56 us
    pallas_call x1, Pallas kernels, local(): pl.pallas_call(first_kernel, in_specs=[whole] * 3, out_shape=jax.ShapeDty...  2.93 us
  transfers between devices with their start and end apart: 3, of which 3 were waited for; matrix products, arithmetic and copies ran while one was open for 0% of the time, Pallas kernels for 1%

profile of v6, /device:TPU:1, one launch (start us, length us, event | category | flops | bytes accessed | tf_op | source)
XLA Modules:
  0.0 103.2 jit_solution(4471307683210643383)
XLA Ops:
  0.6 0.0 copy-start.1
  0.6 0.0 copy-start.4
  0.7 0.0 copy-start.5
  0.7 0.0 copy-start.3
  0.7 0.0 copy-start.7
  0.7 0.0 copy-start.6
  0.7 2.9 %first.1 = f32[832,128]{1,0:T(8,128)} custom-call(f32[1,2,5,2,320]{4,3,2,1,0:T(2,128)} %bitcast.18, f32[8,2,5,2,320]{4,3,2,1,0:T(2,128)} %bitcast.14, bf16[4,160,480]{2,1,0:T(8,128)(2,1)} %constant.15.clone.table_hbm), custom_call_target="tpu_custom_call" | custom-call | tf_op jit(solution)/shard_map/first/pallas_call | solution.py:405
  3.6 0.0 copy-start
  3.6 19.8 %all-to-all-start = ((f32[64,1,1664]{2,1,0:T(1,128)}), f32[64,1,1664]{2,1,0:T(1,128)S(1)}, u32[]{:S(2)}, u32[]{:S(2)}) async-start(f32[64,1,1664]{2,1,0:T(1,128)} %bitcast.2), calls=%async_computation | async-start | bytes 851968 | tf_op jit(solution)/shard_map/all_to_all | solution.py:383
  23.4 0.0 copy-done.1
  23.4 0.0 copy-done.4
  23.4 0.0 copy-done.5
  23.4 0.0 copy-done.3
  23.4 0.1 edge.1
  23.5 2.4 %collective-permute-start = (f32[26,1,2,320]{3,2,1,0:T(2,128)S(1)}, f32[26,1,2,320]{3,2,1,0:T(2,128)S(1)}, u32[]{:S(2)}, u32[]{:S(2)}) collective-permute-start(f32[26,1,2,320]{3,2,1,0:T(2,128)S(1)} %get-tuple-element.14), channel_id=1, source_target_pairs={{1,0},{2,1},{3,2},{4,3},{5,4},{6,5},{7,6},{8,7},{9,8},{10,9},{11,1... | collective-permute-start | bytes 199688 | tf_op jit(solution)/shard_map/ppermute | solution.py:389
  25.9 3.2 %collective-permute-start.1 = (f32[2,1,2,320]{3,2,1,0:T(2,128)S(1)}, f32[2,1,2,320]{3,2,1,0:T(2,128)S(1)}, u32[]{:S(2)}, u32[]{:S(2)}) collective-permute-start(f32[2,1,2,320]{3,2,1,0:T(2,128)S(1)} %get-tuple-element.15), channel_id=1, source_target_pairs={{0,1},{1,2},{2,3},{3,4},{4,5},{5,6},{6,7},{7,8},{8,9},{9,10},{10,1... | collective-permute-start | bytes 15368 | tf_op jit(solution)/shard_map/ppermute | solution.py:389
  29.1 0.0 copy-done.7
  29.1 0.0 copy-done.6
  29.2 0.5 weights.1.weight_ref
  29.6 5.7 %collective-permute-done.1.rim_ref = f32[2,1,2,320]{3,2,1,0:T(2,128)S(1)} collective-permute-done((f32[2,1,2,320]{3,2,1,0:T(2,128)S(1)}, f32[2,1,2,320]{3,2,1,0:T(2,128)S(1)}, u32[]{:S(2)}, u32[]{:S(2)}) %collective-permute-start.1) | collective-permute-done | bytes 5152 | tf_op jit(solution)/shard_map/ppermute | solution.py:389
  35.3 8.8 %collective-permute-done.edge_ref = f32[26,1,2,320]{3,2,1,0:T(2,128)S(1)} collective-permute-done((f32[26,1,2,320]{3,2,1,0:T(2,128)S(1)}, f32[26,1,2,320]{3,2,1,0:T(2,128)S(1)}, u32[]{:S(2)}, u32[]{:S(2)}) %collective-permute-start) | collective-permute-done | bytes 66592 | tf_op jit(solution)/shard_map/ppermute | solution.py:389
  44.1 9.2 %all-to-all-done = f32[64,1,1664]{2,1,0:T(1,128)S(1)} async-done(((f32[64,1,1664]{2,1,0:T(1,128)}), f32[64,1,1664]{2,1,0:T(1,128)S(1)}, u32[]{:S(2)}, u32[]{:S(2)}) %all-to-all-start) | async-done | bytes 426016 | tf_op jit(solution)/shard_map/all_to_all | solution.py:383
  53.3 0.0 copy-done
  53.3 0.0 copy-start.2
  53.3 1.4 %second.1 = f32[960,128]{1,0:T(8,128)S(1)} custom-call(f32[832,128]{1,0:T(8,128)S(1)} %bitcast.13, f32[640,384]{1,0:T(8,128)S(1)} %weights.1.weight_ref, bf16[2,4,160,480]{3,2,1,0:T(8,128)(2,1)S(1)} %copy-done), custom_call_target="tpu_custom_call" | custom-call | tf_op jit(solution)/shard_map/second/pallas_call | solution.py:436
  54.7 37.1 %all_to_all.15 = f32[64,1,1920]{2,1,0:T(1,128)S(1)} all-to-all(f32[64,1,1920]{2,1,0:T(1,128)S(1)} %bitcast.11), channel_id=1, replica_groups=mesh['con'=8,'slab'=64] {'slab'}, dimensions={0} | all-to-all | bytes 983040 | tf_op jit(solution)/shard_map/all_to_all | solution.py:383
  91.8 0.0 copy-done.2
  91.8 1.1 %third.1 = (f32[8,16,384]{2,1,0:T(8,128)S(1)}, f32[8,30,128]{2,1,0:T(8,128)S(1)}) custom-call(s32[1]{0:T(128)} %bitcast.6.last_ref, f32[960,128]{1,0:T(8,128)S(1)} %bitcast.12, f32[160,320]{1,0:T(8,128)S(1)} %get-tuple-element.19.rows_ref, bf16[4,160,480]{2,1,0:T(8,128)(2,1)S(1)} %copy-done.2, f32[1,2,5,2,320]{4,3,2,1,0:T(2,128)S(1)} %bitcast.20, ...), custom_call_target="tpu_custom_call" | custom-call | tf_op jit(solution)/shard_map/third/pallas_call | solution.py:442
  92.9 9.6 %all_to_all.16.energy_ref = f32[8,30,128]{2,1,0:T(8,128)S(1)} all-to-all(f32[8,30,128]{2,1,0:T(8,128)S(1)} %get-tuple-element.22), channel_id=1, replica_groups=mesh['con'=8,'slab'=64] {'con'}, dimensions={0} | all-to-all | bytes 245760 | tf_op jit(solution)/shard_map/all_to_all | solution.py:466
  102.5 0.7 last.1
  (1 shorter events, 0.0 us)
Async XLA Ops:
  0.6 22.8 %copy-start.1 = (f32[8,2,2,5,320]{4,2,3,1,0:T(2,128)S(1)}, f32[8,2,2,5,320]{4,2,3,1,0:T(2,128)}, u32[]{:S(2)}) copy-start(f32[8,2,2,5,320]{4,2,3,1,0:T(2,128)} %param.12) | copy-start | bytes 614404
  0.6 22.8 %copy-start.4 = (f32[1,2,2,5,320]{4,2,3,1,0:T(2,128)S(1)}, f32[1,2,2,5,320]{4,2,3,1,0:T(2,128)}, u32[]{:S(2)}) copy-start(f32[1,2,2,5,320]{4,2,3,1,0:T(2,128)} %param.9) | copy-start | bytes 76804
  0.7 22.8 %copy-start.5 = (f32[1,2,2,5,320]{4,2,3,1,0:T(2,128)S(1)}, f32[1,2,2,5,320]{4,2,3,1,0:T(2,128)}, u32[]{:S(2)}) copy-start(f32[1,2,2,5,320]{4,2,3,1,0:T(2,128)} %param.11) | copy-start | bytes 76804
  0.7 22.8 %copy-start.3 = (f32[1,6,2,5,320]{4,2,3,1,0:T(2,128)S(1)}, f32[1,6,2,5,320]{4,2,3,1,0:T(2,128)}, u32[]{:S(2)}) copy-start(f32[1,6,2,5,320]{4,2,3,1,0:T(2,128)} %param.10) | copy-start | bytes 230404
  0.7 28.5 %copy-start.7 = (f32[1,10,640]{2,0,1:T(1,128)S(1)}, f32[1,10,640]{2,0,1:T(1,128)}, u32[]{:S(2)}) copy-start(f32[1,10,640]{2,0,1:T(1,128)} %param.13) | copy-start | bytes 76804
  0.7 28.5 %copy-start.6 = (bf16[10,384]{1,0:T(8,128)(2,1)S(1)}, bf16[10,384]{1,0:T(8,128)(2,1)}, u32[]{:S(2)}) copy-start(bf16[10,384]{1,0:T(8,128)(2,1)} %constant.14.clone.spread_ref) | copy-start | bytes 23044
  3.6 49.7 %copy-start = (bf16[2,4,160,480]{3,2,1,0:T(8,128)(2,1)S(1)}, bf16[2,4,160,480]{3,2,1,0:T(8,128)(2,1)}, u32[]{:S(2)}) copy-start(bf16[2,4,160,480]{3,2,1,0:T(8,128)(2,1)} %constant.16.clone.table_ref) | copy-start | bytes 3686404
  3.6 49.6 %all-to-all-start = ((f32[64,1,1664]{2,1,0:T(1,128)}), f32[64,1,1664]{2,1,0:T(1,128)S(1)}, u32[]{:S(2)}, u32[]{:S(2)}) async-start(f32[64,1,1664]{2,1,0:T(1,128)} %bitcast.2), calls=%async_computation | async-start | bytes 851968 | tf_op jit(solution)/shard_map/all_to_all | solution.py:383
  23.5 20.6 %collective-permute-start = (f32[26,1,2,320]{3,2,1,0:T(2,128)S(1)}, f32[26,1,2,320]{3,2,1,0:T(2,128)S(1)}, u32[]{:S(2)}, u32[]{:S(2)}) collective-permute-start(f32[26,1,2,320]{3,2,1,0:T(2,128)S(1)} %get-tuple-element.14), channel_id=1, source_target_pairs={{1,0},{2,1},{3,2},{4,3},{5,4},{6,5},{7,6},{8,7},{9,8},{10,9},{11,1... | collective-permute-start | bytes 199688 | tf_op jit(solution)/shard_map/ppermute | solution.py:389
  25.9 9.4 %collective-permute-start.1 = (f32[2,1,2,320]{3,2,1,0:T(2,128)S(1)}, f32[2,1,2,320]{3,2,1,0:T(2,128)S(1)}, u32[]{:S(2)}, u32[]{:S(2)}) collective-permute-start(f32[2,1,2,320]{3,2,1,0:T(2,128)S(1)} %get-tuple-element.15), channel_id=1, source_target_pairs={{0,1},{1,2},{2,3},{3,4},{4,5},{5,6},{6,7},{7,8},{8,9},{9,10},{10,1... | collective-permute-start | bytes 15368 | tf_op jit(solution)/shard_map/ppermute | solution.py:389
  53.3 38.5 %copy-start.2 = (bf16[4,160,480]{2,1,0:T(8,128)(2,1)S(1)}, bf16[4,160,480]{2,1,0:T(8,128)(2,1)}, u32[]{:S(2)}) copy-start(bf16[4,160,480]{2,1,0:T(8,128)(2,1)} %constant.17.clone.table_ref) | copy-start | bytes 1843204

commit v7 on v6

--- a/solution.py
+++ b/solution.py
@@ -23,6 +23,7 @@
 BACK_TILES = 15
 LANES = 128
 WIDE = 384
+PACKED = 25
 
 
 def tile_of(x, b, rows):
@@ -354,17 +355,20 @@
     energy = sum(value * value for value in moved)
     for channel in range(6):
         moved_ref[channel] = moved[channel]
-    for copy in range(energy_ref.shape[0]):
-        for t in range(3):
-            energy_ref[copy, 10 * t : 10 * t + 10, :] = energy[:10, t * LANES : (t + 1) * LANES]
+    rest = energy[:, 2 * LANES :]
+    rest = jnp.where(lane[:5, :LANES] < 64, rest[:5], turn(rest, 64)[5:10])
+    packed = jnp.concatenate([energy[:10, :LANES], energy[:10, LANES : 2 * LANES], rest], axis=0)
+    for at in range(0, energy_ref.shape[0], PACKED):
+        energy_ref[at : at + PACKED, :] = packed
 
 
 def last_kernel(limit, energy_ref, moved_ref, new_ref, out_ref):
-    energy = energy_ref[0]
-    for at in range(1, energy_ref.shape[0]):
-        energy = energy + energy_ref[at]
+    energy = energy_ref[:PACKED, :]
+    for at in range(PACKED, energy_ref.shape[0], PACKED):
+        energy = energy + energy_ref[at : at + PACKED, :]
     scale = 1.0 / jnp.maximum(1.0, jnp.sqrt(energy) / limit)
-    scale = jnp.concatenate([scale[10 * t : 10 * t + 10] for t in range(3)], axis=1)
+    rest = jnp.concatenate([scale[20:], turn(scale[20:], 64)], axis=0)
+    scale = jnp.concatenate([scale[:10], scale[10:20], rest], axis=1)
     for channel in range(6):
         value = moved_ref[channel][:10] * scale
         for x in range(ROWS):
@@ -377,10 +381,9 @@
 PARAMS = pltpu.CompilerParams(vmem_limit_bytes=32 * 2**20)
 
 
-def exchange(value):
-    tiles = value.shape[0] // SLABS
-    blocks = value.reshape(SLABS, 1, tiles * LANES)
-    return lax.all_to_all(blocks, "slab", 0, 0, tiled=True).reshape(SLABS * tiles, LANES)
+def exchange(value, axis, count):
+    blocks = value.reshape(count, 1, -1)
+    return lax.all_to_all(blocks, axis, 0, 0, tiled=True).reshape(value.shape)
 
 
 def shifted(value, axis, by):
@@ -431,7 +434,7 @@
     rim = shifted(rim, "slab", 1)
     is_last = (lax.axis_index("slab") == SLABS - 1).astype(jnp.int32).reshape(1)
     bands, edge, rim, is_last, sens_rows = lax.optimization_barrier(
-        (exchange(bands), edge, rim, is_last, sens_rows)
+        (exchange(bands, "slab", SLABS), edge, rim, is_last, sens_rows)
     )
     returned = pl.pallas_call(
         second_kernel,
@@ -445,7 +448,7 @@
         + [pl.BlockSpec(memory_space=pltpu.VMEM)] * 8,
         out_shape=(
             jax.ShapeDtypeStruct((8, 16, WIDE), jnp.float32),
-            jax.ShapeDtypeStruct((contrasts, 30, LANES), jnp.float32),
+            jax.ShapeDtypeStruct((contrasts * PACKED, LANES), jnp.float32),
         ),
         scratch_shapes=[
             pltpu.VMEM((2, WIDE, LANES), jnp.float32),
@@ -454,7 +457,7 @@
         ],
         compiler_params=PARAMS,
         name="third",
-    )(is_last, exchange(returned), sens_rows, third, image, adjoint_data, dual, edge, rim)
+    )(is_last, exchange(returned, "slab", SLABS), sens_rows, third, image, adjoint_data, dual, edge, rim)
     new_image, new_dual = pl.pallas_call(
         functools.partial(last_kernel, 0.9 * math.sqrt(6.0 * contrasts)),
         out_shape=(
@@ -463,7 +466,7 @@
         ),
         compiler_params=PARAMS,
         name="last",
-    )(lax.all_to_all(energy, "con", 0, 0, tiled=True), moved)
+    )(exchange(energy, "con", contrasts), moved)
     return jnp.swapaxes(new_image, 2, 3), jnp.swapaxes(new_dual, 2, 3)
 
 

time: 104 us -> 103 us (level)
  no operation moved by 1% of the time
where the time goes in v7:
time: 103 us
  blocking collectives  46.4 us (45%)
  starting transfers between devices  25.3 us (25%)
  waiting for transfers between devices  23.7 us (23%)
  Pallas kernels  6.74 us (7%)
    all_to_all x2, blocking collectives, exchange(): return lax.all_to_all(blocks, axis, 0, 0, tiled=True).reshape(value.shape)  46.4 us
    all_to_all x1, starting transfers between devices, exchange(): return lax.all_to_all(blocks, axis, 0, 0, tiled=True).reshape(value.shape)  19.8 us
    ppermute x2, waiting for transfers between devices, shifted(): return lax.ppermute(value, axis, pairs)  14.5 us
    all_to_all x1, waiting for transfers between devices, exchange(): return lax.all_to_all(blocks, axis, 0, 0, tiled=True).reshape(value.shape)  9.19 us
    ppermute x2, starting transfers between devices, shifted(): return lax.ppermute(value, axis, pairs)  5.56 us
    pallas_call x1, Pallas kernels, local(): pl.pallas_call(first_kernel, in_specs=[whole] * 3, out_shape=jax.ShapeDty...  2.93 us
  transfers between devices with their start and end apart: 3, of which 3 were waited for; matrix products, arithmetic and copies ran while one was open for 0% of the time, Pallas kernels for 1%

profile of v7, /device:TPU:1, one launch (start us, length us, event | category | flops | bytes accessed | tf_op | source)
XLA Modules:
  0.0 103.0 jit_solution(297534422883759815)
XLA Ops:
  0.6 0.0 copy-start.1
  0.6 0.0 copy-start.4
  0.7 0.0 copy-start.5
  0.7 0.0 copy-start.3
  0.7 0.0 copy-start.7
  0.7 0.0 copy-start.6
  0.7 2.9 %first.1 = f32[832,128]{1,0:T(8,128)} custom-call(f32[1,2,5,2,320]{4,3,2,1,0:T(2,128)} %bitcast.21, f32[8,2,5,2,320]{4,3,2,1,0:T(2,128)} %bitcast.16, bf16[4,160,480]{2,1,0:T(8,128)(2,1)} %constant.15.clone.table_hbm), custom_call_target="tpu_custom_call" | custom-call | tf_op jit(solution)/shard_map/first/pallas_call | solution.py:408
  3.6 0.0 copy-start
  3.6 19.8 %all-to-all-start = ((f32[64,1,1664]{2,1,0:T(1,128)}), f32[64,1,1664]{2,1,0:T(1,128)S(1)}, u32[]{:S(2)}, u32[]{:S(2)}) async-start(f32[64,1,1664]{2,1,0:T(1,128)} %bitcast.2), calls=%async_computation | async-start | bytes 851968 | tf_op jit(solution)/shard_map/all_to_all | solution.py:386
  23.4 0.0 copy-done.1
  23.4 0.0 copy-done.4
  23.4 0.0 copy-done.5
  23.4 0.0 copy-done.3
  23.4 0.1 edge.1
  23.5 2.4 %collective-permute-start = (f32[26,1,2,320]{3,2,1,0:T(2,128)S(1)}, f32[26,1,2,320]{3,2,1,0:T(2,128)S(1)}, u32[]{:S(2)}, u32[]{:S(2)}) collective-permute-start(f32[26,1,2,320]{3,2,1,0:T(2,128)S(1)} %get-tuple-element.14), channel_id=1, source_target_pairs={{1,0},{2,1},{3,2},{4,3},{5,4},{6,5},{7,6},{8,7},{9,8},{10,9},{11,1... | collective-permute-start | bytes 199688 | tf_op jit(solution)/shard_map/ppermute | solution.py:392
  25.9 3.2 %collective-permute-start.1 = (f32[2,1,2,320]{3,2,1,0:T(2,128)S(1)}, f32[2,1,2,320]{3,2,1,0:T(2,128)S(1)}, u32[]{:S(2)}, u32[]{:S(2)}) collective-permute-start(f32[2,1,2,320]{3,2,1,0:T(2,128)S(1)} %get-tuple-element.15), channel_id=1, source_target_pairs={{0,1},{1,2},{2,3},{3,4},{4,5},{5,6},{6,7},{7,8},{8,9},{9,10},{10,1... | collective-permute-start | bytes 15368 | tf_op jit(solution)/shard_map/ppermute | solution.py:392
  29.1 0.0 copy-done.7
  29.1 0.0 copy-done.6
  29.2 0.5 weights.1.weight_ref
  29.6 5.7 %collective-permute-done.1.rim_ref = f32[2,1,2,320]{3,2,1,0:T(2,128)S(1)} collective-permute-done((f32[2,1,2,320]{3,2,1,0:T(2,128)S(1)}, f32[2,1,2,320]{3,2,1,0:T(2,128)S(1)}, u32[]{:S(2)}, u32[]{:S(2)}) %collective-permute-start.1) | collective-permute-done | bytes 5152 | tf_op jit(solution)/shard_map/ppermute | solution.py:392
  35.3 8.8 %collective-permute-done.edge_ref = f32[26,1,2,320]{3,2,1,0:T(2,128)S(1)} collective-permute-done((f32[26,1,2,320]{3,2,1,0:T(2,128)S(1)}, f32[26,1,2,320]{3,2,1,0:T(2,128)S(1)}, u32[]{:S(2)}, u32[]{:S(2)}) %collective-permute-start) | collective-permute-done | bytes 66592 | tf_op jit(solution)/shard_map/ppermute | solution.py:392
  44.1 9.2 %all-to-all-done = f32[64,1,1664]{2,1,0:T(1,128)S(1)} async-done(((f32[64,1,1664]{2,1,0:T(1,128)}), f32[64,1,1664]{2,1,0:T(1,128)S(1)}, u32[]{:S(2)}, u32[]{:S(2)}) %all-to-all-start) | async-done | bytes 426016 | tf_op jit(solution)/shard_map/all_to_all | solution.py:386
  53.3 0.0 copy-done
  53.3 0.0 copy-start.2
  53.3 1.4 %second.1 = f32[960,128]{1,0:T(8,128)S(1)} custom-call(f32[832,128]{1,0:T(8,128)S(1)} %bitcast.15, f32[640,384]{1,0:T(8,128)S(1)} %weights.1.weight_ref, bf16[2,4,160,480]{3,2,1,0:T(8,128)(2,1)S(1)} %copy-done), custom_call_target="tpu_custom_call" | custom-call | tf_op jit(solution)/shard_map/second/pallas_call | solution.py:439
  54.7 37.1 %all_to_all.15 = f32[64,1,1920]{2,1,0:T(1,128)S(1)} all-to-all(f32[64,1,1920]{2,1,0:T(1,128)S(1)} %bitcast.13), channel_id=1, replica_groups=mesh['con'=8,'slab'=64] {'slab'}, dimensions={0} | all-to-all | bytes 983040 | tf_op jit(solution)/shard_map/all_to_all | solution.py:386
  91.8 0.0 copy-done.2
  91.8 1.1 %third.1 = (f32[8,16,384]{2,1,0:T(8,128)S(1)}, f32[200,128]{1,0:T(8,128)S(1)}) custom-call(s32[1]{0:T(128)} %bitcast.6.last_ref, f32[960,128]{1,0:T(8,128)S(1)} %bitcast.14, f32[160,320]{1,0:T(8,128)S(1)} %get-tuple-element.19.rows_ref, bf16[4,160,480]{2,1,0:T(8,128)(2,1)S(1)} %copy-done.2, f32[1,2,5,2,320]{4,3,2,1,0:T(2,128)S(1)} %bitcast.23, ...), custom_call_target="tpu_custom_call" | custom-call | tf_op jit(solution)/shard_map/third/pallas_call | solution.py:445
  92.9 9.3 %all_to_all.16 = f32[8,1,3200]{2,1,0:T(1,128)S(1)} all-to-all(f32[8,1,3200]{2,1,0:T(1,128)S(1)} %bitcast.26), channel_id=1, replica_groups=mesh['con'=8,'slab'=64] {'con'}, dimensions={0} | all-to-all | bytes 204800 | tf_op jit(solution)/shard_map/all_to_all | solution.py:386
  102.2 0.7 last.1
  (1 shorter events, 0.0 us)
Async XLA Ops:
  0.6 22.8 %copy-start.1 = (f32[8,2,2,5,320]{4,2,3,1,0:T(2,128)S(1)}, f32[8,2,2,5,320]{4,2,3,1,0:T(2,128)}, u32[]{:S(2)}) copy-start(f32[8,2,2,5,320]{4,2,3,1,0:T(2,128)} %param.12) | copy-start | bytes 614404
  0.6 22.8 %copy-start.4 = (f32[1,2,2,5,320]{4,2,3,1,0:T(2,128)S(1)}, f32[1,2,2,5,320]{4,2,3,1,0:T(2,128)}, u32[]{:S(2)}) copy-start(f32[1,2,2,5,320]{4,2,3,1,0:T(2,128)} %param.9) | copy-start | bytes 76804
  0.7 22.8 %copy-start.5 = (f32[1,2,2,5,320]{4,2,3,1,0:T(2,128)S(1)}, f32[1,2,2,5,320]{4,2,3,1,0:T(2,128)}, u32[]{:S(2)}) copy-start(f32[1,2,2,5,320]{4,2,3,1,0:T(2,128)} %param.11) | copy-start | bytes 76804
  0.7 22.8 %copy-start.3 = (f32[1,6,2,5,320]{4,2,3,1,0:T(2,128)S(1)}, f32[1,6,2,5,320]{4,2,3,1,0:T(2,128)}, u32[]{:S(2)}) copy-start(f32[1,6,2,5,320]{4,2,3,1,0:T(2,128)} %param.10) | copy-start | bytes 230404
  0.7 28.5 %copy-start.7 = (f32[1,10,640]{2,0,1:T(1,128)S(1)}, f32[1,10,640]{2,0,1:T(1,128)}, u32[]{:S(2)}) copy-start(f32[1,10,640]{2,0,1:T(1,128)} %param.13) | copy-start | bytes 76804
  0.7 28.5 %copy-start.6 = (bf16[10,384]{1,0:T(8,128)(2,1)S(1)}, bf16[10,384]{1,0:T(8,128)(2,1)}, u32[]{:S(2)}) copy-start(bf16[10,384]{1,0:T(8,128)(2,1)} %constant.14.clone.spread_ref) | copy-start | bytes 23044
  3.6 49.7 %copy-start = (bf16[2,4,160,480]{3,2,1,0:T(8,128)(2,1)S(1)}, bf16[2,4,160,480]{3,2,1,0:T(8,128)(2,1)}, u32[]{:S(2)}) copy-start(bf16[2,4,160,480]{3,2,1,0:T(8,128)(2,1)} %constant.16.clone.table_ref) | copy-start | bytes 3686404
  3.6 49.6 %all-to-all-start = ((f32[64,1,1664]{2,1,0:T(1,128)}), f32[64,1,1664]{2,1,0:T(1,128)S(1)}, u32[]{:S(2)}, u32[]{:S(2)}) async-start(f32[64,1,1664]{2,1,0:T(1,128)} %bitcast.2), calls=%async_computation | async-start | bytes 851968 | tf_op jit(solution)/shard_map/all_to_all | solution.py:386
  23.5 20.6 %collective-permute-start = (f32[26,1,2,320]{3,2,1,0:T(2,128)S(1)}, f32[26,1,2,320]{3,2,1,0:T(2,128)S(1)}, u32[]{:S(2)}, u32[]{:S(2)}) collective-permute-start(f32[26,1,2,320]{3,2,1,0:T(2,128)S(1)} %get-tuple-element.14), channel_id=1, source_target_pairs={{1,0},{2,1},{3,2},{4,3},{5,4},{6,5},{7,6},{8,7},{9,8},{10,9},{11,1... | collective-permute-start | bytes 199688 | tf_op jit(solution)/shard_map/ppermute | solution.py:392
  25.9 9.4 %collective-permute-start.1 = (f32[2,1,2,320]{3,2,1,0:T(2,128)S(1)}, f32[2,1,2,320]{3,2,1,0:T(2,128)S(1)}, u32[]{:S(2)}, u32[]{:S(2)}) collective-permute-start(f32[2,1,2,320]{3,2,1,0:T(2,128)S(1)} %get-tuple-element.15), channel_id=1, source_target_pairs={{0,1},{1,2},{2,3},{3,4},{4,5},{5,6},{6,7},{7,8},{8,9},{9,10},{10,1... | collective-permute-start | bytes 15368 | tf_op jit(solution)/shard_map/ppermute | solution.py:392
  53.3 38.5 %copy-start.2 = (bf16[4,160,480]{2,1,0:T(8,128)(2,1)S(1)}, bf16[4,160,480]{2,1,0:T(8,128)(2,1)}, u32[]{:S(2)}) copy-start(bf16[4,160,480]{2,1,0:T(8,128)(2,1)} %constant.17.clone.table_ref) | copy-start | bytes 1843204

commit v8 on v6

--- a/solution.py
+++ b/solution.py
@@ -426,7 +426,7 @@
         ),
         compiler_params=PARAMS,
         name="edge",
-    )(image, adjoint_data, dual, sens)
+    )(*(pltpu.with_memory_space_constraint(v, pltpu.HBM) for v in (image, adjoint_data, dual, sens)))
     edge = shifted(edge, "slab", -1)
     rim = shifted(rim, "slab", 1)
     is_last = (lax.axis_index("slab") == SLABS - 1).astype(jnp.int32).reshape(1)

time: 104 us -> 103 us (level)
  transfers between devices with their start and end apart: 3 -> 3, of which waited for: 3 -> 3; matrix products, arithmetic and copies ran while one was open for 0% -> 0% of each run, Pallas kernels for 1% -> 2%
where the time goes in v8:
time: 103 us
  blocking collectives  46.7 us (45%)
  starting transfers between devices  25.3 us (25%)
  waiting for transfers between devices  22.7 us (22%)
  Pallas kernels  7.6 us (7%)
    all_to_all x1, blocking collectives, exchange(): lax.all_to_all(blocks, 'slab', 0, 0, tiled=True)  37.1 us
    all_to_all x1, starting transfers between devices, exchange(): lax.all_to_all(blocks, 'slab', 0, 0, tiled=True)  19.8 us
    ppermute x2, waiting for transfers between devices, shifted(): return lax.ppermute(value, axis, pairs)  13.5 us
    all_to_all x1, blocking collectives, local(): lax.all_to_all(energy, 'con', 0, 0, tiled=True)  9.61 us
    all_to_all x1, waiting for transfers between devices, exchange(): lax.all_to_all(blocks, 'slab', 0, 0, tiled=True)  9.19 us
    ppermute x2, starting transfers between devices, shifted(): return lax.ppermute(value, axis, pairs)  5.56 us
    pallas_call x1, Pallas kernels, local(): pl.pallas_call(first_kernel, in_specs=[whole] * 3, out_shape=jax.ShapeDty...  2.84 us
  transfers between devices with their start and end apart: 3, of which 3 were waited for; matrix products, arithmetic and copies ran while one was open for 0% of the time, Pallas kernels for 2%

profile of v8, /device:TPU:1, one launch (start us, length us, event | category | flops | bytes accessed | tf_op | source)
XLA Modules:
  0.0 103.1 jit_solution(889328067159857878)
XLA Ops:
  0.6 0.0 copy-start.6
  0.6 0.0 copy-start.5
  0.7 2.8 %first.1 = f32[832,128]{1,0:T(8,128)} custom-call(f32[1,2,5,2,320]{4,3,2,1,0:T(2,128)} %bitcast.16, f32[8,2,5,2,320]{4,3,2,1,0:T(2,128)} %bitcast.21, bf16[4,160,480]{2,1,0:T(8,128)(2,1)} %constant.15.clone.table_hbm), custom_call_target="tpu_custom_call" | custom-call | tf_op jit(solution)/shard_map/first/pallas_call | solution.py:405
  3.5 0.0 copy-start
  3.5 19.8 %all-to-all-start = ((f32[64,1,1664]{2,1,0:T(1,128)}), f32[64,1,1664]{2,1,0:T(1,128)S(1)}, u32[]{:S(2)}, u32[]{:S(2)}) async-start(f32[64,1,1664]{2,1,0:T(1,128)} %bitcast.2), calls=%async_computation | async-start | bytes 851968 | tf_op jit(solution)/shard_map/all_to_all | solution.py:383
  23.3 1.1 %edge.1 = (f32[26,1,2,320]{3,2,1,0:T(2,128)S(1)}, f32[2,1,2,320]{3,2,1,0:T(2,128)S(1)}, f32[160,320]{1,0:T(8,128)S(1)}) custom-call(f32[1,2,5,2,320]{4,3,2,1,0:T(2,128)} %bitcast.17, f32[1,2,5,2,320]{4,3,2,1,0:T(2,128)} %bitcast.19, f32[1,6,5,2,320]{4,3,2,1,0:T(2,128)} %bitcast.14, f32[8,2,5,2,320]{4,3,2,1,0:T(2,128)} %bitcast.22), custom_call_target="tpu_custom_call" | custom-call | tf_op jit(solution)/shard_map/edge/pallas_call | solution.py:420
  24.4 2.4 %collective-permute-start = (f32[26,1,2,320]{3,2,1,0:T(2,128)S(1)}, f32[26,1,2,320]{3,2,1,0:T(2,128)S(1)}, u32[]{:S(2)}, u32[]{:S(2)}) collective-permute-start(f32[26,1,2,320]{3,2,1,0:T(2,128)S(1)} %get-tuple-element.14), channel_id=1, source_target_pairs={{1,0},{2,1},{3,2},{4,3},{5,4},{6,5},{7,6},{8,7},{9,8},{10,9},{11,1... | collective-permute-start | bytes 199688 | tf_op jit(solution)/shard_map/ppermute | solution.py:389
  26.8 3.2 %collective-permute-start.1 = (f32[2,1,2,320]{3,2,1,0:T(2,128)S(1)}, f32[2,1,2,320]{3,2,1,0:T(2,128)S(1)}, u32[]{:S(2)}, u32[]{:S(2)}) collective-permute-start(f32[2,1,2,320]{3,2,1,0:T(2,128)S(1)} %get-tuple-element.15), channel_id=1, source_target_pairs={{0,1},{1,2},{2,3},{3,4},{4,5},{5,6},{6,7},{7,8},{8,9},{9,10},{10,1... | collective-permute-start | bytes 15368 | tf_op jit(solution)/shard_map/ppermute | solution.py:389
  30.0 0.0 copy-done.6
  30.0 0.0 copy-done.5
  30.0 0.5 weights.1.weight_ref
  30.5 4.7 %collective-permute-done.1.rim_ref = f32[2,1,2,320]{3,2,1,0:T(2,128)S(1)} collective-permute-done((f32[2,1,2,320]{3,2,1,0:T(2,128)S(1)}, f32[2,1,2,320]{3,2,1,0:T(2,128)S(1)}, u32[]{:S(2)}, u32[]{:S(2)}) %collective-permute-start.1) | collective-permute-done | bytes 5152 | tf_op jit(solution)/shard_map/ppermute | solution.py:389
  35.2 8.8 %collective-permute-done.edge_ref = f32[26,1,2,320]{3,2,1,0:T(2,128)S(1)} collective-permute-done((f32[26,1,2,320]{3,2,1,0:T(2,128)S(1)}, f32[26,1,2,320]{3,2,1,0:T(2,128)S(1)}, u32[]{:S(2)}, u32[]{:S(2)}) %collective-permute-start) | collective-permute-done | bytes 66592 | tf_op jit(solution)/shard_map/ppermute | solution.py:389
  44.0 9.2 %all-to-all-done = f32[64,1,1664]{2,1,0:T(1,128)S(1)} async-done(((f32[64,1,1664]{2,1,0:T(1,128)}), f32[64,1,1664]{2,1,0:T(1,128)S(1)}, u32[]{:S(2)}, u32[]{:S(2)}) %all-to-all-start) | async-done | bytes 426016 | tf_op jit(solution)/shard_map/all_to_all | solution.py:383
  53.2 0.0 copy-done
  53.2 0.0 copy-start.1
  53.2 0.0 copy-start.2
  53.2 0.0 copy-start.3
  53.2 0.0 copy-start.4
  53.2 1.4 %second.1 = f32[960,128]{1,0:T(8,128)S(1)} custom-call(f32[832,128]{1,0:T(8,128)S(1)} %bitcast.13, f32[640,384]{1,0:T(8,128)S(1)} %weights.1.weight_ref, bf16[2,4,160,480]{3,2,1,0:T(8,128)(2,1)S(1)} %copy-done), custom_call_target="tpu_custom_call" | custom-call | tf_op jit(solution)/shard_map/second/pallas_call | solution.py:436
  54.6 37.1 %all_to_all.15 = f32[64,1,1920]{2,1,0:T(1,128)S(1)} all-to-all(f32[64,1,1920]{2,1,0:T(1,128)S(1)} %bitcast.11), channel_id=1, replica_groups=mesh['con'=8,'slab'=64] {'slab'}, dimensions={0} | all-to-all | bytes 983040 | tf_op jit(solution)/shard_map/all_to_all | solution.py:383
  91.7 0.0 copy-done.1
  91.7 0.0 copy-done.2
  91.7 0.0 copy-done.3
  91.7 0.0 copy-done.4
  91.7 1.1 %third.1 = (f32[8,16,384]{2,1,0:T(8,128)S(1)}, f32[8,30,128]{2,1,0:T(8,128)S(1)}) custom-call(s32[1]{0:T(128)} %bitcast.6.last_ref, f32[960,128]{1,0:T(8,128)S(1)} %bitcast.12, f32[160,320]{1,0:T(8,128)S(1)} %get-tuple-element.19.rows_ref, bf16[4,160,480]{2,1,0:T(8,128)(2,1)S(1)} %copy-done.1, f32[1,2,5,2,320]{4,3,2,1,0:T(2,128)S(1)} %bitcast.18, ...), custom_call_target="tpu_custom_call" | custom-call | tf_op jit(solution)/shard_map/third/pallas_call | solution.py:442
  92.8 9.6 %all_to_all.16.energy_ref = f32[8,30,128]{2,1,0:T(8,128)S(1)} all-to-all(f32[8,30,128]{2,1,0:T(8,128)S(1)} %get-tuple-element.22), channel_id=1, replica_groups=mesh['con'=8,'slab'=64] {'con'}, dimensions={0} | all-to-all | bytes 245760 | tf_op jit(solution)/shard_map/all_to_all | solution.py:466
  102.4 0.7 last.1
  (1 shorter events, 0.0 us)
Async XLA Ops:
  0.6 29.4 %copy-start.6 = (f32[1,10,640]{2,0,1:T(1,128)S(1)}, f32[1,10,640]{2,0,1:T(1,128)}, u32[]{:S(2)}) copy-start(f32[1,10,640]{2,0,1:T(1,128)} %param.13) | copy-start | bytes 76804
  0.6 29.4 %copy-start.5 = (bf16[10,384]{1,0:T(8,128)(2,1)S(1)}, bf16[10,384]{1,0:T(8,128)(2,1)}, u32[]{:S(2)}) copy-start(bf16[10,384]{1,0:T(8,128)(2,1)} %constant.14.clone.spread_ref) | copy-start | bytes 23044
  3.5 49.7 %copy-start = (bf16[2,4,160,480]{3,2,1,0:T(8,128)(2,1)S(1)}, bf16[2,4,160,480]{3,2,1,0:T(8,128)(2,1)}, u32[]{:S(2)}) copy-start(bf16[2,4,160,480]{3,2,1,0:T(8,128)(2,1)} %constant.16.clone.table_ref) | copy-start | bytes 3686404
  3.5 49.6 %all-to-all-start = ((f32[64,1,1664]{2,1,0:T(1,128)}), f32[64,1,1664]{2,1,0:T(1,128)S(1)}, u32[]{:S(2)}, u32[]{:S(2)}) async-start(f32[64,1,1664]{2,1,0:T(1,128)} %bitcast.2), calls=%async_computation | async-start | bytes 851968 | tf_op jit(solution)/shard_map/all_to_all | solution.py:383
  24.4 19.6 %collective-permute-start = (f32[26,1,2,320]{3,2,1,0:T(2,128)S(1)}, f32[26,1,2,320]{3,2,1,0:T(2,128)S(1)}, u32[]{:S(2)}, u32[]{:S(2)}) collective-permute-start(f32[26,1,2,320]{3,2,1,0:T(2,128)S(1)} %get-tuple-element.14), channel_id=1, source_target_pairs={{1,0},{2,1},{3,2},{4,3},{5,4},{6,5},{7,6},{8,7},{9,8},{10,9},{11,1... | collective-permute-start | bytes 199688 | tf_op jit(solution)/shard_map/ppermute | solution.py:389
  26.8 8.4 %collective-permute-start.1 = (f32[2,1,2,320]{3,2,1,0:T(2,128)S(1)}, f32[2,1,2,320]{3,2,1,0:T(2,128)S(1)}, u32[]{:S(2)}, u32[]{:S(2)}) collective-permute-start(f32[2,1,2,320]{3,2,1,0:T(2,128)S(1)} %get-tuple-element.15), channel_id=1, source_target_pairs={{0,1},{1,2},{2,3},{3,4},{4,5},{5,6},{6,7},{7,8},{8,9},{9,10},{10,1... | collective-permute-start | bytes 15368 | tf_op jit(solution)/shard_map/ppermute | solution.py:389
  53.2 38.6 %copy-start.1 = (bf16[4,160,480]{2,1,0:T(8,128)(2,1)S(1)}, bf16[4,160,480]{2,1,0:T(8,128)(2,1)}, u32[]{:S(2)}) copy-start(bf16[4,160,480]{2,1,0:T(8,128)(2,1)} %constant.17.clone.table_ref) | copy-start | bytes 1843204
  53.2 38.6 %copy-start.2 = (f32[1,6,2,5,320]{4,2,3,1,0:T(2,128)S(1)}, f32[1,6,2,5,320]{4,2,3,1,0:T(2,128)}, u32[]{:S(2)}) copy-start(f32[1,6,2,5,320]{4,2,3,1,0:T(2,128)} %param.10) | copy-start | bytes 230404
  53.2 38.6 %copy-start.3 = (f32[1,2,2,5,320]{4,2,3,1,0:T(2,128)S(1)}, f32[1,2,2,5,320]{4,2,3,1,0:T(2,128)}, u32[]{:S(2)}) copy-start(f32[1,2,2,5,320]{4,2,3,1,0:T(2,128)} %param.9) | copy-start | bytes 76804
  53.2 38.6 %copy-start.4 = (f32[1,2,2,5,320]{4,2,3,1,0:T(2,128)S(1)}, f32[1,2,2,5,320]{4,2,3,1,0:T(2,128)}, u32[]{:S(2)}) copy-start(f32[1,2,2,5,320]{4,2,3,1,0:T(2,128)} %param.11) | copy-start | bytes 76804

commit v9 on v7

--- a/solution.py
+++ b/solution.py
@@ -429,7 +429,7 @@
         ),
         compiler_params=PARAMS,
         name="edge",
-    )(image, adjoint_data, dual, sens)
+    )(*(pltpu.with_memory_space_constraint(v, pltpu.HBM) for v in (image, adjoint_data, dual, sens)))
     edge = shifted(edge, "slab", -1)
     rim = shifted(rim, "slab", 1)
     is_last = (lax.axis_index("slab") == SLABS - 1).astype(jnp.int32).reshape(1)

time: 103 us -> 103 us (level)
  transfers between devices with their start and end apart: 3 -> 3, of which waited for: 3 -> 3; matrix products, arithmetic and copies ran while one was open for 0% -> 0% of each run, Pallas kernels for 1% -> 2%
where the time goes in v9:
time: 103 us
  blocking collectives  46.4 us (45%)
  starting transfers between devices  25.3 us (25%)
  waiting for transfers between devices  22.7 us (22%)
  Pallas kernels  7.69 us (7%)
    all_to_all x2, blocking collectives, exchange(): return lax.all_to_all(blocks, axis, 0, 0, tiled=True).reshape(value.shape)  46.4 us
    all_to_all x1, starting transfers between devices, exchange(): return lax.all_to_all(blocks, axis, 0, 0, tiled=True).reshape(value.shape)  19.8 us
    ppermute x2, waiting for transfers between devices, shifted(): return lax.ppermute(value, axis, pairs)  13.5 us
    all_to_all x1, waiting for transfers between devices, exchange(): return lax.all_to_all(blocks, axis, 0, 0, tiled=True).reshape(value.shape)  9.19 us
    ppermute x2, starting transfers between devices, shifted(): return lax.ppermute(value, axis, pairs)  5.56 us
    pallas_call x1, Pallas kernels, local(): pl.pallas_call(first_kernel, in_specs=[whole] * 3, out_shape=jax.ShapeDty...  2.84 us
  transfers between devices with their start and end apart: 3, of which 3 were waited for; matrix products, arithmetic and copies ran while one was open for 0% of the time, Pallas kernels for 2%

profile of v9, /device:TPU:1, one launch (start us, length us, event | category | flops | bytes accessed | tf_op | source)
XLA Modules:
  0.0 102.9 jit_solution(14801871552364972074)
XLA Ops:
  0.6 0.0 copy-start.6
  0.6 0.0 copy-start.5
  0.7 2.8 %first.1 = f32[832,128]{1,0:T(8,128)} custom-call(f32[1,2,5,2,320]{4,3,2,1,0:T(2,128)} %bitcast.19, f32[8,2,5,2,320]{4,3,2,1,0:T(2,128)} %bitcast.25, bf16[4,160,480]{2,1,0:T(8,128)(2,1)} %constant.15.clone.table_hbm), custom_call_target="tpu_custom_call" | custom-call | tf_op jit(solution)/shard_map/first/pallas_call | solution.py:408
  3.5 0.0 copy-start
  3.5 19.8 %all-to-all-start = ((f32[64,1,1664]{2,1,0:T(1,128)}), f32[64,1,1664]{2,1,0:T(1,128)S(1)}, u32[]{:S(2)}, u32[]{:S(2)}) async-start(f32[64,1,1664]{2,1,0:T(1,128)} %bitcast.2), calls=%async_computation | async-start | bytes 851968 | tf_op jit(solution)/shard_map/all_to_all | solution.py:386
  23.3 1.1 %edge.1 = (f32[26,1,2,320]{3,2,1,0:T(2,128)S(1)}, f32[2,1,2,320]{3,2,1,0:T(2,128)S(1)}, f32[160,320]{1,0:T(8,128)S(1)}) custom-call(f32[1,2,5,2,320]{4,3,2,1,0:T(2,128)} %bitcast.20, f32[1,2,5,2,320]{4,3,2,1,0:T(2,128)} %bitcast.22, f32[1,6,5,2,320]{4,3,2,1,0:T(2,128)} %bitcast.17, f32[8,2,5,2,320]{4,3,2,1,0:T(2,128)} %bitcast.26), custom_call_target="tpu_custom_call" | custom-call | tf_op jit(solution)/shard_map/edge/pallas_call | solution.py:423
  24.4 2.4 %collective-permute-start = (f32[26,1,2,320]{3,2,1,0:T(2,128)S(1)}, f32[26,1,2,320]{3,2,1,0:T(2,128)S(1)}, u32[]{:S(2)}, u32[]{:S(2)}) collective-permute-start(f32[26,1,2,320]{3,2,1,0:T(2,128)S(1)} %get-tuple-element.14), channel_id=1, source_target_pairs={{1,0},{2,1},{3,2},{4,3},{5,4},{6,5},{7,6},{8,7},{9,8},{10,9},{11,1... | collective-permute-start | bytes 199688 | tf_op jit(solution)/shard_map/ppermute | solution.py:392
  26.8 3.2 %collective-permute-start.1 = (f32[2,1,2,320]{3,2,1,0:T(2,128)S(1)}, f32[2,1,2,320]{3,2,1,0:T(2,128)S(1)}, u32[]{:S(2)}, u32[]{:S(2)}) collective-permute-start(f32[2,1,2,320]{3,2,1,0:T(2,128)S(1)} %get-tuple-element.15), channel_id=1, source_target_pairs={{0,1},{1,2},{2,3},{3,4},{4,5},{5,6},{6,7},{7,8},{8,9},{9,10},{10,1... | collective-permute-start | bytes 15368 | tf_op jit(solution)/shard_map/ppermute | solution.py:392
  30.0 0.0 copy-done.6
  30.0 0.0 copy-done.5
  30.0 0.5 weights.1.weight_ref
  30.5 4.7 %collective-permute-done.1.rim_ref = f32[2,1,2,320]{3,2,1,0:T(2,128)S(1)} collective-permute-done((f32[2,1,2,320]{3,2,1,0:T(2,128)S(1)}, f32[2,1,2,320]{3,2,1,0:T(2,128)S(1)}, u32[]{:S(2)}, u32[]{:S(2)}) %collective-permute-start.1) | collective-permute-done | bytes 5152 | tf_op jit(solution)/shard_map/ppermute | solution.py:392
  35.2 8.8 %collective-permute-done.edge_ref = f32[26,1,2,320]{3,2,1,0:T(2,128)S(1)} collective-permute-done((f32[26,1,2,320]{3,2,1,0:T(2,128)S(1)}, f32[26,1,2,320]{3,2,1,0:T(2,128)S(1)}, u32[]{:S(2)}, u32[]{:S(2)}) %collective-permute-start) | collective-permute-done | bytes 66592 | tf_op jit(solution)/shard_map/ppermute | solution.py:392
  44.0 9.2 %all-to-all-done = f32[64,1,1664]{2,1,0:T(1,128)S(1)} async-done(((f32[64,1,1664]{2,1,0:T(1,128)}), f32[64,1,1664]{2,1,0:T(1,128)S(1)}, u32[]{:S(2)}, u32[]{:S(2)}) %all-to-all-start) | async-done | bytes 426016 | tf_op jit(solution)/shard_map/all_to_all | solution.py:386
  53.2 0.0 copy-done
  53.2 0.0 copy-start.1
  53.2 0.0 copy-start.2
  53.2 0.0 copy-start.3
  53.2 0.0 copy-start.4
  53.2 1.4 %second.1 = f32[960,128]{1,0:T(8,128)S(1)} custom-call(f32[832,128]{1,0:T(8,128)S(1)} %bitcast.15, f32[640,384]{1,0:T(8,128)S(1)} %weights.1.weight_ref, bf16[2,4,160,480]{3,2,1,0:T(8,128)(2,1)S(1)} %copy-done), custom_call_target="tpu_custom_call" | custom-call | tf_op jit(solution)/shard_map/second/pallas_call | solution.py:439
  54.6 37.1 %all_to_all.15 = f32[64,1,1920]{2,1,0:T(1,128)S(1)} all-to-all(f32[64,1,1920]{2,1,0:T(1,128)S(1)} %bitcast.13), channel_id=1, replica_groups=mesh['con'=8,'slab'=64] {'slab'}, dimensions={0} | all-to-all | bytes 983040 | tf_op jit(solution)/shard_map/all_to_all | solution.py:386
  91.7 0.0 copy-done.1
  91.7 0.0 copy-done.2
  91.7 0.0 copy-done.3
  91.7 0.0 copy-done.4
  91.7 1.1 %third.1 = (f32[8,16,384]{2,1,0:T(8,128)S(1)}, f32[200,128]{1,0:T(8,128)S(1)}) custom-call(s32[1]{0:T(128)} %bitcast.6.last_ref, f32[960,128]{1,0:T(8,128)S(1)} %bitcast.14, f32[160,320]{1,0:T(8,128)S(1)} %get-tuple-element.19.rows_ref, bf16[4,160,480]{2,1,0:T(8,128)(2,1)S(1)} %copy-done.1, f32[1,2,5,2,320]{4,3,2,1,0:T(2,128)S(1)} %bitcast.21, ...), custom_call_target="tpu_custom_call" | custom-call | tf_op jit(solution)/shard_map/third/pallas_call | solution.py:445
  92.9 9.3 %all_to_all.16 = f32[8,1,3200]{2,1,0:T(1,128)S(1)} all-to-all(f32[8,1,3200]{2,1,0:T(1,128)S(1)} %bitcast.24), channel_id=1, replica_groups=mesh['con'=8,'slab'=64] {'con'}, dimensions={0} | all-to-all | bytes 204800 | tf_op jit(solution)/shard_map/all_to_all | solution.py:386
  102.2 0.7 last.1
  (1 shorter events, 0.0 us)
Async XLA Ops:
  0.6 29.4 %copy-start.6 = (f32[1,10,640]{2,0,1:T(1,128)S(1)}, f32[1,10,640]{2,0,1:T(1,128)}, u32[]{:S(2)}) copy-start(f32[1,10,640]{2,0,1:T(1,128)} %param.13) | copy-start | bytes 76804
  0.6 29.4 %copy-start.5 = (bf16[10,384]{1,0:T(8,128)(2,1)S(1)}, bf16[10,384]{1,0:T(8,128)(2,1)}, u32[]{:S(2)}) copy-start(bf16[10,384]{1,0:T(8,128)(2,1)} %constant.14.clone.spread_ref) | copy-start | bytes 23044
  3.5 49.7 %copy-start = (bf16[2,4,160,480]{3,2,1,0:T(8,128)(2,1)S(1)}, bf16[2,4,160,480]{3,2,1,0:T(8,128)(2,1)}, u32[]{:S(2)}) copy-start(bf16[2,4,160,480]{3,2,1,0:T(8,128)(2,1)} %constant.16.clone.table_ref) | copy-start | bytes 3686404
  3.5 49.6 %all-to-all-start = ((f32[64,1,1664]{2,1,0:T(1,128)}), f32[64,1,1664]{2,1,0:T(1,128)S(1)}, u32[]{:S(2)}, u32[]{:S(2)}) async-start(f32[64,1,1664]{2,1,0:T(1,128)} %bitcast.2), calls=%async_computation | async-start | bytes 851968 | tf_op jit(solution)/shard_map/all_to_all | solution.py:386
  24.4 19.6 %collective-permute-start = (f32[26,1,2,320]{3,2,1,0:T(2,128)S(1)}, f32[26,1,2,320]{3,2,1,0:T(2,128)S(1)}, u32[]{:S(2)}, u32[]{:S(2)}) collective-permute-start(f32[26,1,2,320]{3,2,1,0:T(2,128)S(1)} %get-tuple-element.14), channel_id=1, source_target_pairs={{1,0},{2,1},{3,2},{4,3},{5,4},{6,5},{7,6},{8,7},{9,8},{10,9},{11,1... | collective-permute-start | bytes 199688 | tf_op jit(solution)/shard_map/ppermute | solution.py:392
  26.8 8.4 %collective-permute-start.1 = (f32[2,1,2,320]{3,2,1,0:T(2,128)S(1)}, f32[2,1,2,320]{3,2,1,0:T(2,128)S(1)}, u32[]{:S(2)}, u32[]{:S(2)}) collective-permute-start(f32[2,1,2,320]{3,2,1,0:T(2,128)S(1)} %get-tuple-element.15), channel_id=1, source_target_pairs={{0,1},{1,2},{2,3},{3,4},{4,5},{5,6},{6,7},{7,8},{8,9},{9,10},{10,1... | collective-permute-start | bytes 15368 | tf_op jit(solution)/shard_map/ppermute | solution.py:392
  53.2 38.6 %copy-start.1 = (bf16[4,160,480]{2,1,0:T(8,128)(2,1)S(1)}, bf16[4,160,480]{2,1,0:T(8,128)(2,1)}, u32[]{:S(2)}) copy-start(bf16[4,160,480]{2,1,0:T(8,128)(2,1)} %constant.17.clone.table_ref) | copy-start | bytes 1843204
  53.2 38.6 %copy-start.2 = (f32[1,6,2,5,320]{4,2,3,1,0:T(2,128)S(1)}, f32[1,6,2,5,320]{4,2,3,1,0:T(2,128)}, u32[]{:S(2)}) copy-start(f32[1,6,2,5,320]{4,2,3,1,0:T(2,128)} %param.10) | copy-start | bytes 230404
  53.2 38.6 %copy-start.3 = (f32[1,2,2,5,320]{4,2,3,1,0:T(2,128)S(1)}, f32[1,2,2,5,320]{4,2,3,1,0:T(2,128)}, u32[]{:S(2)}) copy-start(f32[1,2,2,5,320]{4,2,3,1,0:T(2,128)} %param.9) | copy-start | bytes 76804
  53.2 38.6 %copy-start.4 = (f32[1,2,2,5,320]{4,2,3,1,0:T(2,128)S(1)}, f32[1,2,2,5,320]{4,2,3,1,0:T(2,128)}, u32[]{:S(2)}) copy-start(f32[1,2,2,5,320]{4,2,3,1,0:T(2,128)} %param.11) | copy-start | bytes 76804
